TPU v7x, 512 devices: a whole 4x8x8 slice. The times are simulated.
512 devices in a mesh: dp: 16 (over y, core), mp: 32 (over x, z).
Axes of the slice: x: 4, y: 8, z: 8, core: 2. Of those that a mesh axis runs over, the one named last changes fastest.
Arguments:
- packed_rows: bfloat16 [16384, 6144], P(('dp', 'mp')), may hold values from -6 to 6
- dest_group: int32 [16384], P(('dp', 'mp')), may hold values from 0 to 15, as said below
- dest_slot: int32 [16384], P(('dp', 'mp')), may hold values from 0 to 31, as said below
- image_ids: int32 [16, 1024], P('dp', 'mp'), may hold values from 0 to 15, never falling along the last dimension, each value on 1 to 512 neighbouring positions
- ln_gain: float32 [6144], replicated, may hold values from 0.1 to 1.9
- qkv_weight: bfloat16 [3, 6144, 4096], P(None, None, 'mp'), may hold values from -0.078125 to 0.078125
- qk_gain: float32 [2, 4096], P(None, 'mp'), may hold values from 0.6 to 8
Outputs:
- attended: bfloat16 [16384, 4096], P(('dp', 'mp'))
Inputs may be any that keep to these rules, and one draw needn't show every extreme that they name: `dest_group`: rows of the loader at mp index m go to tokens m * 32 to (m + 1) * 32 - 1 of their group. Each loader device sends at most 4 rows to one group, and in every draw some loader device sends exactly 4 rows to one group. `dest_slot`: together with dest_group, every slot of every receiving device gets exactly one row.
All inputs are finite; a program needn't handle non-finite values.
Results may differ from a plain program's by a relative error of at most 0.022.
The roundings to bfloat16 on the way count: a program that leaves them out, or rounds other values in their place, can miss the bound.
Values may be sent and summed in bfloat16 or wider, within the bound.
No kernel may reach another device: no remote copies, remote signals or barrier semaphores. Data moves between devices by JAX's collectives and lax.ppermute only.
A program may use at most 64 MiB of HBM per device.

v0:
```python
import jax
import jax.numpy as jnp
from jax import lax
from jax.sharding import PartitionSpec as P

HD = 128


def norm_rows(rows, gain):
    values = rows.astype(jnp.float32)
    mean = jnp.mean(values, axis=-1, keepdims=True)
    centered = values - mean
    spread = jnp.mean(centered * centered, axis=-1, keepdims=True)
    return (centered * lax.rsqrt(spread + 1e-06) * gain).astype(jnp.bfloat16)


def local(packed_rows, dest_group, dest_slot, image_ids, ln_gain, qkv_weight, qk_gain):
    normed = norm_rows(packed_rows, ln_gain)
    tok_rows = packed_rows.shape[0]
    width = packed_rows.shape[1]
    n_groups = lax.axis_size("dp")
    capacity = max(2, 2 * tok_rows // n_groups)
    positions = jnp.arange(tok_rows, dtype=jnp.int32)
    earlier = (dest_group[:, None] == dest_group[None, :]) & (
        positions[None, :] < positions[:, None]
    )
    rank = jnp.sum(earlier.astype(jnp.int32), axis=1)
    send_rows = (
        jnp.zeros((n_groups, capacity, width), jnp.bfloat16).at[dest_group, rank].set(normed)
    )
    send_slots = (
        jnp.full((n_groups, capacity), -1.0, jnp.bfloat16)
        .at[dest_group, rank]
        .set(dest_slot.astype(jnp.bfloat16))
    )
    got_rows, got_slots = (
        lax.all_to_all(send_rows, "dp", split_axis=0, concat_axis=0, tiled=True),
        lax.all_to_all(send_slots, "dp", split_axis=0, concat_axis=0, tiled=True),
    )
    flat_rows = got_rows.reshape(n_groups * capacity, width)
    flat_slots = got_slots.reshape(n_groups * capacity).astype(jnp.float32)
    placing = (flat_slots[None, :] == positions[:, None].astype(jnp.float32)).astype(jnp.bfloat16)
    tokens = jnp.dot(placing, flat_rows, preferred_element_type=jnp.float32).astype(jnp.bfloat16)
    group_rows, group_ids = (
        lax.all_gather(tokens, "mp", axis=0, tiled=True),
        lax.all_gather(image_ids[0].astype(jnp.bfloat16), "mp", axis=0, tiled=True),
    )
    count = group_rows.shape[0]
    heads = qkv_weight.shape[2] // HD
    projected = jnp.einsum(
        "td,kdc->ktc", group_rows, qkv_weight, preferred_element_type=jnp.float32
    )
    query_n = norm_rows(projected[0].reshape(count, heads, HD), qk_gain[0].reshape(heads, HD))
    key_n = norm_rows(projected[1].reshape(count, heads, HD), qk_gain[1].reshape(heads, HD))
    value = projected[2].astype(jnp.bfloat16).reshape(count, heads, HD)
    scores = jnp.einsum(
        "qhc,khc->hqk", query_n, key_n, preferred_element_type=jnp.float32
    ) * HD ** (-0.5)
    image_f = group_ids.astype(jnp.float32)
    same = image_f[:, None] == image_f[None, :]
    masked = jnp.where(same[None], scores, -1e30)
    top = jnp.max(masked, axis=-1, keepdims=True)
    weights = jnp.exp(masked - top)
    probs = (weights / jnp.sum(weights, axis=-1, keepdims=True)).astype(jnp.bfloat16)
    result = jnp.einsum("hqk,khc->qhc", probs, value, preferred_element_type=jnp.float32)
    result = result.astype(jnp.bfloat16).reshape(count, heads * HD)
    return lax.all_to_all(result, "mp", split_axis=0, concat_axis=1, tiled=True)


def solution(mesh):
    return jax.shard_map(
        local,
        mesh=mesh,
        in_specs=(
            P(("dp", "mp"), None),
            P(("dp", "mp")),
            P(("dp", "mp")),
            P("dp", "mp"),
            P(),
            P(None, None, "mp"),
            P(None, "mp"),
        ),
        out_specs=P(("dp", "mp"), None),
        check_vma=False,
    )
```

profile of v0, /device:TPU:1, one launch (start us, length us, event | category | flops | bytes accessed | tf_op | source)
XLA Modules:
  0.0 227.7 jit_solution(2317695493599553311)
XLA Ops:
  6.5 0.9 convert_reduce_fusion.1
  7.4 0.7 fusion.39
  8.1 0.7 convert_element_type.105
  8.8 2.1 scatter_fusion
  10.8 0.7 copy.22
  11.5 10.1 %all-to-all-start = ((bf16[16,1,4]{2,1,0:T(2,128)(2,1)}), bf16[16,1,4]{2,1,0:T(2,128)(2,1)S(1)}, u32[]{:S(2)}, u32[]{:S(2)}) async-start(bf16[16,1,4]{2,1,0:T(2,128)(2,1)} %copy.22), calls=%async_computation | async-start | bytes 16384 | tf_op jit(solution)/shard_map/all_to_all | solution.py:38
  21.7 1.2 convert_reduce_fusion
  22.8 1.3 fusion.7
  24.1 1.2 fusion.9
  25.3 1.2 broadcast_in_dim.11
  26.5 10.2 %scatter_fusion.1 = bf16[16,4,6144]{2,1,0:T(4,128)(2,1)} fusion(bf16[16,4,6144]{2,1,0:T(4,128)(2,1)} %broadcast_in_dim.11, s32[32]{0:T(128)S(1)} %fusion.39, bf16[32,6144]{1,0:T(8,128)(2,1)S(1)} %fusion.9), kind=kCustom, calls=%fused_computation.1 | custom fusion | bytes 1179904 | tf_op jit(solution)/shard_map/scatter | solution.py:29
  36.7 0.0 all-to-all-done
  36.7 7.3 %all-to-all-start.1 = ((bf16[16,4,6144]{2,1,0:T(4,128)(2,1)}), bf16[16,4,6144]{2,1,0:T(4,128)(2,1)S(1)}, u32[]{:S(2)}, u32[]{:S(2)}) async-start(bf16[16,4,6144]{2,1,0:T(4,128)(2,1)} %scatter_fusion.1), calls=%async_computation.1 | async-start | bytes 1572864 | tf_op jit(solution)/shard_map/all_to_all | solution.py:37
  44.0 0.0 all-gather.3.cloned.1.call-start
  44.1 0.1 reshape.392
  44.2 22.5 %all-to-all-done.1 = bf16[16,4,6144]{2,1,0:T(4,128)(2,1)S(1)} async-done(((bf16[16,4,6144]{2,1,0:T(4,128)(2,1)}), bf16[16,4,6144]{2,1,0:T(4,128)(2,1)S(1)}, u32[]{:S(2)}, u32[]{:S(2)}) %all-to-all-start.1) | async-done | bytes 786464 | tf_op jit(solution)/shard_map/all_to_all | solution.py:37
  66.7 0.2 reshape.391
  66.9 1.1 convolution_convert_fusion
  68.0 0.0 all-gather.3.cloned.1.call-update
  68.0 0.0 copy-start.1
  68.0 0.0 copy-start
  68.0 6.6 %copy.23 = bf16[3,6144,128]{1,2,0:T(8,128)(2,1)} copy(bf16[3,6144,128]{2,1,0:T(8,128)(2,1)} %param.12) | data formatting | bytes 9437184 | tf_op args[5]
  74.7 1.3 dynamic-slice
  76.6 0.0 copy-done.1
  76.6 0.2 dynamic-update-slice
  76.8 65.6 %all-reduce = bf16[1024]{0:T(1024)(128)(2,1)S(1)} all-reduce(bf16[1024]{0:T(1024)(128)(2,1)S(1)} %dynamic-update-slice), channel_id=2, replica_groups=mesh['dp'=16,'mp'=32] {'mp'}, use_global_device_ids=true, to_apply=%add | all-reduce | flops 1024 | bytes 4096
  142.5 0.0 copy-done
  142.5 49.8 %all-gather.3.cloned.1.call-done = bf16[1024,6144]{1,0:T(8,128)(2,1)} async-done(((bf16[32,6144]{1,0:T(8,128)(2,1)}), bf16[1024,6144]{1,0:T(8,128)(2,1)}) %all-gather.3.cloned.1.call-update) | async-done | bytes 12582928 | tf_op jit(solution)/shard_map/all_gather | solution.py:45
  192.2 9.4 %fusion.42 = f32[1024,384]{0,1:S(1)} fusion(bf16[1024,6144]{1,0:T(8,128)(2,1)} %all-gather.3.cloned.1.call-done, bf16[6144,384]{0,1:T(8,128)(2,1)} %bitcast.92), kind=kOutput, calls=%fused_computation.73 | convolution fusion | flops 4831838208 | bytes 18874368
  201.7 0.1 slice_reduce_fusion.1
  201.8 0.1 fusion.16
  201.9 1.0 fusion.1
  202.9 1.0 fusion
  203.9 1.4 fusion.4
  205.3 0.2 copy.24
  205.5 14.6 %all_to_all.33 = bf16[32,32,128]{2,1,0:T(8,128)(2,1)S(1)} all-to-all(bf16[32,32,128]{2,1,0:T(8,128)(2,1)S(1)} %bitcast.97), channel_id=1, replica_groups=mesh['dp'=16,'mp'=32] {'mp'}, dimensions={0} | all-to-all | bytes 524288 | tf_op jit(solution)/shard_map/all_to_all | solution.py:67
  220.1 0.7 copy_bitcast_fusion
  (12 shorter events, 0.1 us)
Async XLA Ops:
  11.5 25.2 %all-to-all-start = ((bf16[16,1,4]{2,1,0:T(2,128)(2,1)}), bf16[16,1,4]{2,1,0:T(2,128)(2,1)S(1)}, u32[]{:S(2)}, u32[]{:S(2)}) async-start(bf16[16,1,4]{2,1,0:T(2,128)(2,1)} %copy.22), calls=%async_computation | async-start | bytes 16384 | tf_op jit(solution)/shard_map/all_to_all | solution.py:38
  36.7 29.9 %all-to-all-start.1 = ((bf16[16,4,6144]{2,1,0:T(4,128)(2,1)}), bf16[16,4,6144]{2,1,0:T(4,128)(2,1)S(1)}, u32[]{:S(2)}, u32[]{:S(2)}) async-start(bf16[16,4,6144]{2,1,0:T(4,128)(2,1)} %scatter_fusion.1), calls=%async_computation.1 | async-start | bytes 1572864 | tf_op jit(solution)/shard_map/all_to_all | solution.py:37
  44.0 148.2 %all-gather.3.cloned.1.call-start = ((), (), s32[]{:S(2)}) async-start(), calls=%async_computation.3 | async-start | bytes 12976128 | tf_op jit(solution)/shard_map/all_gather | solution.py:45
  68.0 8.6 %copy-start.1 = (s32[1,32]{1,0:T(1,128)S(1)}, s32[1,32]{1,0:T(1,128)}, u32[]{:S(2)}) copy-start(s32[1,32]{1,0:T(1,128)} %param.10) | copy-start | bytes 388
  68.0 74.5 %copy-start = (f32[2,128]{1,0:T(2,128)S(1)}, f32[2,128]{1,0:T(2,128)}, u32[]{:S(2)}) copy-start(f32[2,128]{1,0:T(2,128)} %param.13) | copy-start | bytes 3076
Sparse Core Ops, SparseCore 0:
  68.1 124.0 all-gather.2
where the time goes:
time: 230 us; the launch traced here: 228 us
  blocking collectives  80.2 us (35%)
  waiting for transfers between devices  72.3 us (31%)
  local copies, waits for them, and re-layouts  23.5 us (10%)
  starting transfers between devices  17.5 us (8%)
  between operations  14.2 us (6%)
  matrix products  12.9 us (6%)
  other arithmetic  7.15 us (3%)
    unnamed x1, blocking collectives  65.6 us
    all_gather x1, waiting for transfers between devices, local(): lax.all_gather(tokens, 'mp', axis=0, tiled=True)  49.8 us
    all_to_all x1, waiting for transfers between devices, local(): lax.all_to_all(send_rows, 'dp', split_axis=0, concat_axis=0, tiled=True)  22.5 us
    all_to_all x1, blocking collectives, local(): return lax.all_to_all(result, 'mp', split_axis=0, concat_axis=1, tiled=True)  14.6 us
    scatter x1, local copies, waits for them, and re-layouts, local(): jnp.zeros((n_groups, capacity, width), jnp.bfloat16).at[dest_group, rank]  10.2 us
    all_to_all x1, starting transfers between devices, local(): lax.all_to_all(send_slots, 'dp', split_axis=0, concat_axis=0, tiled=True)  10.1 us
    unnamed x1, matrix products  9.44 us
    unnamed x8, local copies, waits for them, and re-layouts  8.16 us
  transfers between devices with their start and end apart: 3, of which 2 were waited for; matrix products, arithmetic and copies ran while one was open for 10% of the time, Pallas kernels for 0%

commit v1 on v0

v1 whole, which is shorter than its diff:
```python
import functools

import jax
import jax.numpy as jnp
import numpy as np
from jax import lax
from jax.experimental import pallas as pl
from jax.experimental.pallas import tpu as pltpu
from jax.sharding import PartitionSpec as P

HD = 128
LANES = 128
NX, NZ = 4, 8
AXES = ("dp", "mp")
BF16 = jnp.bfloat16
F32 = jnp.float32
VMEM = pltpu.VMEM
SMEM = pltpu.SMEM


def vmem_call(body, outs, n_in, scratch=(), smem_in=(), limit=48):
    return pl.pallas_call(
        body,
        out_shape=outs,
        in_specs=[
            pl.BlockSpec(memory_space=SMEM if i in smem_in else VMEM) for i in range(n_in)
        ],
        out_specs=jax.tree.map(lambda _: pl.BlockSpec(memory_space=VMEM), outs),
        scratch_shapes=scratch,
        compiler_params=pltpu.CompilerParams(vmem_limit_bytes=limit << 20),
    )


def pairs(n_dp, move):
    out = []
    for dp in range(n_dp):
        for mp in range(NX * NZ):
            c, x, z = move(dp % 2, mp // NZ, mp % NZ)
            out.append((dp * NX * NZ + mp, (dp // 2 * 2 + c) * NX * NZ + x * NZ + z))
    return out


def send(array, n_dp, move):
    return lax.ppermute(array, AXES, pairs(n_dp, move))


def along_z(c, x, z):
    return c, x, (z + (1 if c == 0 else -1)) % NZ


def across_x(c, x, z):
    return c, x ^ 1, z


def mirror_x(c, x, z):
    return c, 3 - x, z


def other_core(c, x, z):
    return 1 - c, x, z


def to_region(c, x, z):
    return (c, x, z) if c == x // 2 else (1 - c, 3 - x, z)


def block_columns():
    table = np.zeros((2, NX, NZ, NX * NZ), np.int32)
    for c in range(2):
        for x in range(NX):
            for z in range(NZ):
                cols = []
                for mine in (c, 1 - c):
                    turn = 1 if mine == 0 else -1
                    held = [(x, z, mine), (x ^ 1, z, mine)]
                    for s in (1, 2, 3):
                        for xx in (x, x ^ 1):
                            for core in (mine, 1 - mine):
                                held.append((xx, (z - turn * s) % NZ, core))
                    held += [(x, (z + 4) % NZ, mine), (x ^ 1, (z + 4) % NZ, mine)]
                    for xx, zz, core in held:
                        cols.append((xx if core == xx // 2 else 3 - xx) * NZ + zz)
                table[c, x, z] = cols
    return table.reshape(2, NX * NZ, NX * NZ)


def norm_rows(values, gain):
    mean = jnp.mean(values, axis=-1, keepdims=True)
    centered = values - mean
    spread = jnp.mean(centered * centered, axis=-1, keepdims=True)
    return (centered * lax.rsqrt(spread + 1e-06) * gain).astype(BF16)


def pack_body(capacity, rows, group_col, group_row, slot_row, gain, out):
    tok, width = rows.shape
    slots = out.shape[0]
    normed = norm_rows(rows[...].astype(F32), gain[...])
    i = lax.broadcasted_iota(jnp.int32, (tok, tok), 0)
    j = lax.broadcasted_iota(jnp.int32, (tok, tok), 1)
    earlier = (group_col[...] == group_row[...]) & (i < j)
    rank = jnp.sum(jnp.where(earlier, 1, 0), axis=0, keepdims=True)
    target = group_row[...] * capacity + rank
    hit = lax.broadcasted_iota(jnp.int32, (slots, tok), 0) == target
    onehot = jnp.where(hit, 1.0, 0.0)
    out[:, :width] = jnp.dot(
        onehot.astype(BF16), normed, preferred_element_type=F32
    ).astype(BF16)
    slot = jnp.sum(onehot * (slot_row[...].astype(F32) + 1.0), axis=1, keepdims=True) - 1.0
    out[:, width:] = jnp.broadcast_to(slot, (slots, LANES)).astype(BF16)


def place_body(got, ids_col, out):
    tok = out.shape[0]
    width = out.shape[1] - LANES
    slot = got[:, width:].astype(F32)[:, :tok]
    hit = slot == lax.broadcasted_iota(jnp.int32, slot.shape, 1).astype(F32)
    onehot = jnp.where(hit, 1.0, 0.0).astype(BF16)
    out[:, :width] = lax.dot_general(
        onehot, got[:, :width], (((0,), (0,)), ((), ())), preferred_element_type=F32
    ).astype(BF16)
    out[:, width:] = jnp.broadcast_to(ids_col[...].astype(F32), (tok, LANES)).astype(BF16)


def proj_body(n_a, place, *refs):
    a_refs, refs = refs[:n_a], refs[n_a:]
    b_refs, refs = refs[:n_a], refs[n_a:]
    (where_am_i, w_own, w_near, w_far, gain_own, gain_imp, mine, other, tokens, total) = refs
    da = a_refs[0].shape[1]
    width = tokens.shape[1]
    half = width // 2
    for a_ref, b_ref, (a_pieces, b_pieces) in zip(a_refs, b_refs, place):
        for src, dst, n in a_pieces:
            tokens[dst : dst + n, :da] = a_ref[src : src + n, :]
        for src, dst, n in b_pieces:
            tokens[dst : dst + n, da:] = b_ref[src : src + n, : width - da]
            ids = b_ref[src : src + n, width - da :]
            mine[dst : dst + n, 3 * HD :] = ids
            other[dst : dst + n, 3 * HD :] = ids
    core = where_am_i[0]
    step = min(512, half)
    for h, w_imp in enumerate((w_near, w_far)):
        base = (core if h == 0 else 1 - core) * half
        for k in range(half // step):
            at = pl.multiple_of(base + k * step, step)
            lhs = tokens[:, pl.ds(at, step)]
            own = [w_own[j, pl.ds(at, step), :] for j in range(3)]
            imp = [w_imp[j, k * step : (k + 1) * step, :] for j in range(3)]
            six = own + imp
            for n in range(3):
                w = jnp.concatenate(six[2 * n : 2 * n + 2], axis=1)
                part = jnp.dot(lhs, w, preferred_element_type=F32)
                cols = slice(2 * n * HD, (2 * n + 2) * HD)
                if h == 0 and k == 0:
                    total[:, cols] = part
                else:
                    total[:, cols] += part
    home = where_am_i[1] == 1

    def emit(first, second):
        for start, gain, dst in ((0, gain_own, first), (3 * HD, gain_imp, second)):
            for j in range(2):
                cols = total[:, start + j * HD : start + (j + 1) * HD]
                dst[:, j * HD : (j + 1) * HD] = norm_rows(cols, gain[j : j + 1, :])
            dst[:, 2 * HD : 3 * HD] = total[:, start + 2 * HD : start + 3 * HD].astype(BF16)

    @pl.when(home)
    def _():
        emit(mine, other)

    @pl.when(jnp.logical_not(home))
    def _():
        emit(other, mine)


def attend_body(tok, column, first, second, out, ids_row):
    rows = first.shape[0]
    for n, half in enumerate((first, second)):
        turned = jnp.transpose(half[:, 3 * HD :].astype(F32))
        ids_row[:, n * rows : (n + 1) * rows] = turned[0:8, :]
    key = jnp.concatenate([first[:, HD : 2 * HD], second[:, HD : 2 * HD]], axis=0)
    value = jnp.concatenate([first[:, 2 * HD : 3 * HD], second[:, 2 * HD : 3 * HD]], axis=0)
    step = min(256, rows)
    for n, half in enumerate((first, second)):
        for at in range(0, rows, step):
            query = half[at : at + step, :HD]
            scores = lax.dot_general(
                query, key, (((1,), (1,)), ((), ())), preferred_element_type=F32
            ) * HD ** (-0.5)
            same = half[at : at + step, 3 * HD : 3 * HD + 1].astype(F32) == ids_row[0:1, :]
            masked = jnp.where(same, scores, -1e30)
            top = jnp.max(masked, axis=-1, keepdims=True)
            weights = jnp.exp(masked - top)
            probs = (weights / jnp.sum(weights, axis=-1, keepdims=True)).astype(BF16)
            result = jnp.dot(probs, value, preferred_element_type=F32).astype(BF16)
            for b in range(step // tok):
                block = (n * rows + at) // tok + b
                out[column[block]] = result[b * tok : (b + 1) * tok, :]


def local(packed_rows, dest_group, dest_slot, image_ids, ln_gain, qkv_weight, qk_gain):
    tok, width = packed_rows.shape
    n_dp = lax.axis_size("dp")
    capacity = max(2, 2 * tok // n_dp)
    dp, mp = lax.axis_index("dp"), lax.axis_index("mp")
    c = dp % 2
    home = c == mp // NZ // 2
    half = width // 2
    go = functools.partial(lambda array, move: send(array, n_dp, move))

    near = go(lax.dynamic_slice_in_dim(qkv_weight, c * half, half, axis=1), mirror_x)
    far = go(near, other_core)
    gain_imp = go(qk_gain, mirror_x)

    packed = vmem_call(
        functools.partial(pack_body, capacity),
        jax.ShapeDtypeStruct((n_dp * capacity, width + LANES), BF16),
        5,
    )(packed_rows, dest_group[:, None], dest_group[None, :], dest_slot[None, :], ln_gain[None, :])
    got = lax.all_to_all(
        packed.reshape(n_dp, capacity, width + LANES), "dp", split_axis=0, concat_axis=0, tiled=True
    ).reshape(n_dp * capacity, width + LANES)
    placed = vmem_call(
        place_body, jax.ShapeDtypeStruct((tok, width + LANES), BF16), 2
    )(got, image_ids.reshape(tok, 1))

    da = width * 13 // 24 // 256 * 256
    moved = go(placed, to_region)
    twin = go(moved, other_core)
    a, b = moved[:, :da], moved[:, da:]
    b_x = go(b, across_x)
    b_x_twin = go(b_x, other_core)
    a_now = jnp.concatenate([a, twin[:, :da]], axis=0)
    b_now = jnp.concatenate([b, twin[:, da:], b_x, b_x_twin], axis=0)
    a_held, b_held = [a], [b_now]
    for s in range(1, 5):
        if s == 4:
            a_now = a_now[:tok]
            b_now = jnp.concatenate([b_now[:tok], b_now[2 * tok : 3 * tok]], axis=0)
        a_now = go(a_now, along_z)
        b_now = go(b_now, along_z)
        a_held.append(a_now)
        b_held.append(b_now)
    x01 = go(jnp.concatenate(a_held[:2], axis=0), across_x)
    a_x = [x01] + [go(held, across_x) for held in a_held[2:]]

    t = tok
    a_list = a_held + a_x
    a_place = [
        [(0, 0, t)], [(0, 2 * t, 2 * t)], [(0, 6 * t, 2 * t)], [(0, 10 * t, 2 * t)], [(0, 14 * t, t)],
        [(0, t, t), (t, 4 * t, 2 * t)], [(0, 8 * t, 2 * t)], [(0, 12 * t, 2 * t)], [(0, 15 * t, t)],
    ]
    b_place = [
        [(0, 0, t), (2 * t, t, t)], [(0, 2 * t, 4 * t)], [(0, 6 * t, 4 * t)], [(0, 10 * t, 4 * t)],
        [(0, 14 * t, 2 * t)],
    ]
    b_list = b_held + [b_held[-1]] * (len(a_list) - len(b_held))
    b_place = b_place + [[]] * (len(a_list) - len(b_place))
    here = jnp.stack([c, home.astype(jnp.int32)]).astype(jnp.int32)
    rows = 16 * tok
    shape = jax.ShapeDtypeStruct((rows, 4 * HD), BF16)
    n_a = len(a_list)
    mine, other = vmem_call(
        functools.partial(proj_body, n_a, list(zip(a_place, b_place))),
        (shape, shape),
        2 * n_a + 6,
        scratch=[VMEM((rows, width), BF16), VMEM((rows, 6 * HD), F32)],
        smem_in=(2 * n_a,),
        limit=56,
    )(*a_list, *b_list, here, qkv_weight, near, far, qk_gain, gain_imp)
    swapped = go(other, other_core)

    table = jnp.asarray(block_columns())
    column = lax.dynamic_slice(table, (c, mp, 0), (1, 1, NX * NZ)).reshape(NX * NZ)
    result = vmem_call(
        functools.partial(attend_body, tok),
        jax.ShapeDtypeStruct((NX * NZ, tok, HD), BF16),
        3,
        scratch=[VMEM((8, 2 * rows), F32)],
        smem_in=(0,),
    )(column, mine, swapped)

    back = lax.all_to_all(result, "mp", split_axis=0, concat_axis=0, tiled=True)
    low, high = back[: NX * NZ // 2], back[NX * NZ // 2 :]
    first = c == 0
    keep = jnp.where(first, low, high)
    gave = go(jnp.where(first, high, low), other_core)
    gave = jnp.concatenate([gave[NZ:], gave[:NZ]], axis=0)
    heads = jnp.concatenate([jnp.where(first, keep, gave), jnp.where(first, gave, keep)], axis=0)
    return jnp.transpose(heads, (1, 0, 2)).reshape(tok, NX * NZ * HD)


def solution(mesh):
    return jax.shard_map(
        local,
        mesh=mesh,
        in_specs=(
            P(("dp", "mp"), None),
            P(("dp", "mp")),
            P(("dp", "mp")),
            P("dp", "mp"),
            P(),
            P(None, None, "mp"),
            P(None, "mp"),
        ),
        out_specs=P(("dp", "mp"), None),
        check_vma=False,
    )
```

time: 230 us -> 208 us (0.904)
  blocking collectives: 80.2 us -> 0 us
  starting transfers between devices: 17.5 us -> 86.4 us
  Pallas kernels: 0 us -> 18.3 us
  waiting for transfers between devices: 72.3 us -> 88.6 us
  between operations: 14.2 us -> 0.55 us
  matrix products: 12.9 us -> 0 us
  local copies, waits for them, and re-layouts: 23.5 us -> 11.1 us
  other arithmetic: 7.15 us -> 1.61 us
    ppermute x0 -> x21, starting transfers between devices: none -> 72 us  [send(): return lax.ppermute(array, AXES, pairs(n_dp, move))]
    unnamed x1 -> x0, blocking collectives: 65.6 us -> none
    ppermute x0 -> x21, waiting for transfers between devices: none -> 56 us  [send(): return lax.ppermute(array, AXES, pairs(n_dp, move))]
    all_gather x1 -> x0, waiting for transfers between devices: 49.8 us -> none  [local(): lax.all_gather(tokens, 'mp', axis=0, tiled=True)]
    pallas_call x0 -> x4, Pallas kernels: none -> 18.3 us  [the longest x1 13.3 us: local(): vmem_call(functools.partial(proj_body, n_a, list(zip(a_place, b_place))),...]
    all_to_all x1 -> x0, blocking collectives: 14.6 us -> none  [local(): return lax.all_to_all(result, 'mp', split_axis=0, concat_axis=1, tiled=True)]
    scatter x2 -> x0, local copies, waits for them, and re-layouts: 12.3 us -> none  [the longest x1 10.2 us: local(): jnp.zeros((n_groups, capacity, width), jnp.bfloat16).at[dest_group, rank]]
    all_to_all x2, waiting for transfers between devices: 22.5 us -> 32.6 us  [the longest x1 22.9 us: local(): lax.all_to_all(packed.reshape(n_dp, capacity, width + LANES), 'dp', split...]
  transfers between devices with their start and end apart: 3 -> 23, of which waited for: 2 -> 14; matrix products, arithmetic and copies ran while one was open for 10% -> 2% of each run, Pallas kernels for 0% -> 0%
where the time goes in v1:
time: 208 us; the launch traced here: 207 us
  waiting for transfers between devices  88.6 us (43%)
  starting transfers between devices  86.4 us (42%)
  Pallas kernels  18.3 us (9%)
  local copies, waits for them, and re-layouts  11.1 us (5%)
    ppermute x21, starting transfers between devices, send(): return lax.ppermute(array, AXES, pairs(n_dp, move))  72 us
    ppermute x21, waiting for transfers between devices, send(): return lax.ppermute(array, AXES, pairs(n_dp, move))  56 us
    all_to_all x1, waiting for transfers between devices, local(): lax.all_to_all(packed.reshape(n_dp, capacity, width + LANES), 'dp', split...  22.9 us
    pallas_call x1, Pallas kernels, local(): vmem_call(functools.partial(proj_body, n_a, list(zip(a_place, b_place))),...  13.3 us
    all_to_all x1, starting transfers between devices, local(): lax.all_to_all(packed.reshape(n_dp, capacity, width + LANES), 'dp', split...  10.3 us
    all_to_all x1, waiting for transfers between devices, local(): back = lax.all_to_all(result, 'mp', split_axis=0, concat_axis=0, tiled=True)  9.67 us
    unnamed x38, local copies, waits for them, and re-layouts  6.39 us
  transfers between devices with their start and end apart: 23, of which 14 were waited for; matrix products, arithmetic and copies ran while one was open for 2% of the time, Pallas kernels for 0%

profile of v1, /device:TPU:1, one launch (start us, length us, event | category | flops | bytes accessed | tf_op | source)
XLA Modules:
  0.0 206.6 jit_solution(8599616263846698143)
XLA Ops:
  0.0 0.7 copy.11.group_col
  0.7 1.0 copy-done.1
  1.7 0.7 copy-done.2
  4.5 1.1 reshape.16
  5.6 10.3 %all-to-all-start = ((bf16[16,4,6272]{2,1,0:T(4,128)(2,1)}), bf16[16,4,6272]{2,1,0:T(4,128)(2,1)S(1)}, u32[]{:S(2)}, u32[]{:S(2)}) async-start(bf16[16,4,6272]{2,1,0:T(4,128)(2,1)} %reshape.16), calls=%async_computation | async-start | bytes 1605632 | tf_op jit(solution)/shard_map/all_to_all | solution.py:219
  16.0 22.9 %all-to-all-done = bf16[16,4,6272]{2,1,0:T(4,128)(2,1)S(1)} async-done(((bf16[16,4,6272]{2,1,0:T(4,128)(2,1)}), bf16[16,4,6272]{2,1,0:T(4,128)(2,1)S(1)}, u32[]{:S(2)}, u32[]{:S(2)}) %all-to-all-start) | async-done | bytes 802848 | tf_op jit(solution)/shard_map/all_to_all | solution.py:219
  39.4 1.9 collective-permute-start
  41.3 1.8 constant_dynamic-slice_fusion
  43.2 1.9 collective-permute-start.16
  45.1 5.8 %collective-permute-done = bf16[32,6272]{1,0:T(8,128)(2,1)S(1)} collective-permute-done((bf16[32,6272]{1,0:T(8,128)(2,1)S(1)}, bf16[32,6272]{1,0:T(8,128)(2,1)S(1)}, u32[]{:S(2)}, u32[]{:S(2)}) %collective-permute-start) | collective-permute-done | bytes 401440 | tf_op jit(solution)/shard_map/ppermute | solution.py:44
  50.8 1.9 collective-permute-start.1
  52.8 1.9 collective-permute-start.10
  54.7 5.9 %collective-permute-done.10 = bf16[32,2944]{1,0:T(8,128)(2,1)S(1)} collective-permute-done((bf16[32,2944]{1,0:T(8,128)(2,1)S(1)}, bf16[32,2944]{1,0:T(8,128)(2,1)S(1)}, u32[]{:S(2)}, u32[]{:S(2)}) %collective-permute-start.10) | collective-permute-done | bytes 188448 | tf_op jit(solution)/shard_map/ppermute | solution.py:44
  60.6 3.1 %collective-permute-start.11 = (bf16[32,2944]{1,0:T(8,128)(2,1)S(1)}, bf16[32,2944]{1,0:T(8,128)(2,1)S(1)}, u32[]{:S(2)}, u32[]{:S(2)}) collective-permute-start(bf16[32,2944]{1,0:T(8,128)(2,1)S(1)} %collective-permute-done.10), channel_id=1, source_target_pairs={{0,32},{1,33},{2,34},{3,35},{4,36},{5,37},{6,38},{7,39},{8,40},{9,... | collective-permute-start | bytes 565256 | tf_op jit(solution)/shard_map/ppermute | solution.py:44
  63.8 1.0 collective-permute-done.11
  64.8 8.5 %collective-permute-start.12 = (bf16[128,2944]{1,0:T(8,128)(2,1)S(1)}, bf16[128,2944]{1,0:T(8,128)(2,1)S(1)}, u32[]{:S(2)}, u32[]{:S(2)}) collective-permute-start(bf16[128,2944]{1,0:T(8,128)(2,1)S(1)} %pad_maximum_fusion.refs_9_), channel_id=1, source_target_pairs={{0,1},{1,2},{2,3},{3,4},{4,5},{5,6},{6,7},{7,0},{8,9},{9,10},{10,1... | collective-permute-start | bytes 2261000 | tf_op jit(solution)/shard_map/ppermute | solution.py:44
  73.4 8.5 %collective-permute-done.12.refs_10_ = bf16[128,2944]{1,0:T(8,128)(2,1)S(1)} collective-permute-done((bf16[128,2944]{1,0:T(8,128)(2,1)S(1)}, bf16[128,2944]{1,0:T(8,128)(2,1)S(1)}, u32[]{:S(2)}, u32[]{:S(2)}) %collective-permute-start.12) | collective-permute-done | bytes 753696 | tf_op jit(solution)/shard_map/ppermute | solution.py:44
  81.9 5.4 %collective-permute-start.13 = (bf16[128,2944]{1,0:T(8,128)(2,1)S(1)}, bf16[128,2944]{1,0:T(8,128)(2,1)S(1)}, u32[]{:S(2)}, u32[]{:S(2)}) collective-permute-start(bf16[128,2944]{1,0:T(8,128)(2,1)S(1)} %collective-permute-done.12.refs_10_), channel_id=1, source_target_pairs={{0,1},{1,2},{2,3},{3,4},{4,5},{5,6},{6,7},{7,0},{8,9},{9,10},{10,1... | collective-permute-start | bytes 2261000 | tf_op jit(solution)/shard_map/ppermute | solution.py:44
  87.4 1.9 collective-permute-start.2
  89.3 10.4 %collective-permute-done.16.refs_20_ = bf16[3,3072,128]{2,1,0:T(8,128)(2,1)} collective-permute-done((bf16[3,3072,128]{2,1,0:T(8,128)(2,1)S(1)}, bf16[3,3072,128]{2,1,0:T(8,128)(2,1)}, u32[]{:S(2)}, u32[]{:S(2)}) %collective-permute-start.16) | collective-permute-done | bytes 2359328 | tf_op jit(solution)/shard_map/ppermute | solution.py:44
  99.7 3.3 %collective-permute-start.17 = (bf16[3,3072,128]{2,1,0:T(8,128)(2,1)}, bf16[3,3072,128]{2,1,0:T(8,128)(2,1)}, u32[]{:S(2)}, u32[]{:S(2)}) collective-permute-start(bf16[3,3072,128]{2,1,0:T(8,128)(2,1)} %collective-permute-done.16.refs_20_), channel_id=1, source_target_pairs={{0,32},{1,33},{2,34},{3,35},{4,36},{5,37},{6,38},{7,39},{8,40},{9,... | collective-permute-start | bytes 7077896 | tf_op jit(solution)/shard_map/ppermute | solution.py:44
  103.1 9.0 %collective-permute-start.3 = (bf16[64,3328]{1,0:T(8,128)(2,1)S(1)}, bf16[64,3328]{1,0:T(8,128)(2,1)S(1)}, u32[]{:S(2)}, u32[]{:S(2)}) collective-permute-start(bf16[64,3328]{1,0:T(8,128)(2,1)S(1)} %collective-permute-done.2.refs_1_), channel_id=1, source_target_pairs={{0,1},{1,2},{2,3},{3,4},{4,5},{5,6},{6,7},{7,0},{8,9},{9,10},{10,1... | collective-permute-start | bytes 1277960 | tf_op jit(solution)/shard_map/ppermute | solution.py:44
  112.1 2.2 %collective-permute-start.14 = (bf16[128,2944]{1,0:T(8,128)(2,1)S(1)}, bf16[128,2944]{1,0:T(8,128)(2,1)S(1)}, u32[]{:S(2)}, u32[]{:S(2)}) collective-permute-start(bf16[128,2944]{1,0:T(8,128)(2,1)S(1)} %collective-permute-done.13.refs_11_), channel_id=1, source_target_pairs={{0,1},{1,2},{2,3},{3,4},{4,5},{5,6},{6,7},{7,0},{8,9},{9,10},{10,1... | collective-permute-start | bytes 2261000 | tf_op jit(solution)/shard_map/ppermute | solution.py:44
  114.3 2.0 collective-permute-start.18
  116.3 0.8 collective-permute-done.3.refs_2_
  117.1 5.1 %collective-permute-start.4 = (bf16[64,3328]{1,0:T(8,128)(2,1)S(1)}, bf16[64,3328]{1,0:T(8,128)(2,1)S(1)}, u32[]{:S(2)}, u32[]{:S(2)}) collective-permute-start(bf16[64,3328]{1,0:T(8,128)(2,1)S(1)} %collective-permute-done.3.refs_2_), channel_id=1, source_target_pairs={{0,1},{1,2},{2,3},{3,4},{4,5},{5,6},{6,7},{7,0},{8,9},{9,10},{10,1... | collective-permute-start | bytes 1277960 | tf_op jit(solution)/shard_map/ppermute | solution.py:44
  122.3 1.9 collective-permute-start.6
  124.2 5.5 %collective-permute-done.4.refs_3_ = bf16[64,3328]{1,0:T(8,128)(2,1)S(1)} collective-permute-done((bf16[64,3328]{1,0:T(8,128)(2,1)S(1)}, bf16[64,3328]{1,0:T(8,128)(2,1)S(1)}, u32[]{:S(2)}, u32[]{:S(2)}) %collective-permute-start.4) | collective-permute-done | bytes 426016 | tf_op jit(solution)/shard_map/ppermute | solution.py:44
  129.7 1.9 collective-permute-start.7
  131.7 5.0 %collective-permute-start.5 = (bf16[32,3328]{1,0:T(8,128)(2,1)S(1)}, bf16[32,3328]{1,0:T(8,128)(2,1)}, u32[]{:S(2)}, u32[]{:S(2)}) collective-permute-start(bf16[32,3328]{1,0:T(8,128)(2,1)S(1)} %slice.46), channel_id=1, source_target_pairs={{0,1},{1,2},{2,3},{3,4},{4,5},{5,6},{6,7},{7,0},{8,9},{9,10},{10,1... | collective-permute-start | bytes 638984 | tf_op jit(solution)/shard_map/ppermute | solution.py:44
  136.8 3.4 %collective-permute-start.8 = (bf16[64,3328]{1,0:T(8,128)(2,1)S(1)}, bf16[64,3328]{1,0:T(8,128)(2,1)}, u32[]{:S(2)}, u32[]{:S(2)}) collective-permute-start(bf16[64,3328]{1,0:T(8,128)(2,1)S(1)} %collective-permute-done.4.refs_3_), channel_id=1, source_target_pairs={{0,8},{1,9},{2,10},{3,11},{4,12},{5,13},{6,14},{7,15},{8,0},{9,1},... | collective-permute-start | bytes 1277960 | tf_op jit(solution)/shard_map/ppermute | solution.py:44
  140.7 0.9 copy-done.13
  141.6 1.9 collective-permute-start.15
  143.5 1.9 collective-permute-start.9
  146.1 3.7 %collective-permute-done.7.refs_6_ = bf16[64,3328]{1,0:T(8,128)(2,1)} collective-permute-done((bf16[64,3328]{1,0:T(8,128)(2,1)S(1)}, bf16[64,3328]{1,0:T(8,128)(2,1)}, u32[]{:S(2)}, u32[]{:S(2)}) %collective-permute-start.7) | collective-permute-done | bytes 426016 | tf_op jit(solution)/shard_map/ppermute | solution.py:44
  149.8 11.8 %collective-permute-done.9.refs_8_ = bf16[32,3328]{1,0:T(8,128)(2,1)S(1)} collective-permute-done((bf16[32,3328]{1,0:T(8,128)(2,1)}, bf16[32,3328]{1,0:T(8,128)(2,1)S(1)}, u32[]{:S(2)}, u32[]{:S(2)}) %collective-permute-start.9) | collective-permute-done | bytes 213024 | tf_op jit(solution)/shard_map/ppermute | solution.py:44
  162.4 0.7 copy-done.5
  163.1 13.3 %shard_map.84 = (bf16[512,512]{1,0:T(8,128)(2,1)}, bf16[512,512]{1,0:T(8,128)(2,1)}) custom-call(bf16[32,3328]{1,0:T(8,128)(2,1)} %copy-done.6, bf16[64,3328]{1,0:T(8,128)(2,1)} %copy-done.8, bf16[64,3328]{1,0:T(8,128)(2,1)} %copy-done.14, bf16[64,3328]{1,0:T(8,128)(2,1)} %copy-done.10, bf16[32,3328]{1,0:T(8,128)(2,1)} %collective-permute-done.5.refs_4_, ...), custom_call_target="tpu_custom_call" | custom-call | tf_op jit(solution)/shard_map/pallas_call | solution.py:262
  176.4 2.1 %collective-permute-start.19 = (bf16[512,512]{1,0:T(8,128)(2,1)}, bf16[512,512]{1,0:T(8,128)(2,1)S(1)}, u32[]{:S(2)}, u32[]{:S(2)}) collective-permute-start(bf16[512,512]{1,0:T(8,128)(2,1)} %get-tuple-element.8), channel_id=1, source_target_pairs={{0,32},{1,33},{2,34},{3,35},{4,36},{5,37},{6,38},{7,39},{8,40},{9,... | collective-permute-start | bytes 1572872 | tf_op jit(solution)/shard_map/ppermute | solution.py:44
  178.6 0.7 dynamic-slice_bitcast_fusion.column
  179.3 1.2 collective-permute-done.19.second
  180.5 1.0 copy-done
  181.5 4.0 %shard_map.85 = bf16[32,32,128]{2,1,0:T(8,128)(2,1)} custom-call(s32[32]{0:T(128)S(1)} %dynamic-slice_bitcast_fusion.column, bf16[512,512]{1,0:T(8,128)(2,1)S(1)} %copy-done, bf16[512,512]{1,0:T(8,128)(2,1)S(1)} %collective-permute-done.19.second), custom_call_target="tpu_custom_call" | custom-call | tf_op jit(solution)/shard_map/pallas_call | solution.py:274
  185.5 4.1 %all-to-all-start.1 = ((bf16[32,32,128]{2,1,0:T(8,128)(2,1)}), bf16[32,32,128]{2,1,0:T(8,128)(2,1)S(1)}, u32[]{:S(2)}, u32[]{:S(2)}) async-start(bf16[32,32,128]{2,1,0:T(8,128)(2,1)} %shard_map.85), calls=%async_computation.1 | async-start | bytes 524288 | tf_op jit(solution)/shard_map/all_to_all | solution.py:282
  189.6 9.7 %all-to-all-done.1 = bf16[32,32,128]{2,1,0:T(8,128)(2,1)S(1)} async-done(((bf16[32,32,128]{2,1,0:T(8,128)(2,1)}), bf16[32,32,128]{2,1,0:T(8,128)(2,1)S(1)}, u32[]{:S(2)}, u32[]{:S(2)}) %all-to-all-start.1) | async-done | bytes 262176 | tf_op jit(solution)/shard_map/all_to_all | solution.py:282
  199.3 5.6 %collective-permute-start.20 = (bf16[16,32,128]{2,1,0:T(8,128)(2,1)S(1)}, bf16[16,32,128]{2,1,0:T(8,128)(2,1)S(1)}, u32[]{:S(2)}, u32[]{:S(2)}) collective-permute-start(bf16[16,32,128]{2,1,0:T(8,128)(2,1)S(1)} %broadcast_select_fusion.2), channel_id=1, source_target_pairs={{0,32},{1,33},{2,34},{3,35},{4,36},{5,37},{6,38},{7,39},{8,40},{9,... | collective-permute-start | bytes 393224 | tf_op jit(solution)/shard_map/ppermute | solution.py:44
  204.9 1.0 collective-permute-done.20
  205.9 0.7 copy_bitcast_fusion
  (61 shorter events, 4.8 us)
Async XLA Ops:
  0.7 1.0 copy-start.1
  1.7 0.7 copy-start.2
  2.5 0.7 copy-start.3
  3.1 0.7 copy-start.4
  4.5 11.4 %copy-start.18 = (s32[1,32]{1,0:T(1,128)S(1)}, s32[1,32]{1,0:T(1,128)}, u32[]{:S(2)}) copy-start(s32[1,32]{1,0:T(1,128)} %param.11) | copy-start | bytes 388
  5.6 33.3 %all-to-all-start = ((bf16[16,4,6272]{2,1,0:T(4,128)(2,1)}), bf16[16,4,6272]{2,1,0:T(4,128)(2,1)S(1)}, u32[]{:S(2)}, u32[]{:S(2)}) async-start(bf16[16,4,6272]{2,1,0:T(4,128)(2,1)} %reshape.16), calls=%async_computation | async-start | bytes 1605632 | tf_op jit(solution)/shard_map/all_to_all | solution.py:219
  39.4 11.4 %collective-permute-start = (bf16[32,6272]{1,0:T(8,128)(2,1)S(1)}, bf16[32,6272]{1,0:T(8,128)(2,1)S(1)}, u32[]{:S(2)}, u32[]{:S(2)}) collective-permute-start(bf16[32,6272]{1,0:T(8,128)(2,1)S(1)} %shard_map.83), channel_id=1, source_target_pairs={{0,0},{1,1},{2,2},{3,3},{4,4},{5,5},{6,6},{7,7},{8,8},{9,9},{10,10... | collective-permute-start | bytes 1204232 | tf_op jit(solution)/shard_map/ppermute | solution.py:44
  43.2 56.5 %collective-permute-start.16 = (bf16[3,3072,128]{2,1,0:T(8,128)(2,1)S(1)}, bf16[3,3072,128]{2,1,0:T(8,128)(2,1)}, u32[]{:S(2)}, u32[]{:S(2)}) collective-permute-start(bf16[3,3072,128]{2,1,0:T(8,128)(2,1)S(1)} %constant_dynamic-slice_fusion), channel_id=1, source_target_pairs={{0,24},{1,25},{2,26},{3,27},{4,28},{5,29},{6,30},{7,31},{8,16},{9,... | collective-permute-start | bytes 7077896 | tf_op jit(solution)/shard_map/ppermute | solution.py:44
  50.8 12.9 %collective-permute-start.1 = (bf16[32,6272]{1,0:T(8,128)(2,1)S(1)}, bf16[32,6272]{1,0:T(8,128)(2,1)S(1)}, u32[]{:S(2)}, u32[]{:S(2)}) collective-permute-start(bf16[32,6272]{1,0:T(8,128)(2,1)S(1)} %collective-permute-done), channel_id=1, source_target_pairs={{0,32},{1,33},{2,34},{3,35},{4,36},{5,37},{6,38},{7,39},{8,40},{9,... | collective-permute-start | bytes 1204232 | tf_op jit(solution)/shard_map/ppermute | solution.py:44
  52.8 7.8 %collective-permute-start.10 = (bf16[32,2944]{1,0:T(8,128)(2,1)S(1)}, bf16[32,2944]{1,0:T(8,128)(2,1)S(1)}, u32[]{:S(2)}, u32[]{:S(2)}) collective-permute-start(bf16[32,2944]{1,0:T(8,128)(2,1)S(1)} %slice.47), channel_id=1, source_target_pairs={{0,8},{1,9},{2,10},{3,11},{4,12},{5,13},{6,14},{7,15},{8,0},{9,1},... | collective-permute-start | bytes 565256 | tf_op jit(solution)/shard_map/ppermute | solution.py:44
  60.6 4.2 %collective-permute-start.11 = (bf16[32,2944]{1,0:T(8,128)(2,1)S(1)}, bf16[32,2944]{1,0:T(8,128)(2,1)S(1)}, u32[]{:S(2)}, u32[]{:S(2)}) collective-permute-start(bf16[32,2944]{1,0:T(8,128)(2,1)S(1)} %collective-permute-done.10), channel_id=1, source_target_pairs={{0,32},{1,33},{2,34},{3,35},{4,36},{5,37},{6,38},{7,39},{8,40},{9,... | collective-permute-start | bytes 565256 | tf_op jit(solution)/shard_map/ppermute | solution.py:44
  63.8 50.5 %copy-start.16 = (f32[2,128]{1,0:T(2,128)S(1)}, f32[2,128]{1,0:T(2,128)}, u32[]{:S(2)}) copy-start(f32[2,128]{1,0:T(2,128)} %refs_22_.1) | copy-start | bytes 3076
  64.8 66.9 %copy-start.7 = (bf16[128,2944]{1,0:T(8,128)(2,1)}, bf16[128,2944]{1,0:T(8,128)(2,1)S(1)}, u32[]{:S(2)}) copy-start(bf16[128,2944]{1,0:T(8,128)(2,1)S(1)} %pad_maximum_fusion.refs_9_) | copy-start | bytes 2260996
  64.8 17.1 %collective-permute-start.12 = (bf16[128,2944]{1,0:T(8,128)(2,1)S(1)}, bf16[128,2944]{1,0:T(8,128)(2,1)S(1)}, u32[]{:S(2)}, u32[]{:S(2)}) collective-permute-start(bf16[128,2944]{1,0:T(8,128)(2,1)S(1)} %pad_maximum_fusion.refs_9_), channel_id=1, source_target_pairs={{0,1},{1,2},{2,3},{3,4},{4,5},{5,6},{6,7},{7,0},{8,9},{9,10},{10,1... | collective-permute-start | bytes 2261000 | tf_op jit(solution)/shard_map/ppermute | solution.py:44
  73.4 63.4 %copy-start.6 = (bf16[32,3328]{1,0:T(8,128)(2,1)}, bf16[32,3328]{1,0:T(8,128)(2,1)S(1)}, u32[]{:S(2)}) copy-start(bf16[32,3328]{1,0:T(8,128)(2,1)S(1)} %slice.44.refs_0_) | copy-start | bytes 638980
  81.9 54.9 %copy-start.11 = (bf16[128,2944]{1,0:T(8,128)(2,1)}, bf16[128,2944]{1,0:T(8,128)(2,1)S(1)}, u32[]{:S(2)}) copy-start(bf16[128,2944]{1,0:T(8,128)(2,1)S(1)} %collective-permute-done.12.refs_10_) | copy-start | bytes 2260996
  81.9 30.1 %collective-permute-start.13 = (bf16[128,2944]{1,0:T(8,128)(2,1)S(1)}, bf16[128,2944]{1,0:T(8,128)(2,1)S(1)}, u32[]{:S(2)}, u32[]{:S(2)}) collective-permute-start(bf16[128,2944]{1,0:T(8,128)(2,1)S(1)} %collective-permute-done.12.refs_10_), channel_id=1, source_target_pairs={{0,1},{1,2},{2,3},{3,4},{4,5},{5,6},{6,7},{7,0},{8,9},{9,10},{10,1... | collective-permute-start | bytes 2261000 | tf_op jit(solution)/shard_map/ppermute | solution.py:44
  87.4 15.7 %collective-permute-start.2 = (bf16[64,3328]{1,0:T(8,128)(2,1)S(1)}, bf16[64,3328]{1,0:T(8,128)(2,1)S(1)}, u32[]{:S(2)}, u32[]{:S(2)}) collective-permute-start(bf16[64,3328]{1,0:T(8,128)(2,1)S(1)} %pad_maximum_fusion.2), channel_id=1, source_target_pairs={{0,1},{1,2},{2,3},{3,4},{4,5},{5,6},{6,7},{7,0},{8,9},{9,10},{10,1... | collective-permute-start | bytes 1277960 | tf_op jit(solution)/shard_map/ppermute | solution.py:44
  99.7 62.0 %collective-permute-start.17 = (bf16[3,3072,128]{2,1,0:T(8,128)(2,1)}, bf16[3,3072,128]{2,1,0:T(8,128)(2,1)}, u32[]{:S(2)}, u32[]{:S(2)}) collective-permute-start(bf16[3,3072,128]{2,1,0:T(8,128)(2,1)} %collective-permute-done.16.refs_20_), channel_id=1, source_target_pairs={{0,32},{1,33},{2,34},{3,35},{4,36},{5,37},{6,38},{7,39},{8,40},{9,... | collective-permute-start | bytes 7077896 | tf_op jit(solution)/shard_map/ppermute | solution.py:44
  103.1 37.2 %copy-start.8 = (bf16[64,3328]{1,0:T(8,128)(2,1)}, bf16[64,3328]{1,0:T(8,128)(2,1)S(1)}, u32[]{:S(2)}) copy-start(bf16[64,3328]{1,0:T(8,128)(2,1)S(1)} %collective-permute-done.2.refs_1_) | copy-start | bytes 1277956
  103.1 14.0 %collective-permute-start.3 = (bf16[64,3328]{1,0:T(8,128)(2,1)S(1)}, bf16[64,3328]{1,0:T(8,128)(2,1)S(1)}, u32[]{:S(2)}, u32[]{:S(2)}) collective-permute-start(bf16[64,3328]{1,0:T(8,128)(2,1)S(1)} %collective-permute-done.2.refs_1_), channel_id=1, source_target_pairs={{0,1},{1,2},{2,3},{3,4},{4,5},{5,6},{6,7},{7,0},{8,9},{9,10},{10,1... | collective-permute-start | bytes 1277960 | tf_op jit(solution)/shard_map/ppermute | solution.py:44
  112.0 28.2 %copy-start.12 = (bf16[128,2944]{1,0:T(8,128)(2,1)}, bf16[128,2944]{1,0:T(8,128)(2,1)S(1)}, u32[]{:S(2)}) copy-start(bf16[128,2944]{1,0:T(8,128)(2,1)S(1)} %collective-permute-done.13.refs_11_) | copy-start | bytes 2260996
  112.1 19.6 %collective-permute-start.14 = (bf16[128,2944]{1,0:T(8,128)(2,1)S(1)}, bf16[128,2944]{1,0:T(8,128)(2,1)S(1)}, u32[]{:S(2)}, u32[]{:S(2)}) collective-permute-start(bf16[128,2944]{1,0:T(8,128)(2,1)S(1)} %collective-permute-done.13.refs_11_), channel_id=1, source_target_pairs={{0,1},{1,2},{2,3},{3,4},{4,5},{5,6},{6,7},{7,0},{8,9},{9,10},{10,1... | collective-permute-start | bytes 2261000 | tf_op jit(solution)/shard_map/ppermute | solution.py:44
  114.3 22.5 %collective-permute-start.18 = (f32[2,128]{1,0:T(2,128)S(1)}, f32[2,128]{1,0:T(2,128)S(1)}, u32[]{:S(2)}, u32[]{:S(2)}) collective-permute-start(f32[2,128]{1,0:T(2,128)S(1)} %copy-done.16), channel_id=1, source_target_pairs={{0,24},{1,25},{2,26},{3,27},{4,28},{5,29},{6,30},{7,31},{8,16},{9,... | collective-permute-start | bytes 3080 | tf_op jit(solution)/shard_map/ppermute | solution.py:44
  117.1 23.2 %copy-start.14 = (bf16[64,3328]{1,0:T(8,128)(2,1)}, bf16[64,3328]{1,0:T(8,128)(2,1)S(1)}, u32[]{:S(2)}) copy-start(bf16[64,3328]{1,0:T(8,128)(2,1)S(1)} %collective-permute-done.3.refs_2_) | copy-start | bytes 1277956
  117.1 12.6 %collective-permute-start.4 = (bf16[64,3328]{1,0:T(8,128)(2,1)S(1)}, bf16[64,3328]{1,0:T(8,128)(2,1)S(1)}, u32[]{:S(2)}, u32[]{:S(2)}) collective-permute-start(bf16[64,3328]{1,0:T(8,128)(2,1)S(1)} %collective-permute-done.3.refs_2_), channel_id=1, source_target_pairs={{0,1},{1,2},{2,3},{3,4},{4,5},{5,6},{6,7},{7,0},{8,9},{9,10},{10,1... | collective-permute-start | bytes 1277960 | tf_op jit(solution)/shard_map/ppermute | solution.py:44
  122.3 18.5 %collective-permute-start.6 = (bf16[96,3328]{1,0:T(8,128)(2,1)S(1)}, bf16[96,3328]{1,0:T(8,128)(2,1)S(1)}, u32[]{:S(2)}, u32[]{:S(2)}) collective-permute-start(bf16[96,3328]{1,0:T(8,128)(2,1)S(1)} %pad_maximum_fusion.1), channel_id=1, source_target_pairs={{0,8},{1,9},{2,10},{3,11},{4,12},{5,13},{6,14},{7,15},{8,0},{9,1},... | collective-permute-start | bytes 1916936 | tf_op jit(solution)/shard_map/ppermute | solution.py:44
  129.7 32.0 %copy-start.10 = (bf16[64,3328]{1,0:T(8,128)(2,1)}, bf16[64,3328]{1,0:T(8,128)(2,1)S(1)}, u32[]{:S(2)}) copy-start(bf16[64,3328]{1,0:T(8,128)(2,1)S(1)} %collective-permute-done.4.refs_3_) | copy-start | bytes 1277956
  129.7 20.1 %collective-permute-start.7 = (bf16[64,3328]{1,0:T(8,128)(2,1)S(1)}, bf16[64,3328]{1,0:T(8,128)(2,1)}, u32[]{:S(2)}, u32[]{:S(2)}) collective-permute-start(bf16[64,3328]{1,0:T(8,128)(2,1)S(1)} %collective-permute-done.3.refs_2_), channel_id=1, source_target_pairs={{0,8},{1,9},{2,10},{3,11},{4,12},{5,13},{6,14},{7,15},{8,0},{9,1},... | collective-permute-start | bytes 1277960 | tf_op jit(solution)/shard_map/ppermute | solution.py:44
  131.7 30.0 %copy-start.9 = (bf16[128,2944]{1,0:T(8,128)(2,1)}, bf16[128,2944]{1,0:T(8,128)(2,1)S(1)}, u32[]{:S(2)}) copy-start(bf16[128,2944]{1,0:T(8,128)(2,1)S(1)} %collective-permute-done.14.refs_12_) | copy-start | bytes 2260996
  131.7 11.8 %collective-permute-start.5 = (bf16[32,3328]{1,0:T(8,128)(2,1)S(1)}, bf16[32,3328]{1,0:T(8,128)(2,1)}, u32[]{:S(2)}, u32[]{:S(2)}) collective-permute-start(bf16[32,3328]{1,0:T(8,128)(2,1)S(1)} %slice.46), channel_id=1, source_target_pairs={{0,1},{1,2},{2,3},{3,4},{4,5},{5,6},{6,7},{7,0},{8,9},{9,10},{10,1... | collective-permute-start | bytes 638984 | tf_op jit(solution)/shard_map/ppermute | solution.py:44
  136.8 24.9 %copy-start.17 = (f32[2,128]{1,0:T(2,128)}, f32[2,128]{1,0:T(2,128)S(1)}, u32[]{:S(2)}) copy-start(f32[2,128]{1,0:T(2,128)S(1)} %collective-permute-done.18.refs_23_) | copy-start | bytes 3076
  136.8 24.9 %collective-permute-start.8 = (bf16[64,3328]{1,0:T(8,128)(2,1)S(1)}, bf16[64,3328]{1,0:T(8,128)(2,1)}, u32[]{:S(2)}, u32[]{:S(2)}) collective-permute-start(bf16[64,3328]{1,0:T(8,128)(2,1)S(1)} %collective-permute-done.4.refs_3_), channel_id=1, source_target_pairs={{0,8},{1,9},{2,10},{3,11},{4,12},{5,13},{6,14},{7,15},{8,0},{9,1},... | collective-permute-start | bytes 1277960 | tf_op jit(solution)/shard_map/ppermute | solution.py:44
  140.7 0.9 copy-start.13
  141.6 20.1 %collective-permute-start.15 = (bf16[64,2944]{1,0:T(8,128)(2,1)S(1)}, bf16[64,2944]{1,0:T(8,128)(2,1)S(1)}, u32[]{:S(2)}, u32[]{:S(2)}) collective-permute-start(bf16[64,2944]{1,0:T(8,128)(2,1)S(1)} %pad_maximum_fusion.3), channel_id=1, source_target_pairs={{0,1},{1,2},{2,3},{3,4},{4,5},{5,6},{6,7},{7,0},{8,9},{9,10},{10,1... | collective-permute-start | bytes 1130504 | tf_op jit(solution)/shard_map/ppermute | solution.py:44
  143.5 18.2 %collective-permute-start.9 = (bf16[32,3328]{1,0:T(8,128)(2,1)}, bf16[32,3328]{1,0:T(8,128)(2,1)S(1)}, u32[]{:S(2)}, u32[]{:S(2)}) collective-permute-start(bf16[32,3328]{1,0:T(8,128)(2,1)} %collective-permute-done.5.refs_4_), channel_id=1, source_target_pairs={{0,8},{1,9},{2,10},{3,11},{4,12},{5,13},{6,14},{7,15},{8,0},{9,1},... | collective-permute-start | bytes 638984 | tf_op jit(solution)/shard_map/ppermute | solution.py:44
  161.7 0.7 copy-start.15
  162.4 0.7 copy-start.5
  176.4 4.0 %collective-permute-start.19 = (bf16[512,512]{1,0:T(8,128)(2,1)}, bf16[512,512]{1,0:T(8,128)(2,1)S(1)}, u32[]{:S(2)}, u32[]{:S(2)}) collective-permute-start(bf16[512,512]{1,0:T(8,128)(2,1)} %get-tuple-element.8), channel_id=1, source_target_pairs={{0,32},{1,33},{2,34},{3,35},{4,36},{5,37},{6,38},{7,39},{8,40},{9,... | collective-permute-start | bytes 1572872 | tf_op jit(solution)/shard_map/ppermute | solution.py:44
  180.5 1.0 copy-start
  185.5 13.7 %all-to-all-start.1 = ((bf16[32,32,128]{2,1,0:T(8,128)(2,1)}), bf16[32,32,128]{2,1,0:T(8,128)(2,1)S(1)}, u32[]{:S(2)}, u32[]{:S(2)}) async-start(bf16[32,32,128]{2,1,0:T(8,128)(2,1)} %shard_map.85), calls=%async_computation.1 | async-start | bytes 524288 | tf_op jit(solution)/shard_map/all_to_all | solution.py:282
  199.3 6.6 %collective-permute-start.20 = (bf16[16,32,128]{2,1,0:T(8,128)(2,1)S(1)}, bf16[16,32,128]{2,1,0:T(8,128)(2,1)S(1)}, u32[]{:S(2)}, u32[]{:S(2)}) collective-permute-start(bf16[16,32,128]{2,1,0:T(8,128)(2,1)S(1)} %broadcast_select_fusion.2), channel_id=1, source_target_pairs={{0,32},{1,33},{2,34},{3,35},{4,36},{5,37},{6,38},{7,39},{8,40},{9,... | collective-permute-start | bytes 393224 | tf_op jit(solution)/shard_map/ppermute | solution.py:44

commit v2 on v0

v2 whole, which is shorter than its diff:
```python
import functools

import jax
import jax.numpy as jnp
from jax import lax
from jax.experimental import pallas as pl
from jax.experimental.pallas import tpu as pltpu
from jax.sharding import Mesh
from jax.sharding import PartitionSpec as P

HD = 128
LANES = 128
NX, NZ = 4, 8
AXES = ("y", "core", "half", "side", "z")
BF16 = jnp.bfloat16
F32 = jnp.float32
VMEM = pltpu.VMEM
SMEM = pltpu.SMEM


def vmem_call(body, outs, n_in, scratch=(), smem_in=(), hbm_in=(), limit=48):
    spaces = [SMEM if i in smem_in else pl.ANY if i in hbm_in else VMEM for i in range(n_in)]
    return pl.pallas_call(
        body,
        out_shape=outs,
        in_specs=[pl.BlockSpec(memory_space=space) for space in spaces],
        out_specs=jax.tree.map(lambda _: pl.BlockSpec(memory_space=VMEM), outs),
        scratch_shapes=scratch,
        compiler_params=pltpu.CompilerParams(vmem_limit_bytes=limit << 20),
    )


def pairs(n_dp, move):
    out = []
    for dp in range(n_dp):
        for mp in range(NX * NZ):
            to = move(dp % 2, mp // NZ, mp % NZ)
            if to is None:
                continue
            c, x, z = to
            out.append((dp * NX * NZ + mp, (dp // 2 * 2 + c) * NX * NZ + x * NZ + z))
    return out


def send(array, n_dp, move):
    return lax.ppermute(array, AXES, pairs(n_dp, move))


def other_core(c, x, z):
    return 1 - c, x, z


def to_region(c, x, z):
    return None if c == x // 2 else (1 - c, 3 - x, z)


def after(array, *earlier):
    return lax.optimization_barrier((array, *earlier))[0]


def norm_rows(values, gain):
    mean = jnp.mean(values, axis=-1, keepdims=True)
    centered = values - mean
    spread = jnp.mean(centered * centered, axis=-1, keepdims=True)
    return (centered * lax.rsqrt(spread + 1e-06) * gain).astype(BF16)


def pack_body(rows, group_row, slot_row, gain, out):
    tok, width = rows.shape
    groups, capacity, _ = out.shape
    slots = groups * capacity
    normed = norm_rows(rows[...].astype(F32), gain[...])
    i = lax.broadcasted_iota(jnp.int32, (tok, tok), 0)
    j = lax.broadcasted_iota(jnp.int32, (tok, tok), 1)
    across = jnp.broadcast_to(group_row[...], (tok, tok)).astype(F32)
    down = jnp.sum(jnp.where(i == j, across, 0.0), axis=1, keepdims=True)
    rank = jnp.sum(jnp.where((down == across) & (i < j), 1, 0), axis=0, keepdims=True)
    target = group_row[...] * capacity + rank
    hit = lax.broadcasted_iota(jnp.int32, (slots, tok), 0) == target
    onehot = jnp.where(hit, 1.0, 0.0)
    sent = jnp.dot(onehot.astype(BF16), normed, preferred_element_type=F32).astype(BF16)
    slot = jnp.sum(onehot * (slot_row[...].astype(F32) + 1.0), axis=1, keepdims=True) - 1.0
    slot = jnp.broadcast_to(slot, (slots, LANES)).astype(BF16)
    for g in range(groups):
        out[g, :, :width] = sent[g * capacity : (g + 1) * capacity, :]
        out[g, :, width:] = slot[g * capacity : (g + 1) * capacity, :]


def place_body(got, ids_col, out):
    tok = out.shape[0]
    width = out.shape[1] - LANES
    slot = got[:, width:].astype(F32)[:, :tok]
    hit = slot == lax.broadcasted_iota(jnp.int32, slot.shape, 1).astype(F32)
    onehot = jnp.where(hit, 1.0, 0.0).astype(BF16)
    out[:, :width] = lax.dot_general(
        onehot, got[:, :width], (((0,), (0,)), ((), ())), preferred_element_type=F32
    ).astype(BF16)
    out[:, width:] = jnp.broadcast_to(ids_col[...].astype(F32), (tok, LANES)).astype(BF16)


def attend_body(place, tokens, ids, weight, gain, out, total, normed, ids_row):
    k = pl.program_id(0)
    rows = tokens.shape[0]
    tok = out.shape[1]
    three = jnp.concatenate([weight[j] for j in range(3)], axis=1)
    part = jnp.dot(tokens[...], three, preferred_element_type=F32)

    @pl.when(k == 0)
    def _():
        total[...] = part
        ids_row[...] = jnp.transpose(ids[...].astype(F32))[0:8, :]

    @pl.when(k > 0)
    def _():
        total[...] += part

    @pl.when(k == pl.num_programs(0) - 1)
    def _():
        for j in range(2):
            cols = slice(j * HD, (j + 1) * HD)
            normed[:, cols] = norm_rows(total[:, cols], gain[j : j + 1, :])
        normed[:, 2 * HD :] = total[:, 2 * HD :].astype(BF16)
        key, value = normed[:, HD : 2 * HD], normed[:, 2 * HD :]
        half = place[0]
        step = min(256, rows)
        for at in range(0, rows, step):
            scores = lax.dot_general(
                normed[at : at + step, :HD], key, (((1,), (1,)), ((), ())), preferred_element_type=F32
            ) * HD ** (-0.5)
            same = ids[at : at + step, 0:1].astype(F32) == ids_row[0:1, :]
            masked = jnp.where(same, scores, -1e30)
            top = jnp.max(masked, axis=-1, keepdims=True)
            weights = jnp.exp(masked - top)
            probs = (weights / jnp.sum(weights, axis=-1, keepdims=True)).astype(BF16)
            result = jnp.dot(probs, value, preferred_element_type=F32).astype(BF16)
            for b in range(step // tok):
                block = at // tok + b
                core, side, z = block // (2 * NZ), block // NZ % 2, block % NZ
                x = jnp.where(half == core, 2 * half + side, 3 - 2 * half - side)
                out[x * NZ + z] = result[b * tok : (b + 1) * tok, :]


def local(packed_rows, dest_group, dest_slot, image_ids, ln_gain, qkv_weight, qk_gain):
    tok, width = packed_rows.shape
    n_dp = 2 * lax.axis_size("y")
    capacity = max(2, 2 * tok // n_dp)
    c = lax.axis_index("core")
    on_half = lax.axis_index("half")
    home = c == on_half
    go = functools.partial(lambda array, move: send(array, n_dp, move))

    packed = pl.pallas_call(
        pack_body,
        grid=(1,),
        out_shape=jax.ShapeDtypeStruct((n_dp, capacity, width + LANES), BF16),
        compiler_params=pltpu.CompilerParams(vmem_limit_bytes=32 << 20),
    )(packed_rows, dest_group[None, :], dest_slot[None, :], ln_gain[None, :])
    got = lax.all_to_all(packed, ("y", "core"), split_axis=0, concat_axis=0, tiled=True)
    placed = vmem_call(
        place_body, jax.ShapeDtypeStruct((tok, width + LANES), BF16), 2
    )(got.reshape(n_dp * capacity, width + LANES), image_ids.reshape(tok, 1))

    moved = jnp.where(home, placed, go(placed, to_region))
    gathered = lax.all_gather(moved, ("core", "side", "z"), axis=0, tiled=True)
    weight = jnp.where(home, qkv_weight, go(after(qkv_weight, moved), to_region))
    gain = jnp.where(home, qk_gain, go(after(qk_gain, moved), to_region))

    rows = gathered.shape[0]
    step = width // 6
    result = pl.pallas_call(
        attend_body,
        grid=(width // step,),
        out_shape=jax.ShapeDtypeStruct((rows // tok, tok, HD), BF16),
        in_specs=[
            pl.BlockSpec(memory_space=SMEM),
            pl.BlockSpec((rows, step), lambda k: (0, k)),
            pl.BlockSpec((rows, LANES), lambda k: (0, width // LANES)),
            pl.BlockSpec((3, step, HD), lambda k: (0, k, 0)),
            pl.BlockSpec(memory_space=VMEM),
        ],
        out_specs=pl.BlockSpec(memory_space=VMEM),
        scratch_shapes=[
            VMEM((rows, 3 * HD), F32), VMEM((rows, 3 * HD), BF16), VMEM((8, rows), F32)
        ],
        compiler_params=pltpu.CompilerParams(vmem_limit_bytes=48 << 20),
    )(on_half[None], gathered, gathered, weight, gain)

    back = lax.all_to_all(result, ("half", "side", "z"), split_axis=0, concat_axis=0, tiled=True)
    low, high = back[: NX * NZ // 2], back[NX * NZ // 2 :]
    first = c == 0
    keep = jnp.where(first, low, high)
    gave = go(jnp.where(first, high, low), other_core)
    gave = jnp.concatenate([gave[NZ:], gave[:NZ]], axis=0)
    heads = jnp.concatenate([jnp.where(first, keep, gave), jnp.where(first, gave, keep)], axis=0)
    return jnp.transpose(heads, (1, 0, 2)).reshape(tok, NX * NZ * HD)


def solution(mesh):
    n_dp = mesh.devices.shape[0]
    split = Mesh(mesh.devices.reshape(n_dp // 2, 2, 2, NX // 2, NZ), AXES)
    dp, mp = ("y", "core"), ("half", "side", "z")
    return jax.shard_map(
        local,
        mesh=split,
        in_specs=(P(AXES, None), P(AXES), P(AXES), P(dp, mp), P(), P(None, None, mp), P(None, mp)),
        out_specs=P(AXES, None),
        check_vma=False,
    )
```

time: 230 us -> 189 us (0.82)
  blocking collectives: 80.2 us -> 0 us
  waiting for transfers between devices: 72.3 us -> 115 us
  local copies, waits for them, and re-layouts: 23.5 us -> 6.32 us
  Pallas kernels: 0 us -> 16.6 us
  starting transfers between devices: 17.5 us -> 32.8 us
  matrix products: 12.9 us -> 0 us
  other arithmetic: 7.15 us -> 4.33 us
    unnamed x1 -> x0, blocking collectives: 65.6 us -> none
    ppermute x0 -> x4, waiting for transfers between devices: none -> 59.5 us  [send(): return lax.ppermute(array, AXES, pairs(n_dp, move))]
    all_gather x1, waiting for transfers between devices: 49.8 us -> 23.2 us  [local(): gathered = lax.all_gather(moved, ('core', 'side', 'z'), axis=0, tiled=True)]
    pallas_call x0 -> x3, Pallas kernels: none -> 16.6 us  [the longest x1 14.7 us: local(): pl.pallas_call(attend_body, grid=(width // step,), out_shape=jax.ShapeDty...]
    all_to_all x1 -> x0, blocking collectives: 14.6 us -> none  [local(): return lax.all_to_all(result, 'mp', split_axis=0, concat_axis=1, tiled=True)]
    ppermute x0 -> x4, starting transfers between devices: none -> 14 us  [send(): return lax.ppermute(array, AXES, pairs(n_dp, move))]
    scatter x2 -> x0, local copies, waits for them, and re-layouts: 12.3 us -> none  [the longest x1 10.2 us: local(): jnp.zeros((n_groups, capacity, width), jnp.bfloat16).at[dest_group, rank]]
    all_to_all x2, waiting for transfers between devices: 22.5 us -> 32.2 us  [the longest x1 22.3 us: local(): lax.all_to_all(packed, ('y', 'core'), split_axis=0, concat_axis=0, tiled=...]
  transfers between devices with their start and end apart: 3 -> 7, of which waited for: 2 -> 6; matrix products, arithmetic and copies ran while one was open for 10% -> 2% of each run, Pallas kernels for 0% -> 0%
where the time goes in v2:
time: 189 us; the launch traced here: 188 us
  waiting for transfers between devices  115 us (61%)
  starting transfers between devices  32.8 us (17%)
  Pallas kernels  16.6 us (9%)
  between operations  13.5 us (7%)
  local copies, waits for them, and re-layouts  6.32 us (3%)
  other arithmetic  4.33 us (2%)
    ppermute x4, waiting for transfers between devices, send(): return lax.ppermute(array, AXES, pairs(n_dp, move))  59.5 us
    all_gather x1, waiting for transfers between devices, local(): gathered = lax.all_gather(moved, ('core', 'side', 'z'), axis=0, tiled=True)  23.2 us
    all_to_all x1, waiting for transfers between devices, local(): lax.all_to_all(packed, ('y', 'core'), split_axis=0, concat_axis=0, tiled=...  22.3 us
    pallas_call x1, Pallas kernels, local(): pl.pallas_call(attend_body, grid=(width // step,), out_shape=jax.ShapeDty...  14.7 us
    ppermute x4, starting transfers between devices, send(): return lax.ppermute(array, AXES, pairs(n_dp, move))  14 us
    all_to_all x1, starting transfers between devices, local(): lax.all_to_all(packed, ('y', 'core'), split_axis=0, concat_axis=0, tiled=...  10.3 us
    all_to_all x1, waiting for transfers between devices, local(): lax.all_to_all(result, ('half', 'side', 'z'), split_axis=0, concat_axis=0...  9.93 us
    all_to_all x1, starting transfers between devices, local(): lax.all_to_all(result, ('half', 'side', 'z'), split_axis=0, concat_axis=0...  8.46 us
  transfers between devices with their start and end apart: 7, of which 6 were waited for; matrix products, arithmetic and copies ran while one was open for 2% of the time, Pallas kernels for 0%

profile of v2, /device:TPU:1, one launch (start us, length us, event | category | flops | bytes accessed | tf_op | source)
XLA Modules:
  0.0 188.5 jit_solution(15168179459016613912)
XLA Ops:
  6.5 0.0 copy-start.5
  6.5 0.0 copy-start.1
  6.5 1.0 copy-done.1
  7.5 0.0 copy-start.2
  7.5 0.7 copy-done.2
  8.3 0.0 copy-start.3
  8.3 0.7 copy-done.3
  8.9 0.0 copy-start.4
  8.9 0.7 copy-done.4
  9.6 1.6 shard_map.73
  11.2 10.3 %all-to-all-start = ((bf16[16,4,6272]{2,1,0:T(4,128)(2,1)}), bf16[16,4,6272]{2,1,0:T(4,128)(2,1)S(1)}, u32[]{:S(2)}, u32[]{:S(2)}) async-start(bf16[16,4,6272]{2,1,0:T(4,128)(2,1)} %shard_map.73), calls=%async_computation | async-start | bytes 1605632 | tf_op jit(solution)/shard_map/all_to_all | solution.py:158
  21.5 0.0 all-gather.2.cloned.1.call-start
  21.5 0.7 copy.9.ids_col
  22.3 22.3 %all-to-all-done = bf16[16,4,6272]{2,1,0:T(4,128)(2,1)S(1)} async-done(((bf16[16,4,6272]{2,1,0:T(4,128)(2,1)}), bf16[16,4,6272]{2,1,0:T(4,128)(2,1)S(1)}, u32[]{:S(2)}, u32[]{:S(2)}) %all-to-all-start) | async-done | bytes 802848 | tf_op jit(solution)/shard_map/all_to_all | solution.py:158
  44.5 0.2 reshape.9.got
  44.7 0.3 shard_map.74
  45.0 1.9 %collective-permute-start = (bf16[32,6272]{1,0:T(8,128)(2,1)S(1)}, bf16[32,6272]{1,0:T(8,128)(2,1)S(1)}, u32[]{:S(2)}, u32[]{:S(2)}) collective-permute-start(bf16[32,6272]{1,0:T(8,128)(2,1)S(1)} %shard_map.74), channel_id=1, source_target_pairs={{16,40},{17,41},{18,42},{19,43},{20,44},{21,45},{22,46},{23,47},{2... | collective-permute-start | bytes 1204232 | tf_op jit(solution)/shard_map/ppermute | solution.py:46
  46.9 8.5 %collective-permute-done = bf16[32,6272]{1,0:T(8,128)(2,1)S(1)} collective-permute-done((bf16[32,6272]{1,0:T(8,128)(2,1)S(1)}, bf16[32,6272]{1,0:T(8,128)(2,1)S(1)}, u32[]{:S(2)}, u32[]{:S(2)}) %collective-permute-start) | collective-permute-done | bytes 401440 | tf_op jit(solution)/shard_map/ppermute | solution.py:46
  55.4 0.8 broadcast_select_fusion.1
  56.2 0.0 all-gather.2.cloned.1.call-update
  56.2 2.0 %collective-permute-start.1 = (bf16[3,6144,128]{2,1,0:T(8,128)(2,1)}, bf16[3,6144,128]{2,1,0:T(8,128)(2,1)S(1)}, u32[]{:S(2)}, u32[]{:S(2)}) collective-permute-start(bf16[3,6144,128]{2,1,0:T(8,128)(2,1)} %param.12), channel_id=1, source_target_pairs={{16,40},{17,41},{18,42},{19,43},{20,44},{21,45},{22,46},{23,47},{2... | collective-permute-start | bytes 14155784 | tf_op jit(solution)/shard_map/ppermute | solution.py:46
  58.2 0.0 copy-done.5
  58.2 4.8 %collective-permute-start.2 = (f32[2,128]{1,0:T(2,128)S(1)}, f32[2,128]{1,0:T(2,128)S(1)}, u32[]{:S(2)}, u32[]{:S(2)}) collective-permute-start(f32[2,128]{1,0:T(2,128)S(1)} %copy-done.5), channel_id=1, source_target_pairs={{16,40},{17,41},{18,42},{19,43},{20,44},{21,45},{22,46},{23,47},{2... | collective-permute-start | bytes 3080 | tf_op jit(solution)/shard_map/ppermute | solution.py:46
  63.0 50.1 %collective-permute-done.2 = f32[2,128]{1,0:T(2,128)S(1)} collective-permute-done((f32[2,128]{1,0:T(2,128)S(1)}, f32[2,128]{1,0:T(2,128)S(1)}, u32[]{:S(2)}, u32[]{:S(2)}) %collective-permute-start.2) | collective-permute-done | bytes 1056 | tf_op jit(solution)/shard_map/ppermute | solution.py:46
  113.2 0.0 collective-permute-done.1
  113.2 2.7 %broadcast_select_fusion.weight = bf16[3,6144,128]{2,1,0:T(8,128)(2,1)} fusion(bf16[3,6144,128]{2,1,0:T(8,128)(2,1)} %param.12, bf16[3,6144,128]{2,1,0:T(8,128)(2,1)S(1)} %collective-permute-done.1, pred[]{:T(512)S(6)} %eq.7), kind=kLoop, calls=%fused_computation | loop fusion | flops 2359296 | bytes 14155777 | tf_op jit(solution)/shard_map/jit(_where)/select_n | solution.py:165
  115.9 23.2 %all-gather.2.cloned.1.call-done.tokens.ids = bf16[1024,6272]{1,0:T(8,128)(2,1)} async-done(((bf16[32,6272]{1,0:T(8,128)(2,1)}), bf16[1024,6272]{1,0:T(8,128)(2,1)}) %all-gather.2.cloned.1.call-update) | async-done | bytes 12845072 | tf_op jit(solution)/shard_map/all_gather | solution.py:164
  139.1 0.0 copy-start
  139.1 2.3 %copy-done = bf16[3,6144,128]{2,1,0:T(8,128)(2,1)S(1)} copy-done((bf16[3,6144,128]{2,1,0:T(8,128)(2,1)S(1)}, bf16[3,6144,128]{2,1,0:T(8,128)(2,1)}, u32[]{:S(2)}) %copy-start) | copy-done | bytes 4718616
  141.4 14.7 %shard_map.75 = bf16[32,32,128]{2,1,0:T(8,128)(2,1)} custom-call(s32[1]{0:T(128)} %bitcast.place, bf16[1024,6272]{1,0:T(8,128)(2,1)} %all-gather.2.cloned.1.call-done.tokens.ids, bf16[1024,6272]{1,0:T(8,128)(2,1)} %all-gather.2.cloned.1.call-done.tokens.ids, bf16[3,6144,128]{2,1,0:T(8,128)(2,1)S(1)} %copy-done, f32[2,128]{1,0:T(2,128)S(1)} %broadcast_select_fusion.6.gain), custom_call_target="tpu_custom_call" | custom-call | tf_op jit(solution)/shard_map/pallas_call | solution.py:170
  156.1 8.5 %all-to-all-start.1 = ((bf16[32,32,128]{2,1,0:T(8,128)(2,1)}), bf16[32,32,128]{2,1,0:T(8,128)(2,1)S(1)}, u32[]{:S(2)}, u32[]{:S(2)}) async-start(bf16[32,32,128]{2,1,0:T(8,128)(2,1)} %shard_map.75), calls=%async_computation.1 | async-start | bytes 524288 | tf_op jit(solution)/shard_map/all_to_all | solution.py:188
  164.6 9.9 %all-to-all-done.1 = bf16[32,32,128]{2,1,0:T(8,128)(2,1)S(1)} async-done(((bf16[32,32,128]{2,1,0:T(8,128)(2,1)}), bf16[32,32,128]{2,1,0:T(8,128)(2,1)S(1)}, u32[]{:S(2)}, u32[]{:S(2)}) %all-to-all-start.1) | async-done | bytes 262176 | tf_op jit(solution)/shard_map/all_to_all | solution.py:188
  174.6 5.3 %collective-permute-start.3 = (bf16[16,32,128]{2,1,0:T(8,128)(2,1)S(1)}, bf16[16,32,128]{2,1,0:T(8,128)(2,1)S(1)}, u32[]{:S(2)}, u32[]{:S(2)}) collective-permute-start(bf16[16,32,128]{2,1,0:T(8,128)(2,1)S(1)} %broadcast_select_fusion.4), channel_id=1, source_target_pairs={{0,32},{1,33},{2,34},{3,35},{4,36},{5,37},{6,38},{7,39},{8,40},{9,... | collective-permute-start | bytes 393224 | tf_op jit(solution)/shard_map/ppermute | solution.py:46
  179.9 1.0 collective-permute-done.3
  180.9 0.7 copy_bitcast_fusion
  (4 shorter events, 0.1 us)
Async XLA Ops:
  6.5 51.7 %copy-start.5 = (f32[2,128]{1,0:T(2,128)S(1)}, f32[2,128]{1,0:T(2,128)}, u32[]{:S(2)}) copy-start(f32[2,128]{1,0:T(2,128)} %param.13) | copy-start | bytes 3076
  6.5 1.0 copy-start.1
  7.5 0.7 copy-start.2
  8.3 0.7 copy-start.3
  8.9 0.7 copy-start.4
  11.2 33.3 %all-to-all-start = ((bf16[16,4,6272]{2,1,0:T(4,128)(2,1)}), bf16[16,4,6272]{2,1,0:T(4,128)(2,1)S(1)}, u32[]{:S(2)}, u32[]{:S(2)}) async-start(bf16[16,4,6272]{2,1,0:T(4,128)(2,1)} %shard_map.73), calls=%async_computation | async-start | bytes 1605632 | tf_op jit(solution)/shard_map/all_to_all | solution.py:158
  21.5 117.6 %all-gather.2.cloned.1.call-start = ((), (), s32[]{:S(2)}) async-start(), calls=%async_computation.2 | async-start | bytes 13246464 | tf_op jit(solution)/shard_map/all_gather | solution.py:164
  45.0 10.4 %collective-permute-start = (bf16[32,6272]{1,0:T(8,128)(2,1)S(1)}, bf16[32,6272]{1,0:T(8,128)(2,1)S(1)}, u32[]{:S(2)}, u32[]{:S(2)}) collective-permute-start(bf16[32,6272]{1,0:T(8,128)(2,1)S(1)} %shard_map.74), channel_id=1, source_target_pairs={{16,40},{17,41},{18,42},{19,43},{20,44},{21,45},{22,46},{23,47},{2... | collective-permute-start | bytes 1204232 | tf_op jit(solution)/shard_map/ppermute | solution.py:46
  56.2 56.9 %collective-permute-start.1 = (bf16[3,6144,128]{2,1,0:T(8,128)(2,1)}, bf16[3,6144,128]{2,1,0:T(8,128)(2,1)S(1)}, u32[]{:S(2)}, u32[]{:S(2)}) collective-permute-start(bf16[3,6144,128]{2,1,0:T(8,128)(2,1)} %param.12), channel_id=1, source_target_pairs={{16,40},{17,41},{18,42},{19,43},{20,44},{21,45},{22,46},{23,47},{2... | collective-permute-start | bytes 14155784 | tf_op jit(solution)/shard_map/ppermute | solution.py:46
  58.2 54.9 %collective-permute-start.2 = (f32[2,128]{1,0:T(2,128)S(1)}, f32[2,128]{1,0:T(2,128)S(1)}, u32[]{:S(2)}, u32[]{:S(2)}) collective-permute-start(f32[2,128]{1,0:T(2,128)S(1)} %copy-done.5), channel_id=1, source_target_pairs={{16,40},{17,41},{18,42},{19,43},{20,44},{21,45},{22,46},{23,47},{2... | collective-permute-start | bytes 3080 | tf_op jit(solution)/shard_map/ppermute | solution.py:46
  139.1 2.3 %copy-start = (bf16[3,6144,128]{2,1,0:T(8,128)(2,1)S(1)}, bf16[3,6144,128]{2,1,0:T(8,128)(2,1)}, u32[]{:S(2)}) copy-start(bf16[3,6144,128]{2,1,0:T(8,128)(2,1)} %broadcast_select_fusion.weight) | copy-start | bytes 14155780
  156.1 18.4 %all-to-all-start.1 = ((bf16[32,32,128]{2,1,0:T(8,128)(2,1)}), bf16[32,32,128]{2,1,0:T(8,128)(2,1)S(1)}, u32[]{:S(2)}, u32[]{:S(2)}) async-start(bf16[32,32,128]{2,1,0:T(8,128)(2,1)} %shard_map.75), calls=%async_computation.1 | async-start | bytes 524288 | tf_op jit(solution)/shard_map/all_to_all | solution.py:188
  174.6 6.3 %collective-permute-start.3 = (bf16[16,32,128]{2,1,0:T(8,128)(2,1)S(1)}, bf16[16,32,128]{2,1,0:T(8,128)(2,1)S(1)}, u32[]{:S(2)}, u32[]{:S(2)}) collective-permute-start(bf16[16,32,128]{2,1,0:T(8,128)(2,1)S(1)} %broadcast_select_fusion.4), channel_id=1, source_target_pairs={{0,32},{1,33},{2,34},{3,35},{4,36},{5,37},{6,38},{7,39},{8,40},{9,... | collective-permute-start | bytes 393224 | tf_op jit(solution)/shard_map/ppermute | solution.py:46
Sparse Core Ops, SparseCore 0:
  56.4 82.6 all-gather.1

commit v3 on v2

v3 whole, which is shorter than its diff:
```python
import functools

import jax
import jax.numpy as jnp
from jax import lax
from jax.experimental import pallas as pl
from jax.experimental.pallas import tpu as pltpu
from jax.sharding import Mesh
from jax.sharding import PartitionSpec as P

HD = 128
LOG2_E = 1.4426950408889634
LANES = 128
NX, NZ = 4, 8
AXES = ("y", "core", "half", "side", "z")
BF16 = jnp.bfloat16
F32 = jnp.float32
VMEM = pltpu.VMEM
SMEM = pltpu.SMEM


def vmem_call(body, outs, n_in, scratch=(), smem_in=(), hbm_in=(), limit=48):
    spaces = [SMEM if i in smem_in else pl.ANY if i in hbm_in else VMEM for i in range(n_in)]
    return pl.pallas_call(
        body,
        out_shape=outs,
        in_specs=[pl.BlockSpec(memory_space=space) for space in spaces],
        out_specs=jax.tree.map(lambda _: pl.BlockSpec(memory_space=VMEM), outs),
        scratch_shapes=scratch,
        compiler_params=pltpu.CompilerParams(vmem_limit_bytes=limit << 20),
    )


def pairs(n_dp, move):
    out = []
    for dp in range(n_dp):
        for mp in range(NX * NZ):
            to = move(dp % 2, mp // NZ, mp % NZ)
            if to is None:
                continue
            c, x, z = to
            out.append((dp * NX * NZ + mp, (dp // 2 * 2 + c) * NX * NZ + x * NZ + z))
    return out


def send(array, n_dp, move):
    return lax.ppermute(array, AXES, pairs(n_dp, move))


def to_next(c, x, z):
    return (0, x ^ 1, z) if c == 0 else (1, 3 - x, z)


def opposite_x(c, x, z):
    return c, x ^ 2, z


def on_by_side(c, x, z):
    return (1, x ^ 1, z) if c == 1 else None


def on_by_mirror(c, x, z):
    return (1, 3 - x, z) if c == 0 else None


EXCHANGE = (
    lambda c, x, z: (1, x, z) if c == 0 else (0, 3 - x, z),
    lambda c, x, z: (0, x ^ 1, z) if c == 0 else (1, 3 - x, z),
    lambda c, x, z: (1, x ^ 1, z) if c == 0 else (0, x ^ 2, z),
    lambda c, x, z: None if c == 0 else (1, x ^ 2, z),
)


def after(array, *earlier):
    return lax.optimization_barrier((array, *earlier))[0]


def norm_rows(values, gain):
    mean = jnp.mean(values, axis=-1, keepdims=True)
    centered = values - mean
    spread = jnp.mean(centered * centered, axis=-1, keepdims=True)
    return (centered * lax.rsqrt(spread + 1e-06) * gain).astype(BF16)


def pack_body(rows, plan, weight, out, first_two, sem):
    copy = pltpu.make_async_copy(weight.at[0:2], first_two, sem)
    copy.start()
    tok, width = rows.shape
    groups, capacity, _ = out.shape
    slots = groups * capacity
    group_row, slot_row = plan[0:1, :], plan[1:2, :]
    i = lax.broadcasted_iota(jnp.int32, (tok, tok), 0)
    j = lax.broadcasted_iota(jnp.int32, (tok, tok), 1)
    across = jnp.broadcast_to(group_row, (tok, tok)).astype(F32)
    down = jnp.sum(jnp.where(i == j, across, 0.0), axis=1, keepdims=True)
    rank = jnp.sum(jnp.where((down == across) & (i < j), 1, 0), axis=0, keepdims=True)
    target = group_row * capacity + rank
    hit = lax.broadcasted_iota(jnp.int32, (slots, tok), 0) == target
    onehot = jnp.where(hit, 1.0, 0.0)
    sent = jnp.dot(onehot.astype(BF16), rows[...], preferred_element_type=F32).astype(BF16)
    slot = jnp.sum(onehot * (slot_row.astype(F32) + 1.0), axis=1, keepdims=True) - 1.0
    slot = jnp.broadcast_to(slot, (slots, LANES)).astype(BF16)
    for g in range(groups):
        out[g, :, :width] = sent[g * capacity : (g + 1) * capacity, :]
        out[g, :, width:] = slot[g * capacity : (g + 1) * capacity, :]
    copy.wait()


def place_body(got, ids_col, gain, out):
    tok = out.shape[0]
    width = out.shape[1] - LANES
    slot = got[:, width:].astype(F32)[:, :tok]
    hit = slot == lax.broadcasted_iota(jnp.int32, slot.shape, 1).astype(F32)
    onehot = jnp.where(hit, 1.0, 0.0).astype(BF16)
    grouped = lax.dot_general(
        onehot, got[:, :width], (((0,), (0,)), ((), ())), preferred_element_type=F32
    )
    out[:, :width] = norm_rows(grouped, gain[...])
    out[:, width:] = jnp.broadcast_to(ids_col[...].astype(F32), (tok, LANES)).astype(BF16)


def project_body(place, tokens, ids, own, nqk, nv, fq, fk, fv0, fv1, gain, *refs):
    outs, total = refs[:5], refs[5]
    k = pl.program_id(0)
    steps = pl.num_programs(0)
    rows = tokens.shape[0] // 2
    first_core = place[0] == 0
    near = [nqk[0], nqk[1], nv[...]]
    far = [fq[...], fk[...], jnp.where(k < steps // 2, fv0[...], fv1[...])]
    six = [jnp.where(first_core, own[j], near[j]) for j in range(3)]
    six += [jnp.where(first_core, near[j], far[j]) for j in range(3)]
    part = jnp.dot(tokens[...], jnp.concatenate(six, axis=1), preferred_element_type=F32)

    @pl.when(k == 0)
    def _():
        total[...] = part

    @pl.when(k > 0)
    def _():
        total[...] += part

    def emit(dsts):
        turned = jnp.transpose(ids[...].astype(F32))[0:16, :].astype(BF16)
        for n, dst in enumerate(dsts):
            head, group = n // 2, n % 2
            at = slice(group * rows, (group + 1) * rows)
            for j in range(2):
                cols = total[at, (3 * head + j) * HD : (3 * head + j + 1) * HD]
                dst[:rows, j * HD : (j + 1) * HD] = norm_rows(
                    cols, gain[2 * head + j : 2 * head + j + 1, :]
                )
            dst[:rows, 2 * HD :] = total[at, (3 * head + 2) * HD : (3 * head + 3) * HD].astype(BF16)
            dst[rows:, :rows] = turned[:, at]
            dst[rows:, rows:] = jnp.zeros((16, 3 * HD - rows), BF16)

    @pl.when((k == steps - 1) & first_core)
    def _():
        emit(outs[:4])
        outs[4][...] = jnp.zeros_like(outs[4])

    @pl.when((k == steps - 1) & jnp.logical_not(first_core))
    def _():
        outs[0][...] = jnp.zeros_like(outs[0])
        emit(outs[1:])


def attend_body(place, kept, got0, got1, got2, got3, out, qkv, ids_row, ids_col):
    rows = kept.shape[0] - 16
    tok = out.shape[1]
    per = rows // tok
    first_core = place[0] == 0
    for n, (a, b) in enumerate(((kept, got0), (got0, got1), (got1, got2), (got2, got3))):
        at = slice(n * rows, (n + 1) * rows)
        qkv[at, :] = jnp.where(first_core, a[:rows, :], b[:rows, :])
        packed = jnp.where(first_core, a[rows:, :rows], b[rows:, :rows]).astype(F32)
        ids_row[:, at] = packed[0:8, :]
    ids_col[...] = jnp.transpose(jnp.broadcast_to(ids_row[0:1, :], (LANES, 4 * rows)))
    key, value = qkv[:, HD : 2 * HD], qkv[:, 2 * HD :]
    x = place[1]
    side = x + 1 - 2 * (x % 2)
    columns = (x, 3 - x, side, 3 - side)
    for n in range(4):
        at = slice(n * rows, (n + 1) * rows)
        scores = lax.dot_general(
            qkv[at, :HD], key, (((1,), (1,)), ((), ())), preferred_element_type=F32
        )
        same = ids_col[at, 0:1] == ids_row[0:1, :]
        masked = jnp.where(same, scores, -1e30)
        top = jnp.max(masked, axis=-1, keepdims=True)
        weights = jnp.exp2((masked - top) * (HD ** (-0.5) * LOG2_E))
        scale = 1.0 / jnp.sum(weights, axis=-1, keepdims=True)
        probs = (weights * scale).astype(BF16)
        result = jnp.dot(probs, value, preferred_element_type=F32).astype(BF16)
        for z in range(per):
            out[columns[n] * per + z] = result[z * tok : (z + 1) * tok, :]


def local(packed_rows, dest_group, dest_slot, image_ids, ln_gain, qkv_weight, qk_gain):
    tok, width = packed_rows.shape
    n_dp = 2 * lax.axis_size("y")
    capacity = max(2, 2 * tok // n_dp)
    c = lax.axis_index("core")
    first_core = c == 0
    go = functools.partial(lambda array, move: send(array, n_dp, move))

    packed, qk_weight = pl.pallas_call(
        pack_body,
        out_shape=(
            jax.ShapeDtypeStruct((n_dp, capacity, width + LANES), BF16),
            jax.ShapeDtypeStruct((2, width, HD), BF16),
        ),
        in_specs=[
            pl.BlockSpec(memory_space=VMEM),
            pl.BlockSpec(memory_space=VMEM),
            pl.BlockSpec(memory_space=pltpu.HBM),
        ],
        out_specs=(pl.BlockSpec(memory_space=VMEM), pl.BlockSpec(memory_space=pltpu.HBM)),
        scratch_shapes=[pltpu.SemaphoreType.DMA],
        compiler_params=pltpu.CompilerParams(vmem_limit_bytes=32 << 20),
    )(packed_rows, jnp.stack([dest_group, dest_slot]), qkv_weight)
    near_qk = go(qk_weight, to_next)
    gain_next = go(after(qk_gain, packed), to_next)
    gain_far = go(after(qk_gain, packed), opposite_x)
    got = lax.all_to_all(packed, ("y", "core"), split_axis=0, concat_axis=0, tiled=True)
    placed = vmem_call(
        place_body, jax.ShapeDtypeStruct((tok, width + LANES), BF16), 3
    )(
        got.reshape(n_dp * capacity, width + LANES),
        image_ids.reshape(tok, 1),
        ln_gain[None, :],
    )
    placed = after(placed, near_qk, gain_next, gain_far)
    gathered = lax.all_gather(placed, ("core", "z"), axis=0, tiled=True)
    half = width // 2
    near_v = go(after(qkv_weight[2], placed), to_next)
    far = [go(after(near_qk[0], placed), on_by_side), go(after(near_qk[1], placed), on_by_mirror)]
    far.append(go(near_v[:half], on_by_side))
    far.append(go(near_v[half:], on_by_mirror))
    gain = jnp.concatenate(
        [jnp.where(first_core, qk_gain, gain_next), jnp.where(first_core, gain_next, gain_far)], axis=0
    )
    place = jnp.stack([c, lax.axis_index(("half", "side"))])

    rows = gathered.shape[0]
    step = width // 6
    steps = width // step
    whole = pl.BlockSpec((step, HD), lambda k: (k, 0))
    qkv = jax.ShapeDtypeStruct((rows // 2 + 16, 3 * HD), BF16)
    kept, *sent = pl.pallas_call(
        project_body,
        grid=(steps,),
        out_shape=(qkv,) * 5,
        in_specs=[
            pl.BlockSpec(memory_space=SMEM),
            pl.BlockSpec((rows, step), lambda k: (0, k)),
            pl.BlockSpec((rows, LANES), lambda k: (0, width // LANES)),
            pl.BlockSpec((3, step, HD), lambda k: (0, k, 0)),
            pl.BlockSpec((2, step, HD), lambda k: (0, k, 0)),
            whole,
            whole,
            whole,
            pl.BlockSpec((step, HD), lambda k: (jnp.minimum(k, steps // 2 - 1), 0)),
            pl.BlockSpec((step, HD), lambda k: (jnp.maximum(k - steps // 2, 0), 0)),
            pl.BlockSpec(memory_space=VMEM),
        ],
        out_specs=(pl.BlockSpec(memory_space=VMEM),) * 5,
        scratch_shapes=[VMEM((rows, 6 * HD), F32)],
        compiler_params=pltpu.CompilerParams(vmem_limit_bytes=48 << 20),
    )(place, gathered, gathered, qkv_weight, near_qk, near_v, *far, gain)
    swapped = [go(array, move) for array, move in zip(sent, EXCHANGE)]
    result = vmem_call(
        attend_body,
        jax.ShapeDtypeStruct((2 * rows // tok, tok, HD), BF16),
        6,
        scratch=[
            VMEM((2 * rows, 3 * HD), BF16), VMEM((8, 2 * rows), F32), VMEM((2 * rows, LANES), F32)
        ],
        smem_in=(0,),
    )(place, kept, *swapped)
    heads = lax.all_to_all(result, ("half", "side", "z"), split_axis=0, concat_axis=0, tiled=True)
    return jnp.transpose(heads, (1, 0, 2)).reshape(tok, NX * NZ * HD)


def solution(mesh):
    n_dp = mesh.devices.shape[0]
    split = Mesh(mesh.devices.reshape(n_dp // 2, 2, 2, NX // 2, NZ), AXES)
    dp, mp = ("y", "core"), ("half", "side", "z")
    return jax.shard_map(
        local,
        mesh=split,
        in_specs=(P(AXES, None), P(AXES), P(AXES), P(dp, mp), P(), P(None, None, mp), P(None, mp)),
        out_specs=P(AXES, None),
        check_vma=False,
    )
```

time: 189 us -> 168 us (0.89); the launches traced: 188 us -> 165 us
  waiting for transfers between devices: 115 us -> 67.2 us
  blocking collectives: 0 us -> 13.2 us
  starting transfers between devices: 32.8 us -> 41 us
  local copies, waits for them, and re-layouts: 6.32 us -> 10.9 us
  other arithmetic: 4.33 us -> 0.77 us
  Pallas kernels: 16.6 us -> 18.7 us
    all_gather x1, waiting for transfers between devices: 23.2 us -> 0.01 us  [local(): gathered = lax.all_gather(placed, ('core', 'z'), axis=0, tiled=True)]
    ppermute x4 -> x12, starting transfers between devices: 14 us -> 33.7 us  [send(): return lax.ppermute(array, AXES, pairs(n_dp, move))]
    all_to_all x0 -> x1, blocking collectives: none -> 13.2 us  [local(): lax.all_to_all(result, ('half', 'side', 'z'), split_axis=0, concat_axis=0...]
    all_to_all x1 -> x0, waiting for transfers between devices: 9.93 us -> none  [local(): lax.all_to_all(result, ('half', 'side', 'z'), split_axis=0, concat_axis=0...]
    all_to_all x1 -> x0, starting transfers between devices: 8.46 us -> none  [local(): lax.all_to_all(result, ('half', 'side', 'z'), split_axis=0, concat_axis=0...]
    ppermute x4 -> x12, waiting for transfers between devices: 59.5 us -> 51.5 us  [send(): return lax.ppermute(array, AXES, pairs(n_dp, move))]
    all_to_all x1, waiting for transfers between devices: 22.3 us -> 15.7 us  [local(): lax.all_to_all(packed, ('y', 'core'), split_axis=0, concat_axis=0, tiled=...]
    squeeze x0 -> x2, local copies, waits for them, and re-layouts: none -> 5.33 us  [the longest x1 3.82 us: local(): near_qk[1]]
  transfers between devices with their start and end apart: 7 -> 14, of which waited for: 6 -> 8; matrix products, arithmetic and copies ran while one was open for 2% -> 4% of each run, Pallas kernels for 0% -> 1%
where the time goes in v3:
time: 168 us; the launch traced here: 165 us
  waiting for transfers between devices  67.2 us (40%)
  starting transfers between devices  41 us (24%)
  Pallas kernels  18.7 us (11%)
  between operations  13.6 us (8%)
  blocking collectives  13.2 us (8%)
  local copies, waits for them, and re-layouts  10.9 us (6%)
    ppermute x12, waiting for transfers between devices, send(): return lax.ppermute(array, AXES, pairs(n_dp, move))  51.5 us
    ppermute x12, starting transfers between devices, send(): return lax.ppermute(array, AXES, pairs(n_dp, move))  33.7 us
    all_to_all x1, waiting for transfers between devices, local(): lax.all_to_all(packed, ('y', 'core'), split_axis=0, concat_axis=0, tiled=...  15.7 us
    all_to_all x1, blocking collectives, local(): lax.all_to_all(result, ('half', 'side', 'z'), split_axis=0, concat_axis=0...  13.2 us
    pallas_call x1, Pallas kernels, local(): pl.pallas_call(project_body, grid=(steps,), out_shape=(qkv,) * 5, in_spec...  11.4 us
    all_to_all x1, starting transfers between devices, local(): lax.all_to_all(packed, ('y', 'core'), split_axis=0, concat_axis=0, tiled=...  7.24 us
    squeeze x1, local copies, waits for them, and re-layouts, local(): near_qk[1]  3.82 us
  transfers between devices with their start and end apart: 14, of which 8 were waited for; matrix products, arithmetic and copies ran while one was open for 4% of the time, Pallas kernels for 1%

profile of v3, /device:TPU:1, one launch (start us, length us, event | category | flops | bytes accessed | tf_op | source)
XLA Modules:
  0.0 165.4 jit_solution(428927734907936692)
XLA Ops:
  6.5 0.7 pad_add_fusion.plan
  7.2 2.3 %copy-done = bf16[3,6144,128]{2,1,0:T(8,128)(2,1)S(1)} copy-done((bf16[3,6144,128]{2,1,0:T(8,128)(2,1)S(1)}, bf16[3,6144,128]{2,1,0:T(8,128)(2,1)}, u32[]{:S(2)}) %copy-start) | copy-done | bytes 4718616
  9.6 1.0 copy-done.1
  10.5 2.5 %shard_map.73 = (bf16[16,4,6272]{2,1,0:T(4,128)(2,1)}, bf16[2,6144,128]{2,1,0:T(8,128)(2,1)}) custom-call(bf16[32,6144]{1,0:T(8,128)(2,1)S(1)} %copy-done.1, s32[2,32]{1,0:T(2,128)S(1)} %pad_add_fusion.plan, bf16[3,6144,128]{2,1,0:T(8,128)(2,1)S(1)} %copy-done), custom_call_target="tpu_custom_call" | custom-call | tf_op jit(solution)/shard_map/pallas_call | solution.py:206
  13.1 0.0 copy-start.3
  13.1 0.0 copy-start.4
  13.1 5.2 %collective-permute-start = (bf16[2,6144,128]{2,1,0:T(8,128)(2,1)}, bf16[2,6144,128]{2,1,0:T(8,128)(2,1)}, u32[]{:S(2)}, u32[]{:S(2)}) collective-permute-start(bf16[2,6144,128]{2,1,0:T(8,128)(2,1)} %get-tuple-element.18), channel_id=1, source_target_pairs={{0,8},{1,9},{2,10},{3,11},{4,12},{5,13},{6,14},{7,15},{8,0},{9,1},... | collective-permute-start | bytes 9437192 | tf_op jit(solution)/shard_map/ppermute | solution.py:47
  18.3 0.0 copy-start.2
  18.4 7.2 %all-to-all-start = ((bf16[16,4,6272]{2,1,0:T(4,128)(2,1)}), bf16[16,4,6272]{2,1,0:T(4,128)(2,1)S(1)}, u32[]{:S(2)}, u32[]{:S(2)}) async-start(bf16[16,4,6272]{2,1,0:T(4,128)(2,1)} %get-tuple-element.17), calls=%async_computation | async-start | bytes 1605632 | tf_op jit(solution)/shard_map/all_to_all | solution.py:224
  25.6 0.0 all-gather.2.cloned.1.call-start
  25.6 0.0 copy-done.3
  25.7 3.3 %collective-permute-start.1 = (f32[2,128]{1,0:T(2,128)S(1)}, f32[2,128]{1,0:T(2,128)S(1)}, u32[]{:S(2)}, u32[]{:S(2)}) collective-permute-start(f32[2,128]{1,0:T(2,128)S(1)} %copy-done.3), channel_id=1, source_target_pairs={{0,8},{1,9},{2,10},{3,11},{4,12},{5,13},{6,14},{7,15},{8,0},{9,1},... | collective-permute-start | bytes 3080 | tf_op jit(solution)/shard_map/ppermute | solution.py:47
  29.0 3.8 %collective-permute-start.2 = (f32[2,128]{1,0:T(2,128)S(1)}, f32[2,128]{1,0:T(2,128)S(1)}, u32[]{:S(2)}, u32[]{:S(2)}) collective-permute-start(f32[2,128]{1,0:T(2,128)S(1)} %copy-done.3), channel_id=1, source_target_pairs={{0,16},{1,17},{2,18},{3,19},{4,20},{5,21},{6,22},{7,23},{8,24},{9,... | collective-permute-start | bytes 3080 | tf_op jit(solution)/shard_map/ppermute | solution.py:47
  32.8 0.0 copy-done.4
  32.8 0.1 copy.9.ids_col
  32.9 15.7 %all-to-all-done = bf16[16,4,6272]{2,1,0:T(4,128)(2,1)S(1)} async-done(((bf16[16,4,6272]{2,1,0:T(4,128)(2,1)}), bf16[16,4,6272]{2,1,0:T(4,128)(2,1)S(1)}, u32[]{:S(2)}, u32[]{:S(2)}) %all-to-all-start) | async-done | bytes 802848 | tf_op jit(solution)/shard_map/all_to_all | solution.py:224
  48.6 0.2 reshape.9.got
  48.8 1.5 shard_map.74
  50.2 3.1 %collective-permute-done.1 = f32[2,128]{1,0:T(2,128)S(1)} collective-permute-done((f32[2,128]{1,0:T(2,128)S(1)}, f32[2,128]{1,0:T(2,128)S(1)}, u32[]{:S(2)}, u32[]{:S(2)}) %collective-permute-start.1) | collective-permute-done | bytes 1056 | tf_op jit(solution)/shard_map/ppermute | solution.py:47
  53.3 0.0 collective-permute-done.2
  53.3 0.0 collective-permute-done.nqk
  53.3 0.0 all-gather.2.cloned.1.call-update
  53.3 1.5 slice_bitcast_fusion.2
  54.9 4.6 %collective-permute-start.3 = (bf16[6144,128]{1,0:T(8,128)(2,1)S(1)}, bf16[6144,128]{1,0:T(8,128)(2,1)S(1)}, u32[]{:S(2)}, u32[]{:S(2)}) collective-permute-start(bf16[6144,128]{1,0:T(8,128)(2,1)S(1)} %slice_bitcast_fusion.2), channel_id=1, source_target_pairs={{0,8},{1,9},{2,10},{3,11},{4,12},{5,13},{6,14},{7,15},{8,0},{9,1},... | collective-permute-start | bytes 4718600 | tf_op jit(solution)/shard_map/ppermute | solution.py:47
  59.4 3.8 %slice_bitcast_fusion = (bf16[6144,128]{1,0:T(8,128)(2,1)}, bf16[6144,128]{1,0:T(8,128)(2,1)}) fusion(bf16[2,6144,128]{2,1,0:T(8,128)(2,1)} %collective-permute-done.nqk), kind=kLoop, calls=%fused_computation | loop fusion | bytes 6291456 | tf_op jit(solution)/shard_map/squeeze | solution.py:236
  63.3 1.3 collective-permute-start.5
  64.6 1.9 %collective-permute-start.4 = (bf16[6144,128]{1,0:T(8,128)(2,1)}, bf16[6144,128]{1,0:T(8,128)(2,1)S(1)}, u32[]{:S(2)}, u32[]{:S(2)}) collective-permute-start(bf16[6144,128]{1,0:T(8,128)(2,1)} %get-tuple-element.22), channel_id=1, source_target_pairs={{32,40},{33,41},{34,42},{35,43},{36,44},{37,45},{38,46},{39,47},{4... | collective-permute-start | bytes 4718600 | tf_op jit(solution)/shard_map/ppermute | solution.py:47
  66.5 18.1 %collective-permute-done.3.nv = bf16[6144,128]{1,0:T(8,128)(2,1)S(1)} collective-permute-done((bf16[6144,128]{1,0:T(8,128)(2,1)S(1)}, bf16[6144,128]{1,0:T(8,128)(2,1)S(1)}, u32[]{:S(2)}, u32[]{:S(2)}) %collective-permute-start.3) | collective-permute-done | bytes 1572896 | tf_op jit(solution)/shard_map/ppermute | solution.py:47
  84.5 1.3 fusion
  85.8 1.9 %collective-permute-start.6 = (bf16[3072,128]{1,0:T(8,128)(2,1)}, bf16[3072,128]{1,0:T(8,128)(2,1)}, u32[]{:S(2)}, u32[]{:S(2)}) collective-permute-start(bf16[3072,128]{1,0:T(8,128)(2,1)} %get-tuple-element.32), channel_id=1, source_target_pairs={{32,40},{33,41},{34,42},{35,43},{36,44},{37,45},{38,46},{39,47},{4... | collective-permute-start | bytes 2359304 | tf_op jit(solution)/shard_map/ppermute | solution.py:47
  87.7 1.3 collective-permute-start.7
  89.0 0.1 pad_add_fusion.1.place
  89.1 5.4 %collective-permute-done.5.fk = bf16[6144,128]{1,0:T(8,128)(2,1)} collective-permute-done((bf16[6144,128]{1,0:T(8,128)(2,1)}, bf16[6144,128]{1,0:T(8,128)(2,1)}, u32[]{:S(2)}, u32[]{:S(2)}) %collective-permute-start.5) | collective-permute-done | bytes 1572896 | tf_op jit(solution)/shard_map/ppermute | solution.py:47
  94.5 5.4 %collective-permute-done.4.fq = bf16[6144,128]{1,0:T(8,128)(2,1)S(1)} collective-permute-done((bf16[6144,128]{1,0:T(8,128)(2,1)}, bf16[6144,128]{1,0:T(8,128)(2,1)S(1)}, u32[]{:S(2)}, u32[]{:S(2)}) %collective-permute-start.4) | collective-permute-done | bytes 1572896 | tf_op jit(solution)/shard_map/ppermute | solution.py:47
  99.9 8.1 %collective-permute-done.6.fv0 = bf16[3072,128]{1,0:T(8,128)(2,1)} collective-permute-done((bf16[3072,128]{1,0:T(8,128)(2,1)}, bf16[3072,128]{1,0:T(8,128)(2,1)}, u32[]{:S(2)}, u32[]{:S(2)}) %collective-permute-start.6) | collective-permute-done | bytes 786464 | tf_op jit(solution)/shard_map/ppermute | solution.py:47
  108.0 7.4 %collective-permute-done.7.fv1 = bf16[3072,128]{1,0:T(8,128)(2,1)} collective-permute-done((bf16[3072,128]{1,0:T(8,128)(2,1)}, bf16[3072,128]{1,0:T(8,128)(2,1)}, u32[]{:S(2)}, u32[]{:S(2)}) %collective-permute-start.7) | collective-permute-done | bytes 786464 | tf_op jit(solution)/shard_map/ppermute | solution.py:47
  115.5 11.4 %shard_map.75 = (bf16[272,384]{1,0:T(8,128)(2,1)S(1)}, bf16[272,384]{1,0:T(8,128)(2,1)S(1)}, bf16[272,384]{1,0:T(8,128)(2,1)S(1)}, bf16[272,384]{1,0:T(8,128)(2,1)S(1)}, bf16[272,384]{1,0:T(8,128)(2,1)S(1)}) custom-call(s32[2]{0:T(128)S(1)} %pad_add_fusion.1.place, bf16[512,6272]{1,0:T(8,128)(2,1)} %all-gather.2.cloned.1.call-done.tokens.ids, ...), custom_call_target="tpu_custom_call" | custom-call | tf_op jit(solution)/shard_map/pallas_call | solution.py:249
  126.9 1.9 %collective-permute-start.10 = (bf16[272,384]{1,0:T(8,128)(2,1)S(1)}, bf16[272,384]{1,0:T(8,128)(2,1)S(1)}, u32[]{:S(2)}, u32[]{:S(2)}) collective-permute-start(bf16[272,384]{1,0:T(8,128)(2,1)S(1)} %get-tuple-element.27), channel_id=1, source_target_pairs={{0,40},{1,41},{2,42},{3,43},{4,44},{5,45},{6,46},{7,47},{8,32},{9,... | collective-permute-start | bytes 626696 | tf_op jit(solution)/shard_map/ppermute | solution.py:47
  128.8 1.9 %collective-permute-start.11 = (bf16[272,384]{1,0:T(8,128)(2,1)S(1)}, bf16[272,384]{1,0:T(8,128)(2,1)S(1)}, u32[]{:S(2)}, u32[]{:S(2)}) collective-permute-start(bf16[272,384]{1,0:T(8,128)(2,1)S(1)} %get-tuple-element.28), channel_id=1, source_target_pairs={{32,48},{33,49},{34,50},{35,51},{36,52},{37,53},{38,54},{39,55},{4... | collective-permute-start | bytes 626696 | tf_op jit(solution)/shard_map/ppermute | solution.py:47
  130.7 1.9 %collective-permute-start.8 = (bf16[272,384]{1,0:T(8,128)(2,1)S(1)}, bf16[272,384]{1,0:T(8,128)(2,1)S(1)}, u32[]{:S(2)}, u32[]{:S(2)}) collective-permute-start(bf16[272,384]{1,0:T(8,128)(2,1)S(1)} %get-tuple-element.25), channel_id=1, source_target_pairs={{0,32},{1,33},{2,34},{3,35},{4,36},{5,37},{6,38},{7,39},{8,40},{9,... | collective-permute-start | bytes 626696 | tf_op jit(solution)/shard_map/ppermute | solution.py:47
  132.7 4.7 %collective-permute-start.9 = (bf16[272,384]{1,0:T(8,128)(2,1)S(1)}, bf16[272,384]{1,0:T(8,128)(2,1)S(1)}, u32[]{:S(2)}, u32[]{:S(2)}) collective-permute-start(bf16[272,384]{1,0:T(8,128)(2,1)S(1)} %get-tuple-element.26), channel_id=1, source_target_pairs={{0,8},{1,9},{2,10},{3,11},{4,12},{5,13},{6,14},{7,15},{8,0},{9,1},... | collective-permute-start | bytes 626696 | tf_op jit(solution)/shard_map/ppermute | solution.py:47
  137.3 0.0 collective-permute-done.10.got2
  137.3 0.0 collective-permute-done.11.got3
  137.4 0.0 collective-permute-done.8.got0
  137.4 4.0 %collective-permute-done.9.got1 = bf16[272,384]{1,0:T(8,128)(2,1)S(1)} collective-permute-done((bf16[272,384]{1,0:T(8,128)(2,1)S(1)}, bf16[272,384]{1,0:T(8,128)(2,1)S(1)}, u32[]{:S(2)}, u32[]{:S(2)}) %collective-permute-start.9) | collective-permute-done | bytes 208928 | tf_op jit(solution)/shard_map/ppermute | solution.py:47
  141.3 3.3 %shard_map.76 = bf16[32,32,128]{2,1,0:T(8,128)(2,1)S(1)} custom-call(s32[2]{0:T(128)S(1)} %pad_add_fusion.1.place, bf16[272,384]{1,0:T(8,128)(2,1)S(1)} %get-tuple-element.24.kept, bf16[272,384]{1,0:T(8,128)(2,1)S(1)} %collective-permute-done.8.got0, bf16[272,384]{1,0:T(8,128)(2,1)S(1)} %collective-permute-done.9.got1, ...), custom_call_target="tpu_custom_call" | custom-call | tf_op jit(solution)/shard_map/pallas_call | solution.py:271
  144.6 13.2 %all_to_all.10 = bf16[32,32,128]{2,1,0:T(8,128)(2,1)S(1)} all-to-all(bf16[32,32,128]{2,1,0:T(8,128)(2,1)S(1)} %shard_map.76), channel_id=1, replica_groups=mesh['y'=8,'core'=2,'half'=2,'side'=2,'z'=8] {'half','side','z'}, dimensions={0} | all-to-all | bytes 524288 | tf_op jit(solution)/shard_map/all_to_all | solution.py:280
  157.8 0.7 copy_bitcast_fusion
  (6 shorter events, 0.0 us)
Async XLA Ops:
  7.2 2.3 %copy-start = (bf16[3,6144,128]{2,1,0:T(8,128)(2,1)S(1)}, bf16[3,6144,128]{2,1,0:T(8,128)(2,1)}, u32[]{:S(2)}) copy-start(bf16[3,6144,128]{2,1,0:T(8,128)(2,1)} %own.1) | copy-start | bytes 14155780
  9.6 1.0 copy-start.1
  13.1 12.5 %copy-start.3 = (f32[2,128]{1,0:T(2,128)S(1)}, f32[2,128]{1,0:T(2,128)}, u32[]{:S(2)}) copy-start(f32[2,128]{1,0:T(2,128)} %param.13) | copy-start | bytes 3076
  13.1 19.7 %copy-start.4 = (s32[1,32]{1,0:T(1,128)S(1)}, s32[1,32]{1,0:T(1,128)}, u32[]{:S(2)}) copy-start(s32[1,32]{1,0:T(1,128)} %param.10) | copy-start | bytes 388
  13.1 40.2 %collective-permute-start = (bf16[2,6144,128]{2,1,0:T(8,128)(2,1)}, bf16[2,6144,128]{2,1,0:T(8,128)(2,1)}, u32[]{:S(2)}, u32[]{:S(2)}) collective-permute-start(bf16[2,6144,128]{2,1,0:T(8,128)(2,1)} %get-tuple-element.18), channel_id=1, source_target_pairs={{0,8},{1,9},{2,10},{3,11},{4,12},{5,13},{6,14},{7,15},{8,0},{9,1},... | collective-permute-start | bytes 9437192 | tf_op jit(solution)/shard_map/ppermute | solution.py:47
  18.3 30.4 %copy-start.2 = (f32[6144]{0:T(1024)S(1)}, f32[6144]{0:T(1024)}, u32[]{:S(2)}) copy-start(f32[6144]{0:T(1024)} %param.11) | copy-start | bytes 73732
  18.4 30.2 %all-to-all-start = ((bf16[16,4,6272]{2,1,0:T(4,128)(2,1)}), bf16[16,4,6272]{2,1,0:T(4,128)(2,1)S(1)}, u32[]{:S(2)}, u32[]{:S(2)}) async-start(bf16[16,4,6272]{2,1,0:T(4,128)(2,1)} %get-tuple-element.17), calls=%async_computation | async-start | bytes 1605632 | tf_op jit(solution)/shard_map/all_to_all | solution.py:224
  25.6 89.9 %all-gather.2.cloned.1.call-start = ((), (), s32[]{:S(2)}) async-start(), calls=%async_computation.2 | async-start | bytes 6823936 | tf_op jit(solution)/shard_map/all_gather | solution.py:233
  25.7 27.7 %collective-permute-start.1 = (f32[2,128]{1,0:T(2,128)S(1)}, f32[2,128]{1,0:T(2,128)S(1)}, u32[]{:S(2)}, u32[]{:S(2)}) collective-permute-start(f32[2,128]{1,0:T(2,128)S(1)} %copy-done.3), channel_id=1, source_target_pairs={{0,8},{1,9},{2,10},{3,11},{4,12},{5,13},{6,14},{7,15},{8,0},{9,1},... | collective-permute-start | bytes 3080 | tf_op jit(solution)/shard_map/ppermute | solution.py:47
  29.0 24.4 %collective-permute-start.2 = (f32[2,128]{1,0:T(2,128)S(1)}, f32[2,128]{1,0:T(2,128)S(1)}, u32[]{:S(2)}, u32[]{:S(2)}) collective-permute-start(f32[2,128]{1,0:T(2,128)S(1)} %copy-done.3), channel_id=1, source_target_pairs={{0,16},{1,17},{2,18},{3,19},{4,20},{5,21},{6,22},{7,23},{8,24},{9,... | collective-permute-start | bytes 3080 | tf_op jit(solution)/shard_map/ppermute | solution.py:47
  54.9 29.7 %collective-permute-start.3 = (bf16[6144,128]{1,0:T(8,128)(2,1)S(1)}, bf16[6144,128]{1,0:T(8,128)(2,1)S(1)}, u32[]{:S(2)}, u32[]{:S(2)}) collective-permute-start(bf16[6144,128]{1,0:T(8,128)(2,1)S(1)} %slice_bitcast_fusion.2), channel_id=1, source_target_pairs={{0,8},{1,9},{2,10},{3,11},{4,12},{5,13},{6,14},{7,15},{8,0},{9,1},... | collective-permute-start | bytes 4718600 | tf_op jit(solution)/shard_map/ppermute | solution.py:47
  63.3 31.2 %collective-permute-start.5 = (bf16[6144,128]{1,0:T(8,128)(2,1)}, bf16[6144,128]{1,0:T(8,128)(2,1)}, u32[]{:S(2)}, u32[]{:S(2)}) collective-permute-start(bf16[6144,128]{1,0:T(8,128)(2,1)} %get-tuple-element.23), channel_id=1, source_target_pairs={{0,56},{1,57},{2,58},{3,59},{4,60},{5,61},{6,62},{7,63},{8,48},{9,... | collective-permute-start | bytes 4718600 | tf_op jit(solution)/shard_map/ppermute | solution.py:47
  64.6 35.4 %collective-permute-start.4 = (bf16[6144,128]{1,0:T(8,128)(2,1)}, bf16[6144,128]{1,0:T(8,128)(2,1)S(1)}, u32[]{:S(2)}, u32[]{:S(2)}) collective-permute-start(bf16[6144,128]{1,0:T(8,128)(2,1)} %get-tuple-element.22), channel_id=1, source_target_pairs={{32,40},{33,41},{34,42},{35,43},{36,44},{37,45},{38,46},{39,47},{4... | collective-permute-start | bytes 4718600 | tf_op jit(solution)/shard_map/ppermute | solution.py:47
  85.8 22.3 %collective-permute-start.6 = (bf16[3072,128]{1,0:T(8,128)(2,1)}, bf16[3072,128]{1,0:T(8,128)(2,1)}, u32[]{:S(2)}, u32[]{:S(2)}) collective-permute-start(bf16[3072,128]{1,0:T(8,128)(2,1)} %get-tuple-element.32), channel_id=1, source_target_pairs={{32,40},{33,41},{34,42},{35,43},{36,44},{37,45},{38,46},{39,47},{4... | collective-permute-start | bytes 2359304 | tf_op jit(solution)/shard_map/ppermute | solution.py:47
  87.7 27.8 %collective-permute-start.7 = (bf16[3072,128]{1,0:T(8,128)(2,1)}, bf16[3072,128]{1,0:T(8,128)(2,1)}, u32[]{:S(2)}, u32[]{:S(2)}) collective-permute-start(bf16[3072,128]{1,0:T(8,128)(2,1)} %get-tuple-element.31), channel_id=1, source_target_pairs={{0,56},{1,57},{2,58},{3,59},{4,60},{5,61},{6,62},{7,63},{8,48},{9,... | collective-permute-start | bytes 2359304 | tf_op jit(solution)/shard_map/ppermute | solution.py:47
  126.9 10.5 %collective-permute-start.10 = (bf16[272,384]{1,0:T(8,128)(2,1)S(1)}, bf16[272,384]{1,0:T(8,128)(2,1)S(1)}, u32[]{:S(2)}, u32[]{:S(2)}) collective-permute-start(bf16[272,384]{1,0:T(8,128)(2,1)S(1)} %get-tuple-element.27), channel_id=1, source_target_pairs={{0,40},{1,41},{2,42},{3,43},{4,44},{5,45},{6,46},{7,47},{8,32},{9,... | collective-permute-start | bytes 626696 | tf_op jit(solution)/shard_map/ppermute | solution.py:47
  128.8 8.5 %collective-permute-start.11 = (bf16[272,384]{1,0:T(8,128)(2,1)S(1)}, bf16[272,384]{1,0:T(8,128)(2,1)S(1)}, u32[]{:S(2)}, u32[]{:S(2)}) collective-permute-start(bf16[272,384]{1,0:T(8,128)(2,1)S(1)} %get-tuple-element.28), channel_id=1, source_target_pairs={{32,48},{33,49},{34,50},{35,51},{36,52},{37,53},{38,54},{39,55},{4... | collective-permute-start | bytes 626696 | tf_op jit(solution)/shard_map/ppermute | solution.py:47
  130.7 6.6 %collective-permute-start.8 = (bf16[272,384]{1,0:T(8,128)(2,1)S(1)}, bf16[272,384]{1,0:T(8,128)(2,1)S(1)}, u32[]{:S(2)}, u32[]{:S(2)}) collective-permute-start(bf16[272,384]{1,0:T(8,128)(2,1)S(1)} %get-tuple-element.25), channel_id=1, source_target_pairs={{0,32},{1,33},{2,34},{3,35},{4,36},{5,37},{6,38},{7,39},{8,40},{9,... | collective-permute-start | bytes 626696 | tf_op jit(solution)/shard_map/ppermute | solution.py:47
  132.7 8.7 %collective-permute-start.9 = (bf16[272,384]{1,0:T(8,128)(2,1)S(1)}, bf16[272,384]{1,0:T(8,128)(2,1)S(1)}, u32[]{:S(2)}, u32[]{:S(2)}) collective-permute-start(bf16[272,384]{1,0:T(8,128)(2,1)S(1)} %get-tuple-element.26), channel_id=1, source_target_pairs={{0,8},{1,9},{2,10},{3,11},{4,12},{5,13},{6,14},{7,15},{8,0},{9,1},... | collective-permute-start | bytes 626696 | tf_op jit(solution)/shard_map/ppermute | solution.py:47
Sparse Core Ops, SparseCore 0:
  53.5 55.2 all-gather.1

commit v4 on v3

--- a/solution.py
+++ b/solution.py
@@ -82,9 +82,24 @@
     return (centered * lax.rsqrt(spread + 1e-06) * gain).astype(BF16)
 
 
-def pack_body(rows, plan, weight, out, first_two, sem):
-    copy = pltpu.make_async_copy(weight.at[0:2], first_two, sem)
-    copy.start()
+def pack_body(rows, plan, gain, weight, out, q_out, k_out, v_out, parts, sem):
+    depth = weight.shape[1]
+    high = gain[...].astype(BF16)
+    rest = gain[...] - high.astype(F32)
+    middle = rest.astype(BF16)
+    low = (rest - middle.astype(F32)).astype(BF16)
+    pad = jnp.zeros((10, HD), F32)
+    parts[...] = jnp.concatenate(
+        [high.astype(F32), middle.astype(F32), low.astype(F32), pad], axis=0
+    ).astype(BF16)
+    copies = [
+        pltpu.make_async_copy(weight.at[0], q_out, sem.at[0]),
+        pltpu.make_async_copy(weight.at[1], k_out.at[pl.ds(0, depth), :], sem.at[1]),
+        pltpu.make_async_copy(parts, k_out.at[pl.ds(depth, 16), :], sem.at[2]),
+        pltpu.make_async_copy(weight.at[2], v_out, sem.at[3]),
+    ]
+    for copy in copies:
+        copy.start()
     tok, width = rows.shape
     groups, capacity, _ = out.shape
     slots = groups * capacity
@@ -103,7 +118,8 @@
     for g in range(groups):
         out[g, :, :width] = sent[g * capacity : (g + 1) * capacity, :]
         out[g, :, width:] = slot[g * capacity : (g + 1) * capacity, :]
-    copy.wait()
+    for copy in copies:
+        copy.wait()
 
 
 def place_body(got, ids_col, gain, out):
@@ -119,13 +135,13 @@
     out[:, width:] = jnp.broadcast_to(ids_col[...].astype(F32), (tok, LANES)).astype(BF16)
 
 
-def project_body(place, tokens, ids, own, nqk, nv, fq, fk, fv0, fv1, gain, *refs):
-    outs, total = refs[:5], refs[5]
+def project_body(place, tokens, ids, own, nq, nk, nv, fq, fk, fv0, fv1, own_gain, *refs):
+    parts, outs, total = refs[:2], refs[2:7], refs[7]
     k = pl.program_id(0)
     steps = pl.num_programs(0)
     rows = tokens.shape[0] // 2
     first_core = place[0] == 0
-    near = [nqk[0], nqk[1], nv[...]]
+    near = [nq[...], nk[...], nv[...]]
     far = [fq[...], fk[...], jnp.where(k < steps // 2, fv0[...], fv1[...])]
     six = [jnp.where(first_core, own[j], near[j]) for j in range(3)]
     six += [jnp.where(first_core, near[j], far[j]) for j in range(3)]
@@ -140,15 +156,21 @@
         total[...] += part
 
     def emit(dsts):
+        near_gain, far_gain = [
+            p[0:2, :].astype(F32) + p[2:4, :].astype(F32) + p[4:6, :].astype(F32) for p in parts
+        ]
+        both = (
+            jnp.where(first_core, own_gain[...], near_gain),
+            jnp.where(first_core, near_gain, far_gain),
+        )
+        gains = [rows_of[j : j + 1, :] for rows_of in both for j in range(2)]
         turned = jnp.transpose(ids[...].astype(F32))[0:16, :].astype(BF16)
         for n, dst in enumerate(dsts):
             head, group = n // 2, n % 2
             at = slice(group * rows, (group + 1) * rows)
             for j in range(2):
                 cols = total[at, (3 * head + j) * HD : (3 * head + j + 1) * HD]
-                dst[:rows, j * HD : (j + 1) * HD] = norm_rows(
-                    cols, gain[2 * head + j : 2 * head + j + 1, :]
-                )
+                dst[:rows, j * HD : (j + 1) * HD] = norm_rows(cols, gains[2 * head + j])
             dst[:rows, 2 * HD :] = total[at, (3 * head + 2) * HD : (3 * head + 3) * HD].astype(BF16)
             dst[rows:, :rows] = turned[:, at]
             dst[rows:, rows:] = jnp.zeros((16, 3 * HD - rows), BF16)
@@ -203,24 +225,26 @@
     first_core = c == 0
     go = functools.partial(lambda array, move: send(array, n_dp, move))
 
-    packed, qk_weight = pl.pallas_call(
+    packed, q_weight, k_weight, v_weight = pl.pallas_call(
         pack_body,
         out_shape=(
             jax.ShapeDtypeStruct((n_dp, capacity, width + LANES), BF16),
-            jax.ShapeDtypeStruct((2, width, HD), BF16),
+            jax.ShapeDtypeStruct((width, HD), BF16),
+            jax.ShapeDtypeStruct((width + 16, HD), BF16),
+            jax.ShapeDtypeStruct((width, HD), BF16),
         ),
-        in_specs=[
-            pl.BlockSpec(memory_space=VMEM),
+        in_specs=[pl.BlockSpec(memory_space=VMEM)] * 3 + [pl.BlockSpec(memory_space=pltpu.HBM)],
+        out_specs=(
             pl.BlockSpec(memory_space=VMEM),
             pl.BlockSpec(memory_space=pltpu.HBM),
-        ],
-        out_specs=(pl.BlockSpec(memory_space=VMEM), pl.BlockSpec(memory_space=pltpu.HBM)),
-        scratch_shapes=[pltpu.SemaphoreType.DMA],
+            pl.BlockSpec(memory_space=pltpu.HBM),
+            pl.BlockSpec(memory_space=pltpu.HBM),
+        ),
+        scratch_shapes=[VMEM((16, HD), BF16), pltpu.SemaphoreType.DMA((4,))],
         compiler_params=pltpu.CompilerParams(vmem_limit_bytes=32 << 20),
-    )(packed_rows, jnp.stack([dest_group, dest_slot]), qkv_weight)
-    near_qk = go(qk_weight, to_next)
-    gain_next = go(after(qk_gain, packed), to_next)
-    gain_far = go(after(qk_gain, packed), opposite_x)
+    )(packed_rows, jnp.stack([dest_group, dest_slot]), qk_gain, qkv_weight)
+    near_q = go(q_weight, to_next)
+    near_k = go(k_weight, to_next)
     got = lax.all_to_all(packed, ("y", "core"), split_axis=0, concat_axis=0, tiled=True)
     placed = vmem_call(
         place_body, jax.ShapeDtypeStruct((tok, width + LANES), BF16), 3
@@ -229,44 +253,56 @@
         image_ids.reshape(tok, 1),
         ln_gain[None, :],
     )
-    placed = after(placed, near_qk, gain_next, gain_far)
+    placed = after(after(placed, near_q), near_k)
     gathered = lax.all_gather(placed, ("core", "z"), axis=0, tiled=True)
     half = width // 2
-    near_v = go(after(qkv_weight[2], placed), to_next)
-    far = [go(after(near_qk[0], placed), on_by_side), go(after(near_qk[1], placed), on_by_mirror)]
+    near_v = go(after(v_weight, placed), to_next)
+    far = [go(after(near_q, placed), on_by_side), go(after(near_k, placed), on_by_mirror)]
     far.append(go(near_v[:half], on_by_side))
     far.append(go(near_v[half:], on_by_mirror))
-    gain = jnp.concatenate(
-        [jnp.where(first_core, qk_gain, gain_next), jnp.where(first_core, gain_next, gain_far)], axis=0
-    )
     place = jnp.stack([c, lax.axis_index(("half", "side"))])
 
     rows = gathered.shape[0]
     step = width // 6
     steps = width // step
-    whole = pl.BlockSpec((step, HD), lambda k: (k, 0))
     qkv = jax.ShapeDtypeStruct((rows // 2 + 16, 3 * HD), BF16)
+
+    def on(core, k, place, low=0, high=steps):
+        return jnp.where(place[0] == core, jnp.clip(k - low, 0, high - low - 1), 0)
+
+    def block_of(core, low=0, high=steps):
+        return pl.BlockSpec((step, HD), lambda k, place: (on(core, k, place, low, high), 0))
+
+    near_block = pl.BlockSpec((step, HD), lambda k, place: (k, 0))
+    tail = pl.BlockSpec((16, HD), lambda k, place: (width // 16, 0))
     kept, *sent = pl.pallas_call(
         project_body,
-        grid=(steps,),
         out_shape=(qkv,) * 5,
-        in_specs=[
-            pl.BlockSpec(memory_space=SMEM),
-            pl.BlockSpec((rows, step), lambda k: (0, k)),
-            pl.BlockSpec((rows, LANES), lambda k: (0, width // LANES)),
-            pl.BlockSpec((3, step, HD), lambda k: (0, k, 0)),
-            pl.BlockSpec((2, step, HD), lambda k: (0, k, 0)),
-            whole,
-            whole,
-            whole,
-            pl.BlockSpec((step, HD), lambda k: (jnp.minimum(k, steps // 2 - 1), 0)),
-            pl.BlockSpec((step, HD), lambda k: (jnp.maximum(k - steps // 2, 0), 0)),
-            pl.BlockSpec(memory_space=VMEM),
-        ],
-        out_specs=(pl.BlockSpec(memory_space=VMEM),) * 5,
-        scratch_shapes=[VMEM((rows, 6 * HD), F32)],
+        grid_spec=pltpu.PrefetchScalarGridSpec(
+            num_scalar_prefetch=1,
+            grid=(steps,),
+            in_specs=[
+                pl.BlockSpec((rows, step), lambda k, place: (0, k)),
+                pl.BlockSpec((rows, LANES), lambda k, place: (0, width // LANES)),
+                pl.BlockSpec((3, step, HD), lambda k, place: (0, on(0, k, place), 0)),
+                near_block,
+                near_block,
+                near_block,
+                block_of(1),
+                block_of(1),
+                block_of(1, 0, steps // 2),
+                block_of(1, steps // 2),
+                pl.BlockSpec(memory_space=VMEM),
+                tail,
+                tail,
+            ],
+            out_specs=(pl.BlockSpec(memory_space=VMEM),) * 5,
+            scratch_shapes=[VMEM((rows, 6 * HD), F32)],
+        ),
         compiler_params=pltpu.CompilerParams(vmem_limit_bytes=48 << 20),
-    )(place, gathered, gathered, qkv_weight, near_qk, near_v, *far, gain)
+    )(
+        place, gathered, gathered, qkv_weight, near_q, near_k, near_v, *far, qk_gain, near_k, far[1]
+    )
     swapped = [go(array, move) for array, move in zip(sent, EXCHANGE)]
     result = vmem_call(
         attend_body,

time: 168 us -> 172 us (1.024); the launches traced: 165 us -> 171 us
  waiting for transfers between devices: 67.2 us -> 72.3 us
  blocking collectives: 13.2 us -> 17.4 us
  local copies, waits for them, and re-layouts: 10.9 us -> 7.45 us
    all_to_all x1, waiting for transfers between devices: 15.7 us -> 22.9 us  [local(): lax.all_to_all(packed, ('y', 'core'), split_axis=0, concat_axis=0, tiled=...]
    squeeze x2 -> x0, local copies, waits for them, and re-layouts: 5.33 us -> none  [the longest x1 3.82 us: local(): near_qk[1]]
    ppermute x12 -> x11, waiting for transfers between devices: 51.5 us -> 46.7 us  [send(): return lax.ppermute(array, AXES, pairs(n_dp, move))]
    all_to_all x1, blocking collectives: 13.2 us -> 17.4 us  [local(): lax.all_to_all(result, ('half', 'side', 'z'), split_axis=0, concat_axis=0...]
    all_gather x1, waiting for transfers between devices: 0.01 us -> 2.71 us  [local(): gathered = lax.all_gather(placed, ('core', 'z'), axis=0, tiled=True)]
    unnamed x10 -> x14, local copies, waits for them, and re-layouts: 3.35 us -> 5.22 us
    all_to_all x1, starting transfers between devices: 7.24 us -> 9 us  [local(): lax.all_to_all(packed, ('y', 'core'), split_axis=0, concat_axis=0, tiled=...]
    ppermute x12 -> x11, starting transfers between devices: 33.7 us -> 32 us  [send(): return lax.ppermute(array, AXES, pairs(n_dp, move))]
  transfers between devices with their start and end apart: 14 -> 13, of which waited for: 8 -> 8; matrix products, arithmetic and copies ran while one was open for 4% -> 1% of each run, Pallas kernels for 1% -> 1%
where the time goes in v4:
time: 172 us; the launch traced here: 171 us
  waiting for transfers between devices  72.3 us (42%)
  starting transfers between devices  41 us (24%)
  Pallas kernels  18.8 us (11%)
  blocking collectives  17.4 us (10%)
  between operations  13.6 us (8%)
  local copies, waits for them, and re-layouts  7.45 us (4%)
    ppermute x11, waiting for transfers between devices, send(): return lax.ppermute(array, AXES, pairs(n_dp, move))  46.7 us
    ppermute x11, starting transfers between devices, send(): return lax.ppermute(array, AXES, pairs(n_dp, move))  32 us
    all_to_all x1, waiting for transfers between devices, local(): lax.all_to_all(packed, ('y', 'core'), split_axis=0, concat_axis=0, tiled=...  22.9 us
    all_to_all x1, blocking collectives, local(): lax.all_to_all(result, ('half', 'side', 'z'), split_axis=0, concat_axis=0...  17.4 us
    pallas_call x1, Pallas kernels, local(): pl.pallas_call(project_body, out_shape=(qkv,) * 5, grid_spec=pltpu.Prefet...  11.5 us
    all_to_all x1, starting transfers between devices, local(): lax.all_to_all(packed, ('y', 'core'), split_axis=0, concat_axis=0, tiled=...  9 us
    unnamed x14, local copies, waits for them, and re-layouts  5.22 us
  transfers between devices with their start and end apart: 13, of which 8 were waited for; matrix products, arithmetic and copies ran while one was open for 1% of the time, Pallas kernels for 1%

profile of v4, /device:TPU:1, one launch (start us, length us, event | category | flops | bytes accessed | tf_op | source)
XLA Modules:
  0.0 171.3 jit_solution(9710459522382232515)
XLA Ops:
  6.5 0.7 pad_add_fusion.plan
  7.2 2.3 %copy-done = bf16[3,6144,128]{2,1,0:T(8,128)(2,1)S(1)} copy-done((bf16[3,6144,128]{2,1,0:T(8,128)(2,1)S(1)}, bf16[3,6144,128]{2,1,0:T(8,128)(2,1)}, u32[]{:S(2)}) %copy-start) | copy-done | bytes 4718616
  9.6 1.0 copy-done.1
  10.6 0.7 copy-done.3
  11.2 2.6 %shard_map.73 = (bf16[16,4,6272]{2,1,0:T(4,128)(2,1)}, bf16[6144,128]{1,0:T(8,128)(2,1)}, bf16[6160,128]{1,0:T(8,128)(2,1)}, bf16[6144,128]{1,0:T(8,128)(2,1)S(1)}) custom-call(bf16[32,6144]{1,0:T(8,128)(2,1)S(1)} %copy-done.1, s32[2,32]{1,0:T(2,128)S(1)} %pad_add_fusion.plan, f32[2,128]{1,0:T(2,128)S(1)} %copy-done.3, bf16[3,6144,128]{2,1,0:T(8,128)(2,1)S(1)} %copy-done), custom_call_target="tpu_custom_call" | custom-call | tf_op jit(solution)/shard_map/pallas_call | solution.py:228
  13.8 0.0 copy-start.5
  13.8 1.2 copy-done.5
  15.0 5.3 %collective-permute-start.1 = (bf16[6160,128]{1,0:T(8,128)(2,1)}, bf16[6160,128]{1,0:T(8,128)(2,1)}, u32[]{:S(2)}, u32[]{:S(2)}) collective-permute-start(bf16[6160,128]{1,0:T(8,128)(2,1)} %get-tuple-element.22), channel_id=1, source_target_pairs={{0,8},{1,9},{2,10},{3,11},{4,12},{5,13},{6,14},{7,15},{8,0},{9,1},... | collective-permute-start | bytes 4730888 | tf_op jit(solution)/shard_map/ppermute | solution.py:47
  20.4 1.9 %collective-permute-start = (bf16[6144,128]{1,0:T(8,128)(2,1)}, bf16[6144,128]{1,0:T(8,128)(2,1)S(1)}, u32[]{:S(2)}, u32[]{:S(2)}) collective-permute-start(bf16[6144,128]{1,0:T(8,128)(2,1)} %get-tuple-element.20), channel_id=1, source_target_pairs={{0,8},{1,9},{2,10},{3,11},{4,12},{5,13},{6,14},{7,15},{8,0},{9,1},... | collective-permute-start | bytes 4718600 | tf_op jit(solution)/shard_map/ppermute | solution.py:47
  22.3 0.0 copy-start.2
  22.3 9.0 %all-to-all-start = ((bf16[16,4,6272]{2,1,0:T(4,128)(2,1)}), bf16[16,4,6272]{2,1,0:T(4,128)(2,1)S(1)}, u32[]{:S(2)}, u32[]{:S(2)}) async-start(bf16[16,4,6272]{2,1,0:T(4,128)(2,1)} %get-tuple-element.19), calls=%async_computation | async-start | bytes 1605632 | tf_op jit(solution)/shard_map/all_to_all | solution.py:248
  31.3 0.0 all-gather.2.cloned.1.call-start
  31.3 0.0 copy-done.6
  31.3 0.1 copy.9.ids_col
  31.4 22.9 %all-to-all-done = bf16[16,4,6272]{2,1,0:T(4,128)(2,1)S(1)} async-done(((bf16[16,4,6272]{2,1,0:T(4,128)(2,1)}), bf16[16,4,6272]{2,1,0:T(4,128)(2,1)S(1)}, u32[]{:S(2)}, u32[]{:S(2)}) %all-to-all-start) | async-done | bytes 802848 | tf_op jit(solution)/shard_map/all_to_all | solution.py:248
  54.3 0.2 reshape.9.got
  54.5 0.0 copy-done.2
  54.5 1.4 shard_map.74
  56.0 0.0 collective-permute-done.nq
  56.0 0.0 collective-permute-done.1.nk.refs_0_
  56.0 0.0 all-gather.2.cloned.1.call-update
  56.0 0.0 copy-start.4
  56.0 3.8 %collective-permute-start.2 = (bf16[6144,128]{1,0:T(8,128)(2,1)}, bf16[6144,128]{1,0:T(8,128)(2,1)S(1)}, u32[]{:S(2)}, u32[]{:S(2)}) collective-permute-start(bf16[6144,128]{1,0:T(8,128)(2,1)} %copy-done.5), channel_id=1, source_target_pairs={{0,8},{1,9},{2,10},{3,11},{4,12},{5,13},{6,14},{7,15},{8,0},{9,1},... | collective-permute-start | bytes 4718600 | tf_op jit(solution)/shard_map/ppermute | solution.py:47
  59.9 1.3 collective-permute-start.4
  61.2 1.9 %collective-permute-start.3 = (bf16[6144,128]{1,0:T(8,128)(2,1)S(1)}, bf16[6144,128]{1,0:T(8,128)(2,1)}, u32[]{:S(2)}, u32[]{:S(2)}) collective-permute-start(bf16[6144,128]{1,0:T(8,128)(2,1)S(1)} %collective-permute-done.nq), channel_id=1, source_target_pairs={{32,40},{33,41},{34,42},{35,43},{36,44},{37,45},{38,46},{39,47},{4... | collective-permute-start | bytes 4718600 | tf_op jit(solution)/shard_map/ppermute | solution.py:47
  63.1 28.2 %collective-permute-done.2.nv = bf16[6144,128]{1,0:T(8,128)(2,1)S(1)} collective-permute-done((bf16[6144,128]{1,0:T(8,128)(2,1)}, bf16[6144,128]{1,0:T(8,128)(2,1)S(1)}, u32[]{:S(2)}, u32[]{:S(2)}) %collective-permute-start.2) | collective-permute-done | bytes 1572896 | tf_op jit(solution)/shard_map/ppermute | solution.py:47
  91.3 1.2 fusion
  92.6 1.3 collective-permute-start.6
  93.9 1.9 %collective-permute-start.5 = (bf16[3072,128]{1,0:T(8,128)(2,1)}, bf16[3072,128]{1,0:T(8,128)(2,1)}, u32[]{:S(2)}, u32[]{:S(2)}) collective-permute-start(bf16[3072,128]{1,0:T(8,128)(2,1)} %get-tuple-element.34), channel_id=1, source_target_pairs={{32,40},{33,41},{34,42},{35,43},{36,44},{37,45},{38,46},{39,47},{4... | collective-permute-start | bytes 2359304 | tf_op jit(solution)/shard_map/ppermute | solution.py:47
  95.8 0.1 pad_add_fusion.1.place
  95.9 2.7 %collective-permute-done.3.fq = bf16[6144,128]{1,0:T(8,128)(2,1)} collective-permute-done((bf16[6144,128]{1,0:T(8,128)(2,1)S(1)}, bf16[6144,128]{1,0:T(8,128)(2,1)}, u32[]{:S(2)}, u32[]{:S(2)}) %collective-permute-start.3) | collective-permute-done | bytes 1572896 | tf_op jit(solution)/shard_map/ppermute | solution.py:47
  98.6 0.0 collective-permute-done.4.fk.refs_1_
  98.6 9.3 %collective-permute-done.6.fv1 = bf16[3072,128]{1,0:T(8,128)(2,1)} collective-permute-done((bf16[3072,128]{1,0:T(8,128)(2,1)}, bf16[3072,128]{1,0:T(8,128)(2,1)}, u32[]{:S(2)}, u32[]{:S(2)}) %collective-permute-start.6) | collective-permute-done | bytes 786464 | tf_op jit(solution)/shard_map/ppermute | solution.py:47
  107.9 0.1 collective-permute-done.5.fv0
  108.0 2.7 %all-gather.2.cloned.1.call-done.tokens.ids = bf16[512,6272]{1,0:T(8,128)(2,1)} async-done(((bf16[32,6272]{1,0:T(8,128)(2,1)}), bf16[512,6272]{1,0:T(8,128)(2,1)}) %all-gather.2.cloned.1.call-update) | async-done | bytes 6422544 | tf_op jit(solution)/shard_map/all_gather | solution.py:257
  110.7 0.0 copy-done.4
  110.7 11.5 %shard_map.75 = (bf16[272,384]{1,0:T(8,128)(2,1)S(1)}, bf16[272,384]{1,0:T(8,128)(2,1)S(1)}, bf16[272,384]{1,0:T(8,128)(2,1)S(1)}, bf16[272,384]{1,0:T(8,128)(2,1)S(1)}, bf16[272,384]{1,0:T(8,128)(2,1)S(1)}) custom-call(s32[2]{0:T(128)S(1)} %pad_add_fusion.1.place, bf16[512,6272]{1,0:T(8,128)(2,1)} %all-gather.2.cloned.1.call-done.tokens.ids, ...), custom_call_target="tpu_custom_call" | custom-call | tf_op jit(solution)/shard_map/pallas_call | solution.py:278
  122.3 4.5 %collective-permute-start.7 = (bf16[272,384]{1,0:T(8,128)(2,1)S(1)}, bf16[272,384]{1,0:T(8,128)(2,1)S(1)}, u32[]{:S(2)}, u32[]{:S(2)}) collective-permute-start(bf16[272,384]{1,0:T(8,128)(2,1)S(1)} %get-tuple-element.29), channel_id=1, source_target_pairs={{0,32},{1,33},{2,34},{3,35},{4,36},{5,37},{6,38},{7,39},{8,40},{9,... | collective-permute-start | bytes 626696 | tf_op jit(solution)/shard_map/ppermute | solution.py:47
  126.8 4.3 %collective-permute-start.8 = (bf16[272,384]{1,0:T(8,128)(2,1)S(1)}, bf16[272,384]{1,0:T(8,128)(2,1)S(1)}, u32[]{:S(2)}, u32[]{:S(2)}) collective-permute-start(bf16[272,384]{1,0:T(8,128)(2,1)S(1)} %get-tuple-element.30), channel_id=1, source_target_pairs={{0,8},{1,9},{2,10},{3,11},{4,12},{5,13},{6,14},{7,15},{8,0},{9,1},... | collective-permute-start | bytes 626696 | tf_op jit(solution)/shard_map/ppermute | solution.py:47
  131.1 3.8 %collective-permute-start.9 = (bf16[272,384]{1,0:T(8,128)(2,1)S(1)}, bf16[272,384]{1,0:T(8,128)(2,1)S(1)}, u32[]{:S(2)}, u32[]{:S(2)}) collective-permute-start(bf16[272,384]{1,0:T(8,128)(2,1)S(1)} %get-tuple-element.31), channel_id=1, source_target_pairs={{0,40},{1,41},{2,42},{3,43},{4,44},{5,45},{6,46},{7,47},{8,32},{9,... | collective-permute-start | bytes 626696 | tf_op jit(solution)/shard_map/ppermute | solution.py:47
  134.8 1.9 %collective-permute-start.10 = (bf16[272,384]{1,0:T(8,128)(2,1)S(1)}, bf16[272,384]{1,0:T(8,128)(2,1)S(1)}, u32[]{:S(2)}, u32[]{:S(2)}) collective-permute-start(bf16[272,384]{1,0:T(8,128)(2,1)S(1)} %get-tuple-element.32), channel_id=1, source_target_pairs={{32,48},{33,49},{34,50},{35,51},{36,52},{37,53},{38,54},{39,55},{4... | collective-permute-start | bytes 626696 | tf_op jit(solution)/shard_map/ppermute | solution.py:47
  136.8 0.0 collective-permute-done.7.got0
  136.8 0.0 collective-permute-done.8.got1
  136.8 3.6 %collective-permute-done.9.got2 = bf16[272,384]{1,0:T(8,128)(2,1)S(1)} collective-permute-done((bf16[272,384]{1,0:T(8,128)(2,1)S(1)}, bf16[272,384]{1,0:T(8,128)(2,1)S(1)}, u32[]{:S(2)}, u32[]{:S(2)}) %collective-permute-start.9) | collective-permute-done | bytes 208928 | tf_op jit(solution)/shard_map/ppermute | solution.py:47
  140.4 2.7 %collective-permute-done.10.got3 = bf16[272,384]{1,0:T(8,128)(2,1)S(1)} collective-permute-done((bf16[272,384]{1,0:T(8,128)(2,1)S(1)}, bf16[272,384]{1,0:T(8,128)(2,1)S(1)}, u32[]{:S(2)}, u32[]{:S(2)}) %collective-permute-start.10) | collective-permute-done | bytes 208928 | tf_op jit(solution)/shard_map/ppermute | solution.py:47
  143.1 3.3 %shard_map.76 = bf16[32,32,128]{2,1,0:T(8,128)(2,1)S(1)} custom-call(s32[2]{0:T(128)S(1)} %pad_add_fusion.1.place, bf16[272,384]{1,0:T(8,128)(2,1)S(1)} %get-tuple-element.28.kept, bf16[272,384]{1,0:T(8,128)(2,1)S(1)} %collective-permute-done.7.got0, bf16[272,384]{1,0:T(8,128)(2,1)S(1)} %collective-permute-done.8.got1, ...), custom_call_target="tpu_custom_call" | custom-call | tf_op jit(solution)/shard_map/pallas_call | solution.py:307
  146.4 17.4 %all_to_all.10 = bf16[32,32,128]{2,1,0:T(8,128)(2,1)S(1)} all-to-all(bf16[32,32,128]{2,1,0:T(8,128)(2,1)S(1)} %shard_map.76), channel_id=1, replica_groups=mesh['y'=8,'core'=2,'half'=2,'side'=2,'z'=8] {'half','side','z'}, dimensions={0} | all-to-all | bytes 524288 | tf_op jit(solution)/shard_map/all_to_all | solution.py:316
  163.7 0.7 copy_bitcast_fusion
  (4 shorter events, 0.0 us)
Async XLA Ops:
  7.2 2.3 %copy-start = (bf16[3,6144,128]{2,1,0:T(8,128)(2,1)S(1)}, bf16[3,6144,128]{2,1,0:T(8,128)(2,1)}, u32[]{:S(2)}) copy-start(bf16[3,6144,128]{2,1,0:T(8,128)(2,1)} %own.1) | copy-start | bytes 14155780
  9.6 1.0 copy-start.1
  10.5 0.7 copy-start.3
  13.8 1.2 copy-start.5
  15.0 16.3 %copy-start.6 = (s32[1,32]{1,0:T(1,128)S(1)}, s32[1,32]{1,0:T(1,128)}, u32[]{:S(2)}) copy-start(s32[1,32]{1,0:T(1,128)} %param.10) | copy-start | bytes 388
  15.0 41.0 %collective-permute-start.1 = (bf16[6160,128]{1,0:T(8,128)(2,1)}, bf16[6160,128]{1,0:T(8,128)(2,1)}, u32[]{:S(2)}, u32[]{:S(2)}) collective-permute-start(bf16[6160,128]{1,0:T(8,128)(2,1)} %get-tuple-element.22), channel_id=1, source_target_pairs={{0,8},{1,9},{2,10},{3,11},{4,12},{5,13},{6,14},{7,15},{8,0},{9,1},... | collective-permute-start | bytes 4730888 | tf_op jit(solution)/shard_map/ppermute | solution.py:47
  20.4 35.6 %collective-permute-start = (bf16[6144,128]{1,0:T(8,128)(2,1)}, bf16[6144,128]{1,0:T(8,128)(2,1)S(1)}, u32[]{:S(2)}, u32[]{:S(2)}) collective-permute-start(bf16[6144,128]{1,0:T(8,128)(2,1)} %get-tuple-element.20), channel_id=1, source_target_pairs={{0,8},{1,9},{2,10},{3,11},{4,12},{5,13},{6,14},{7,15},{8,0},{9,1},... | collective-permute-start | bytes 4718600 | tf_op jit(solution)/shard_map/ppermute | solution.py:47
  22.3 32.2 %copy-start.2 = (f32[6144]{0:T(1024)S(1)}, f32[6144]{0:T(1024)}, u32[]{:S(2)}) copy-start(f32[6144]{0:T(1024)} %param.11) | copy-start | bytes 73732
  22.3 32.0 %all-to-all-start = ((bf16[16,4,6272]{2,1,0:T(4,128)(2,1)}), bf16[16,4,6272]{2,1,0:T(4,128)(2,1)S(1)}, u32[]{:S(2)}, u32[]{:S(2)}) async-start(bf16[16,4,6272]{2,1,0:T(4,128)(2,1)} %get-tuple-element.19), calls=%async_computation | async-start | bytes 1605632 | tf_op jit(solution)/shard_map/all_to_all | solution.py:248
  31.3 79.4 %all-gather.2.cloned.1.call-start = ((), (), s32[]{:S(2)}) async-start(), calls=%async_computation.2 | async-start | bytes 6823936 | tf_op jit(solution)/shard_map/all_gather | solution.py:257
  56.0 54.7 %copy-start.4 = (f32[2,128]{1,0:T(2,128)S(1)}, f32[2,128]{1,0:T(2,128)}, u32[]{:S(2)}) copy-start(f32[2,128]{1,0:T(2,128)} %own_gain.1) | copy-start | bytes 3076
  56.0 35.3 %collective-permute-start.2 = (bf16[6144,128]{1,0:T(8,128)(2,1)}, bf16[6144,128]{1,0:T(8,128)(2,1)S(1)}, u32[]{:S(2)}, u32[]{:S(2)}) collective-permute-start(bf16[6144,128]{1,0:T(8,128)(2,1)} %copy-done.5), channel_id=1, source_target_pairs={{0,8},{1,9},{2,10},{3,11},{4,12},{5,13},{6,14},{7,15},{8,0},{9,1},... | collective-permute-start | bytes 4718600 | tf_op jit(solution)/shard_map/ppermute | solution.py:47
  59.9 38.8 %collective-permute-start.4 = (bf16[6160,128]{1,0:T(8,128)(2,1)}, bf16[6160,128]{1,0:T(8,128)(2,1)}, u32[]{:S(2)}, u32[]{:S(2)}) collective-permute-start(bf16[6160,128]{1,0:T(8,128)(2,1)} %collective-permute-done.1.nk.refs_0_), channel_id=1, source_target_pairs={{0,56},{1,57},{2,58},{3,59},{4,60},{5,61},{6,62},{7,63},{8,48},{9,... | collective-permute-start | bytes 4730888 | tf_op jit(solution)/shard_map/ppermute | solution.py:47
  61.2 37.5 %collective-permute-start.3 = (bf16[6144,128]{1,0:T(8,128)(2,1)S(1)}, bf16[6144,128]{1,0:T(8,128)(2,1)}, u32[]{:S(2)}, u32[]{:S(2)}) collective-permute-start(bf16[6144,128]{1,0:T(8,128)(2,1)S(1)} %collective-permute-done.nq), channel_id=1, source_target_pairs={{32,40},{33,41},{34,42},{35,43},{36,44},{37,45},{38,46},{39,47},{4... | collective-permute-start | bytes 4718600 | tf_op jit(solution)/shard_map/ppermute | solution.py:47
  92.6 15.3 %collective-permute-start.6 = (bf16[3072,128]{1,0:T(8,128)(2,1)}, bf16[3072,128]{1,0:T(8,128)(2,1)}, u32[]{:S(2)}, u32[]{:S(2)}) collective-permute-start(bf16[3072,128]{1,0:T(8,128)(2,1)} %get-tuple-element.33), channel_id=1, source_target_pairs={{0,56},{1,57},{2,58},{3,59},{4,60},{5,61},{6,62},{7,63},{8,48},{9,... | collective-permute-start | bytes 2359304 | tf_op jit(solution)/shard_map/ppermute | solution.py:47
  93.9 14.1 %collective-permute-start.5 = (bf16[3072,128]{1,0:T(8,128)(2,1)}, bf16[3072,128]{1,0:T(8,128)(2,1)}, u32[]{:S(2)}, u32[]{:S(2)}) collective-permute-start(bf16[3072,128]{1,0:T(8,128)(2,1)} %get-tuple-element.34), channel_id=1, source_target_pairs={{32,40},{33,41},{34,42},{35,43},{36,44},{37,45},{38,46},{39,47},{4... | collective-permute-start | bytes 2359304 | tf_op jit(solution)/shard_map/ppermute | solution.py:47
  122.3 14.5 %collective-permute-start.7 = (bf16[272,384]{1,0:T(8,128)(2,1)S(1)}, bf16[272,384]{1,0:T(8,128)(2,1)S(1)}, u32[]{:S(2)}, u32[]{:S(2)}) collective-permute-start(bf16[272,384]{1,0:T(8,128)(2,1)S(1)} %get-tuple-element.29), channel_id=1, source_target_pairs={{0,32},{1,33},{2,34},{3,35},{4,36},{5,37},{6,38},{7,39},{8,40},{9,... | collective-permute-start | bytes 626696 | tf_op jit(solution)/shard_map/ppermute | solution.py:47
  126.8 10.0 %collective-permute-start.8 = (bf16[272,384]{1,0:T(8,128)(2,1)S(1)}, bf16[272,384]{1,0:T(8,128)(2,1)S(1)}, u32[]{:S(2)}, u32[]{:S(2)}) collective-permute-start(bf16[272,384]{1,0:T(8,128)(2,1)S(1)} %get-tuple-element.30), channel_id=1, source_target_pairs={{0,8},{1,9},{2,10},{3,11},{4,12},{5,13},{6,14},{7,15},{8,0},{9,1},... | collective-permute-start | bytes 626696 | tf_op jit(solution)/shard_map/ppermute | solution.py:47
  131.1 9.4 %collective-permute-start.9 = (bf16[272,384]{1,0:T(8,128)(2,1)S(1)}, bf16[272,384]{1,0:T(8,128)(2,1)S(1)}, u32[]{:S(2)}, u32[]{:S(2)}) collective-permute-start(bf16[272,384]{1,0:T(8,128)(2,1)S(1)} %get-tuple-element.31), channel_id=1, source_target_pairs={{0,40},{1,41},{2,42},{3,43},{4,44},{5,45},{6,46},{7,47},{8,32},{9,... | collective-permute-start | bytes 626696 | tf_op jit(solution)/shard_map/ppermute | solution.py:47
  134.8 8.3 %collective-permute-start.10 = (bf16[272,384]{1,0:T(8,128)(2,1)S(1)}, bf16[272,384]{1,0:T(8,128)(2,1)S(1)}, u32[]{:S(2)}, u32[]{:S(2)}) collective-permute-start(bf16[272,384]{1,0:T(8,128)(2,1)S(1)} %get-tuple-element.32), channel_id=1, source_target_pairs={{32,48},{33,49},{34,50},{35,51},{36,52},{37,53},{38,54},{39,55},{4... | collective-permute-start | bytes 626696 | tf_op jit(solution)/shard_map/ppermute | solution.py:47
Sparse Core Ops, SparseCore 0:
  56.1 54.5 all-gather.1

commit v5 on v3

--- a/solution.py
+++ b/solution.py
@@ -82,9 +82,13 @@
     return (centered * lax.rsqrt(spread + 1e-06) * gain).astype(BF16)
 
 
-def pack_body(rows, plan, weight, out, first_two, sem):
-    copy = pltpu.make_async_copy(weight.at[0:2], first_two, sem)
-    copy.start()
+def pack_body(rows, plan, weight, out, first_two, last, sem):
+    copies = [
+        pltpu.make_async_copy(weight.at[0:2], first_two, sem.at[0]),
+        pltpu.make_async_copy(weight.at[2], last, sem.at[1]),
+    ]
+    for copy in copies:
+        copy.start()
     tok, width = rows.shape
     groups, capacity, _ = out.shape
     slots = groups * capacity
@@ -103,7 +107,8 @@
     for g in range(groups):
         out[g, :, :width] = sent[g * capacity : (g + 1) * capacity, :]
         out[g, :, width:] = slot[g * capacity : (g + 1) * capacity, :]
-    copy.wait()
+    for copy in copies:
+        copy.wait()
 
 
 def place_body(got, ids_col, gain, out):
@@ -203,19 +208,24 @@
     first_core = c == 0
     go = functools.partial(lambda array, move: send(array, n_dp, move))
 
-    packed, qk_weight = pl.pallas_call(
+    packed, qk_weight, v_weight = pl.pallas_call(
         pack_body,
         out_shape=(
             jax.ShapeDtypeStruct((n_dp, capacity, width + LANES), BF16),
             jax.ShapeDtypeStruct((2, width, HD), BF16),
+            jax.ShapeDtypeStruct((width, HD), BF16),
         ),
         in_specs=[
             pl.BlockSpec(memory_space=VMEM),
             pl.BlockSpec(memory_space=VMEM),
             pl.BlockSpec(memory_space=pltpu.HBM),
         ],
-        out_specs=(pl.BlockSpec(memory_space=VMEM), pl.BlockSpec(memory_space=pltpu.HBM)),
-        scratch_shapes=[pltpu.SemaphoreType.DMA],
+        out_specs=(
+            pl.BlockSpec(memory_space=VMEM),
+            pl.BlockSpec(memory_space=pltpu.HBM),
+            pl.BlockSpec(memory_space=pltpu.HBM),
+        ),
+        scratch_shapes=[pltpu.SemaphoreType.DMA((2,))],
         compiler_params=pltpu.CompilerParams(vmem_limit_bytes=32 << 20),
     )(packed_rows, jnp.stack([dest_group, dest_slot]), qkv_weight)
     near_qk = go(qk_weight, to_next)
@@ -232,7 +242,7 @@
     placed = after(placed, near_qk, gain_next, gain_far)
     gathered = lax.all_gather(placed, ("core", "z"), axis=0, tiled=True)
     half = width // 2
-    near_v = go(after(qkv_weight[2], placed), to_next)
+    near_v = go(v_weight, to_next)
     far = [go(after(near_qk[0], placed), on_by_side), go(after(near_qk[1], placed), on_by_mirror)]
     far.append(go(near_v[:half], on_by_side))
     far.append(go(near_v[half:], on_by_mirror))
@@ -242,7 +252,7 @@
     place = jnp.stack([c, lax.axis_index(("half", "side"))])
 
     rows = gathered.shape[0]
-    step = width // 6
+    step = width // 4
     steps = width // step
     whole = pl.BlockSpec((step, HD), lambda k: (k, 0))
     qkv = jax.ShapeDtypeStruct((rows // 2 + 16, 3 * HD), BF16)

time: 168 us -> 166 us (0.988)
  transfers between devices with their start and end apart: 14 -> 14, of which waited for: 8 -> 6; matrix products, arithmetic and copies ran while one was open for 4% -> 3% of each run, Pallas kernels for 1% -> 1%
where the time goes in v5:
time: 166 us; the launch traced here: 164 us
  waiting for transfers between devices  67.7 us (41%)
  starting transfers between devices  41 us (25%)
  Pallas kernels  18.3 us (11%)
  between operations  13.6 us (8%)
  blocking collectives  13.2 us (8%)
  local copies, waits for them, and re-layouts  9.41 us (6%)
    ppermute x12, waiting for transfers between devices, send(): return lax.ppermute(array, AXES, pairs(n_dp, move))  51.9 us
    ppermute x12, starting transfers between devices, send(): return lax.ppermute(array, AXES, pairs(n_dp, move))  33.7 us
    all_to_all x1, waiting for transfers between devices, local(): lax.all_to_all(packed, ('y', 'core'), split_axis=0, concat_axis=0, tiled=...  15.7 us
    all_to_all x1, blocking collectives, local(): lax.all_to_all(result, ('half', 'side', 'z'), split_axis=0, concat_axis=0...  13.2 us
    pallas_call x1, Pallas kernels, local(): pl.pallas_call(project_body, grid=(steps,), out_shape=(qkv,) * 5, in_spec...  10.5 us
    all_to_all x1, starting transfers between devices, local(): lax.all_to_all(packed, ('y', 'core'), split_axis=0, concat_axis=0, tiled=...  7.24 us
    squeeze x1, local copies, waits for them, and re-layouts, local(): near_qk[1]  3.82 us
    unnamed x10, local copies, waits for them, and re-layouts  3.35 us
  transfers between devices with their start and end apart: 14, of which 6 were waited for; matrix products, arithmetic and copies ran while one was open for 3% of the time, Pallas kernels for 1%

profile of v5, /device:TPU:1, one launch (start us, length us, event | category | flops | bytes accessed | tf_op | source)
XLA Modules:
  0.0 164.0 jit_solution(2245556814584536051)
XLA Ops:
  6.5 0.7 pad_add_fusion.plan
  7.2 2.3 %copy-done = bf16[3,6144,128]{2,1,0:T(8,128)(2,1)S(1)} copy-done((bf16[3,6144,128]{2,1,0:T(8,128)(2,1)S(1)}, bf16[3,6144,128]{2,1,0:T(8,128)(2,1)}, u32[]{:S(2)}) %copy-start) | copy-done | bytes 4718616
  9.6 1.0 copy-done.1
  10.5 3.1 %shard_map.73 = (bf16[16,4,6272]{2,1,0:T(4,128)(2,1)}, bf16[2,6144,128]{2,1,0:T(8,128)(2,1)}, bf16[6144,128]{1,0:T(8,128)(2,1)}) custom-call(bf16[32,6144]{1,0:T(8,128)(2,1)S(1)} %copy-done.1, s32[2,32]{1,0:T(2,128)S(1)} %pad_add_fusion.plan, bf16[3,6144,128]{2,1,0:T(8,128)(2,1)S(1)} %copy-done), custom_call_target="tpu_custom_call" | custom-call | tf_op jit(solution)/shard_map/pallas_call | solution.py:211
  13.7 0.0 copy-start.3
  13.7 0.0 copy-start.4
  13.7 5.2 %collective-permute-start = (bf16[2,6144,128]{2,1,0:T(8,128)(2,1)}, bf16[2,6144,128]{2,1,0:T(8,128)(2,1)}, u32[]{:S(2)}, u32[]{:S(2)}) collective-permute-start(bf16[2,6144,128]{2,1,0:T(8,128)(2,1)} %get-tuple-element.18), channel_id=1, source_target_pairs={{0,8},{1,9},{2,10},{3,11},{4,12},{5,13},{6,14},{7,15},{8,0},{9,1},... | collective-permute-start | bytes 9437192 | tf_op jit(solution)/shard_map/ppermute | solution.py:47
  18.9 0.0 copy-start.2
  18.9 7.2 %all-to-all-start = ((bf16[16,4,6272]{2,1,0:T(4,128)(2,1)}), bf16[16,4,6272]{2,1,0:T(4,128)(2,1)S(1)}, u32[]{:S(2)}, u32[]{:S(2)}) async-start(bf16[16,4,6272]{2,1,0:T(4,128)(2,1)} %get-tuple-element.17), calls=%async_computation | async-start | bytes 1605632 | tf_op jit(solution)/shard_map/all_to_all | solution.py:234
  26.2 0.0 all-gather.2.cloned.1.call-start
  26.2 3.3 %collective-permute-start.1 = (f32[2,128]{1,0:T(2,128)S(1)}, f32[2,128]{1,0:T(2,128)S(1)}, u32[]{:S(2)}, u32[]{:S(2)}) collective-permute-start(f32[2,128]{1,0:T(2,128)S(1)} %copy-done.3), channel_id=1, source_target_pairs={{0,8},{1,9},{2,10},{3,11},{4,12},{5,13},{6,14},{7,15},{8,0},{9,1},... | collective-permute-start | bytes 3080 | tf_op jit(solution)/shard_map/ppermute | solution.py:47
  29.5 3.8 %collective-permute-start.2 = (f32[2,128]{1,0:T(2,128)S(1)}, f32[2,128]{1,0:T(2,128)S(1)}, u32[]{:S(2)}, u32[]{:S(2)}) collective-permute-start(f32[2,128]{1,0:T(2,128)S(1)} %copy-done.3), channel_id=1, source_target_pairs={{0,16},{1,17},{2,18},{3,19},{4,20},{5,21},{6,22},{7,23},{8,24},{9,... | collective-permute-start | bytes 3080 | tf_op jit(solution)/shard_map/ppermute | solution.py:47
  33.3 0.0 copy-done.4
  33.3 0.1 copy.9.ids_col
  33.4 15.7 %all-to-all-done = bf16[16,4,6272]{2,1,0:T(4,128)(2,1)S(1)} async-done(((bf16[16,4,6272]{2,1,0:T(4,128)(2,1)}), bf16[16,4,6272]{2,1,0:T(4,128)(2,1)S(1)}, u32[]{:S(2)}, u32[]{:S(2)}) %all-to-all-start) | async-done | bytes 802848 | tf_op jit(solution)/shard_map/all_to_all | solution.py:234
  49.2 0.2 reshape.9.got
  49.3 0.0 copy-done.2
  49.4 1.5 shard_map.74
  50.8 3.1 %collective-permute-done.1 = f32[2,128]{1,0:T(2,128)S(1)} collective-permute-done((f32[2,128]{1,0:T(2,128)S(1)}, f32[2,128]{1,0:T(2,128)S(1)}, u32[]{:S(2)}, u32[]{:S(2)}) %collective-permute-start.1) | collective-permute-done | bytes 1056 | tf_op jit(solution)/shard_map/ppermute | solution.py:47
  53.9 0.0 collective-permute-done.2
  53.9 0.0 collective-permute-done.nqk
  53.9 0.0 all-gather.2.cloned.1.call-update
  53.9 4.6 %collective-permute-start.3 = (bf16[6144,128]{1,0:T(8,128)(2,1)}, bf16[6144,128]{1,0:T(8,128)(2,1)S(1)}, u32[]{:S(2)}, u32[]{:S(2)}) collective-permute-start(bf16[6144,128]{1,0:T(8,128)(2,1)} %get-tuple-element.21), channel_id=1, source_target_pairs={{0,8},{1,9},{2,10},{3,11},{4,12},{5,13},{6,14},{7,15},{8,0},{9,1},... | collective-permute-start | bytes 4718600 | tf_op jit(solution)/shard_map/ppermute | solution.py:47
  58.5 3.8 %slice_bitcast_fusion = (bf16[6144,128]{1,0:T(8,128)(2,1)}, bf16[6144,128]{1,0:T(8,128)(2,1)}) fusion(bf16[2,6144,128]{2,1,0:T(8,128)(2,1)} %collective-permute-done.nqk), kind=kLoop, calls=%fused_computation | loop fusion | bytes 6291456 | tf_op jit(solution)/shard_map/squeeze | solution.py:246
  62.3 1.3 collective-permute-start.5
  63.6 1.9 %collective-permute-start.4 = (bf16[6144,128]{1,0:T(8,128)(2,1)}, bf16[6144,128]{1,0:T(8,128)(2,1)S(1)}, u32[]{:S(2)}, u32[]{:S(2)}) collective-permute-start(bf16[6144,128]{1,0:T(8,128)(2,1)} %get-tuple-element.22), channel_id=1, source_target_pairs={{32,40},{33,41},{34,42},{35,43},{36,44},{37,45},{38,46},{39,47},{4... | collective-permute-start | bytes 4718600 | tf_op jit(solution)/shard_map/ppermute | solution.py:47
  65.5 18.6 %collective-permute-done.3.nv = bf16[6144,128]{1,0:T(8,128)(2,1)S(1)} collective-permute-done((bf16[6144,128]{1,0:T(8,128)(2,1)}, bf16[6144,128]{1,0:T(8,128)(2,1)S(1)}, u32[]{:S(2)}, u32[]{:S(2)}) %collective-permute-start.3) | collective-permute-done | bytes 1572896 | tf_op jit(solution)/shard_map/ppermute | solution.py:47
  84.1 1.3 fusion
  85.4 1.9 %collective-permute-start.6 = (bf16[3072,128]{1,0:T(8,128)(2,1)}, bf16[3072,128]{1,0:T(8,128)(2,1)}, u32[]{:S(2)}, u32[]{:S(2)}) collective-permute-start(bf16[3072,128]{1,0:T(8,128)(2,1)} %get-tuple-element.32), channel_id=1, source_target_pairs={{32,40},{33,41},{34,42},{35,43},{36,44},{37,45},{38,46},{39,47},{4... | collective-permute-start | bytes 2359304 | tf_op jit(solution)/shard_map/ppermute | solution.py:47
  87.3 1.3 collective-permute-start.7
  88.6 0.1 pad_add_fusion.1.place
  88.7 18.9 %collective-permute-done.6.fv0 = bf16[3072,128]{1,0:T(8,128)(2,1)} collective-permute-done((bf16[3072,128]{1,0:T(8,128)(2,1)}, bf16[3072,128]{1,0:T(8,128)(2,1)}, u32[]{:S(2)}, u32[]{:S(2)}) %collective-permute-start.6) | collective-permute-done | bytes 786464 | tf_op jit(solution)/shard_map/ppermute | solution.py:47
  107.6 7.4 %collective-permute-done.7.fv1 = bf16[3072,128]{1,0:T(8,128)(2,1)} collective-permute-done((bf16[3072,128]{1,0:T(8,128)(2,1)}, bf16[3072,128]{1,0:T(8,128)(2,1)}, u32[]{:S(2)}, u32[]{:S(2)}) %collective-permute-start.7) | collective-permute-done | bytes 786464 | tf_op jit(solution)/shard_map/ppermute | solution.py:47
  115.0 0.0 collective-permute-done.5.fk
  115.0 0.0 collective-permute-done.4.fq
  115.0 0.0 all-gather.2.cloned.1.call-done.tokens.ids
  115.0 10.5 %shard_map.75 = (bf16[272,384]{1,0:T(8,128)(2,1)S(1)}, bf16[272,384]{1,0:T(8,128)(2,1)S(1)}, bf16[272,384]{1,0:T(8,128)(2,1)S(1)}, bf16[272,384]{1,0:T(8,128)(2,1)S(1)}, bf16[272,384]{1,0:T(8,128)(2,1)S(1)}) custom-call(s32[2]{0:T(128)S(1)} %pad_add_fusion.1.place, bf16[512,6272]{1,0:T(8,128)(2,1)} %all-gather.2.cloned.1.call-done.tokens.ids, ...), custom_call_target="tpu_custom_call" | custom-call | tf_op jit(solution)/shard_map/pallas_call | solution.py:259
  125.5 1.9 %collective-permute-start.10 = (bf16[272,384]{1,0:T(8,128)(2,1)S(1)}, bf16[272,384]{1,0:T(8,128)(2,1)S(1)}, u32[]{:S(2)}, u32[]{:S(2)}) collective-permute-start(bf16[272,384]{1,0:T(8,128)(2,1)S(1)} %get-tuple-element.27), channel_id=1, source_target_pairs={{0,40},{1,41},{2,42},{3,43},{4,44},{5,45},{6,46},{7,47},{8,32},{9,... | collective-permute-start | bytes 626696 | tf_op jit(solution)/shard_map/ppermute | solution.py:47
  127.4 1.9 %collective-permute-start.11 = (bf16[272,384]{1,0:T(8,128)(2,1)S(1)}, bf16[272,384]{1,0:T(8,128)(2,1)S(1)}, u32[]{:S(2)}, u32[]{:S(2)}) collective-permute-start(bf16[272,384]{1,0:T(8,128)(2,1)S(1)} %get-tuple-element.28), channel_id=1, source_target_pairs={{32,48},{33,49},{34,50},{35,51},{36,52},{37,53},{38,54},{39,55},{4... | collective-permute-start | bytes 626696 | tf_op jit(solution)/shard_map/ppermute | solution.py:47
  129.4 1.9 %collective-permute-start.8 = (bf16[272,384]{1,0:T(8,128)(2,1)S(1)}, bf16[272,384]{1,0:T(8,128)(2,1)S(1)}, u32[]{:S(2)}, u32[]{:S(2)}) collective-permute-start(bf16[272,384]{1,0:T(8,128)(2,1)S(1)} %get-tuple-element.25), channel_id=1, source_target_pairs={{0,32},{1,33},{2,34},{3,35},{4,36},{5,37},{6,38},{7,39},{8,40},{9,... | collective-permute-start | bytes 626696 | tf_op jit(solution)/shard_map/ppermute | solution.py:47
  131.3 4.7 %collective-permute-start.9 = (bf16[272,384]{1,0:T(8,128)(2,1)S(1)}, bf16[272,384]{1,0:T(8,128)(2,1)S(1)}, u32[]{:S(2)}, u32[]{:S(2)}) collective-permute-start(bf16[272,384]{1,0:T(8,128)(2,1)S(1)} %get-tuple-element.26), channel_id=1, source_target_pairs={{0,8},{1,9},{2,10},{3,11},{4,12},{5,13},{6,14},{7,15},{8,0},{9,1},... | collective-permute-start | bytes 626696 | tf_op jit(solution)/shard_map/ppermute | solution.py:47
  136.0 0.0 collective-permute-done.10.got2
  136.0 0.0 collective-permute-done.11.got3
  136.0 0.0 collective-permute-done.8.got0
  136.0 4.0 %collective-permute-done.9.got1 = bf16[272,384]{1,0:T(8,128)(2,1)S(1)} collective-permute-done((bf16[272,384]{1,0:T(8,128)(2,1)S(1)}, bf16[272,384]{1,0:T(8,128)(2,1)S(1)}, u32[]{:S(2)}, u32[]{:S(2)}) %collective-permute-start.9) | collective-permute-done | bytes 208928 | tf_op jit(solution)/shard_map/ppermute | solution.py:47
  140.0 3.3 %shard_map.76 = bf16[32,32,128]{2,1,0:T(8,128)(2,1)S(1)} custom-call(s32[2]{0:T(128)S(1)} %pad_add_fusion.1.place, bf16[272,384]{1,0:T(8,128)(2,1)S(1)} %get-tuple-element.24.kept, bf16[272,384]{1,0:T(8,128)(2,1)S(1)} %collective-permute-done.8.got0, bf16[272,384]{1,0:T(8,128)(2,1)S(1)} %collective-permute-done.9.got1, ...), custom_call_target="tpu_custom_call" | custom-call | tf_op jit(solution)/shard_map/pallas_call | solution.py:281
  143.2 13.2 %all_to_all.10 = bf16[32,32,128]{2,1,0:T(8,128)(2,1)S(1)} all-to-all(bf16[32,32,128]{2,1,0:T(8,128)(2,1)S(1)} %shard_map.76), channel_id=1, replica_groups=mesh['y'=8,'core'=2,'half'=2,'side'=2,'z'=8] {'half','side','z'}, dimensions={0} | all-to-all | bytes 524288 | tf_op jit(solution)/shard_map/all_to_all | solution.py:290
  156.5 0.7 copy_bitcast_fusion
  (5 shorter events, 0.0 us)
Async XLA Ops:
  7.2 2.3 %copy-start = (bf16[3,6144,128]{2,1,0:T(8,128)(2,1)S(1)}, bf16[3,6144,128]{2,1,0:T(8,128)(2,1)}, u32[]{:S(2)}) copy-start(bf16[3,6144,128]{2,1,0:T(8,128)(2,1)} %own.1) | copy-start | bytes 14155780
  9.6 1.0 copy-start.1
  13.7 12.5 %copy-start.3 = (f32[2,128]{1,0:T(2,128)S(1)}, f32[2,128]{1,0:T(2,128)}, u32[]{:S(2)}) copy-start(f32[2,128]{1,0:T(2,128)} %param.13) | copy-start | bytes 3076
  13.7 19.7 %copy-start.4 = (s32[1,32]{1,0:T(1,128)S(1)}, s32[1,32]{1,0:T(1,128)}, u32[]{:S(2)}) copy-start(s32[1,32]{1,0:T(1,128)} %param.10) | copy-start | bytes 388
  13.7 40.2 %collective-permute-start = (bf16[2,6144,128]{2,1,0:T(8,128)(2,1)}, bf16[2,6144,128]{2,1,0:T(8,128)(2,1)}, u32[]{:S(2)}, u32[]{:S(2)}) collective-permute-start(bf16[2,6144,128]{2,1,0:T(8,128)(2,1)} %get-tuple-element.18), channel_id=1, source_target_pairs={{0,8},{1,9},{2,10},{3,11},{4,12},{5,13},{6,14},{7,15},{8,0},{9,1},... | collective-permute-start | bytes 9437192 | tf_op jit(solution)/shard_map/ppermute | solution.py:47
  18.9 30.4 %copy-start.2 = (f32[6144]{0:T(1024)S(1)}, f32[6144]{0:T(1024)}, u32[]{:S(2)}) copy-start(f32[6144]{0:T(1024)} %param.11) | copy-start | bytes 73732
  18.9 30.2 %all-to-all-start = ((bf16[16,4,6272]{2,1,0:T(4,128)(2,1)}), bf16[16,4,6272]{2,1,0:T(4,128)(2,1)S(1)}, u32[]{:S(2)}, u32[]{:S(2)}) async-start(bf16[16,4,6272]{2,1,0:T(4,128)(2,1)} %get-tuple-element.17), calls=%async_computation | async-start | bytes 1605632 | tf_op jit(solution)/shard_map/all_to_all | solution.py:234
  26.2 88.8 %all-gather.2.cloned.1.call-start = ((), (), s32[]{:S(2)}) async-start(), calls=%async_computation.2 | async-start | bytes 6823936 | tf_op jit(solution)/shard_map/all_gather | solution.py:243
  26.2 27.7 %collective-permute-start.1 = (f32[2,128]{1,0:T(2,128)S(1)}, f32[2,128]{1,0:T(2,128)S(1)}, u32[]{:S(2)}, u32[]{:S(2)}) collective-permute-start(f32[2,128]{1,0:T(2,128)S(1)} %copy-done.3), channel_id=1, source_target_pairs={{0,8},{1,9},{2,10},{3,11},{4,12},{5,13},{6,14},{7,15},{8,0},{9,1},... | collective-permute-start | bytes 3080 | tf_op jit(solution)/shard_map/ppermute | solution.py:47
  29.5 24.4 %collective-permute-start.2 = (f32[2,128]{1,0:T(2,128)S(1)}, f32[2,128]{1,0:T(2,128)S(1)}, u32[]{:S(2)}, u32[]{:S(2)}) collective-permute-start(f32[2,128]{1,0:T(2,128)S(1)} %copy-done.3), channel_id=1, source_target_pairs={{0,16},{1,17},{2,18},{3,19},{4,20},{5,21},{6,22},{7,23},{8,24},{9,... | collective-permute-start | bytes 3080 | tf_op jit(solution)/shard_map/ppermute | solution.py:47
  53.9 30.2 %collective-permute-start.3 = (bf16[6144,128]{1,0:T(8,128)(2,1)}, bf16[6144,128]{1,0:T(8,128)(2,1)S(1)}, u32[]{:S(2)}, u32[]{:S(2)}) collective-permute-start(bf16[6144,128]{1,0:T(8,128)(2,1)} %get-tuple-element.21), channel_id=1, source_target_pairs={{0,8},{1,9},{2,10},{3,11},{4,12},{5,13},{6,14},{7,15},{8,0},{9,1},... | collective-permute-start | bytes 4718600 | tf_op jit(solution)/shard_map/ppermute | solution.py:47
  62.3 52.7 %collective-permute-start.5 = (bf16[6144,128]{1,0:T(8,128)(2,1)}, bf16[6144,128]{1,0:T(8,128)(2,1)}, u32[]{:S(2)}, u32[]{:S(2)}) collective-permute-start(bf16[6144,128]{1,0:T(8,128)(2,1)} %get-tuple-element.23), channel_id=1, source_target_pairs={{0,56},{1,57},{2,58},{3,59},{4,60},{5,61},{6,62},{7,63},{8,48},{9,... | collective-permute-start | bytes 4718600 | tf_op jit(solution)/shard_map/ppermute | solution.py:47
  63.6 51.4 %collective-permute-start.4 = (bf16[6144,128]{1,0:T(8,128)(2,1)}, bf16[6144,128]{1,0:T(8,128)(2,1)S(1)}, u32[]{:S(2)}, u32[]{:S(2)}) collective-permute-start(bf16[6144,128]{1,0:T(8,128)(2,1)} %get-tuple-element.22), channel_id=1, source_target_pairs={{32,40},{33,41},{34,42},{35,43},{36,44},{37,45},{38,46},{39,47},{4... | collective-permute-start | bytes 4718600 | tf_op jit(solution)/shard_map/ppermute | solution.py:47
  85.4 22.2 %collective-permute-start.6 = (bf16[3072,128]{1,0:T(8,128)(2,1)}, bf16[3072,128]{1,0:T(8,128)(2,1)}, u32[]{:S(2)}, u32[]{:S(2)}) collective-permute-start(bf16[3072,128]{1,0:T(8,128)(2,1)} %get-tuple-element.32), channel_id=1, source_target_pairs={{32,40},{33,41},{34,42},{35,43},{36,44},{37,45},{38,46},{39,47},{4... | collective-permute-start | bytes 2359304 | tf_op jit(solution)/shard_map/ppermute | solution.py:47
  87.3 27.7 %collective-permute-start.7 = (bf16[3072,128]{1,0:T(8,128)(2,1)}, bf16[3072,128]{1,0:T(8,128)(2,1)}, u32[]{:S(2)}, u32[]{:S(2)}) collective-permute-start(bf16[3072,128]{1,0:T(8,128)(2,1)} %get-tuple-element.31), channel_id=1, source_target_pairs={{0,56},{1,57},{2,58},{3,59},{4,60},{5,61},{6,62},{7,63},{8,48},{9,... | collective-permute-start | bytes 2359304 | tf_op jit(solution)/shard_map/ppermute | solution.py:47
  125.5 10.5 %collective-permute-start.10 = (bf16[272,384]{1,0:T(8,128)(2,1)S(1)}, bf16[272,384]{1,0:T(8,128)(2,1)S(1)}, u32[]{:S(2)}, u32[]{:S(2)}) collective-permute-start(bf16[272,384]{1,0:T(8,128)(2,1)S(1)} %get-tuple-element.27), channel_id=1, source_target_pairs={{0,40},{1,41},{2,42},{3,43},{4,44},{5,45},{6,46},{7,47},{8,32},{9,... | collective-permute-start | bytes 626696 | tf_op jit(solution)/shard_map/ppermute | solution.py:47
  127.4 8.6 %collective-permute-start.11 = (bf16[272,384]{1,0:T(8,128)(2,1)S(1)}, bf16[272,384]{1,0:T(8,128)(2,1)S(1)}, u32[]{:S(2)}, u32[]{:S(2)}) collective-permute-start(bf16[272,384]{1,0:T(8,128)(2,1)S(1)} %get-tuple-element.28), channel_id=1, source_target_pairs={{32,48},{33,49},{34,50},{35,51},{36,52},{37,53},{38,54},{39,55},{4... | collective-permute-start | bytes 626696 | tf_op jit(solution)/shard_map/ppermute | solution.py:47
  129.4 6.6 %collective-permute-start.8 = (bf16[272,384]{1,0:T(8,128)(2,1)S(1)}, bf16[272,384]{1,0:T(8,128)(2,1)S(1)}, u32[]{:S(2)}, u32[]{:S(2)}) collective-permute-start(bf16[272,384]{1,0:T(8,128)(2,1)S(1)} %get-tuple-element.25), channel_id=1, source_target_pairs={{0,32},{1,33},{2,34},{3,35},{4,36},{5,37},{6,38},{7,39},{8,40},{9,... | collective-permute-start | bytes 626696 | tf_op jit(solution)/shard_map/ppermute | solution.py:47
  131.3 8.7 %collective-permute-start.9 = (bf16[272,384]{1,0:T(8,128)(2,1)S(1)}, bf16[272,384]{1,0:T(8,128)(2,1)S(1)}, u32[]{:S(2)}, u32[]{:S(2)}) collective-permute-start(bf16[272,384]{1,0:T(8,128)(2,1)S(1)} %get-tuple-element.26), channel_id=1, source_target_pairs={{0,8},{1,9},{2,10},{3,11},{4,12},{5,13},{6,14},{7,15},{8,0},{9,1},... | collective-permute-start | bytes 626696 | tf_op jit(solution)/shard_map/ppermute | solution.py:47
Sparse Core Ops, SparseCore 0:
  54.0 55.2 all-gather.1

commit v6 on v5

--- a/solution.py
+++ b/solution.py
@@ -51,10 +51,6 @@
     return (0, x ^ 1, z) if c == 0 else (1, 3 - x, z)
 
 
-def opposite_x(c, x, z):
-    return c, x ^ 2, z
-
-
 def on_by_side(c, x, z):
     return (1, x ^ 1, z) if c == 1 else None
 
@@ -82,10 +78,20 @@
     return (centered * lax.rsqrt(spread + 1e-06) * gain).astype(BF16)
 
 
-def pack_body(rows, plan, weight, out, first_two, last, sem):
+def pack_body(rows, plan, gain, weight, out, first_two, last, parts, sem):
+    depth = weight.shape[1]
+    high = gain[...].astype(BF16)
+    rest = gain[...] - high.astype(F32)
+    middle = rest.astype(BF16)
+    low = (rest - middle.astype(F32)).astype(BF16)
+    pad = jnp.zeros((10, HD), F32)
+    parts[...] = jnp.concatenate(
+        [high.astype(F32), middle.astype(F32), low.astype(F32), pad], axis=0
+    ).astype(BF16)
     copies = [
         pltpu.make_async_copy(weight.at[0:2], first_two, sem.at[0]),
-        pltpu.make_async_copy(weight.at[2], last, sem.at[1]),
+        pltpu.make_async_copy(weight.at[2], last.at[pl.ds(0, depth), :], sem.at[1]),
+        pltpu.make_async_copy(parts, last.at[pl.ds(depth, 16), :], sem.at[2]),
     ]
     for copy in copies:
         copy.start()
@@ -124,8 +130,8 @@
     out[:, width:] = jnp.broadcast_to(ids_col[...].astype(F32), (tok, LANES)).astype(BF16)
 
 
-def project_body(place, tokens, ids, own, nqk, nv, fq, fk, fv0, fv1, gain, *refs):
-    outs, total = refs[:5], refs[5]
+def project_body(place, tokens, ids, own, nqk, nv, fq, fk, fv0, fv1, own_gain, *refs):
+    parts, outs, total = refs[:2], refs[2:7], refs[7]
     k = pl.program_id(0)
     steps = pl.num_programs(0)
     rows = tokens.shape[0] // 2
@@ -145,6 +151,13 @@
         total[...] += part
 
     def emit(dsts):
+        near_gain, far_gain = [
+            p[0:2, :].astype(F32) + p[2:4, :].astype(F32) + p[4:6, :].astype(F32) for p in parts
+        ]
+        gains = (
+            jnp.where(first_core, own_gain[...], near_gain),
+            jnp.where(first_core, near_gain, far_gain),
+        )
         turned = jnp.transpose(ids[...].astype(F32))[0:16, :].astype(BF16)
         for n, dst in enumerate(dsts):
             head, group = n // 2, n % 2
@@ -152,7 +165,7 @@
             for j in range(2):
                 cols = total[at, (3 * head + j) * HD : (3 * head + j + 1) * HD]
                 dst[:rows, j * HD : (j + 1) * HD] = norm_rows(
-                    cols, gain[2 * head + j : 2 * head + j + 1, :]
+                    cols, gains[head][j : j + 1, :]
                 )
             dst[:rows, 2 * HD :] = total[at, (3 * head + 2) * HD : (3 * head + 3) * HD].astype(BF16)
             dst[rows:, :rows] = turned[:, at]
@@ -213,9 +226,10 @@
         out_shape=(
             jax.ShapeDtypeStruct((n_dp, capacity, width + LANES), BF16),
             jax.ShapeDtypeStruct((2, width, HD), BF16),
-            jax.ShapeDtypeStruct((width, HD), BF16),
+            jax.ShapeDtypeStruct((width + 16, HD), BF16),
         ),
         in_specs=[
+            pl.BlockSpec(memory_space=VMEM),
             pl.BlockSpec(memory_space=VMEM),
             pl.BlockSpec(memory_space=VMEM),
             pl.BlockSpec(memory_space=pltpu.HBM),
@@ -225,12 +239,10 @@
             pl.BlockSpec(memory_space=pltpu.HBM),
             pl.BlockSpec(memory_space=pltpu.HBM),
         ),
-        scratch_shapes=[pltpu.SemaphoreType.DMA((2,))],
+        scratch_shapes=[VMEM((16, HD), BF16), pltpu.SemaphoreType.DMA((3,))],
         compiler_params=pltpu.CompilerParams(vmem_limit_bytes=32 << 20),
-    )(packed_rows, jnp.stack([dest_group, dest_slot]), qkv_weight)
+    )(packed_rows, jnp.stack([dest_group, dest_slot]), qk_gain, qkv_weight)
     near_qk = go(qk_weight, to_next)
-    gain_next = go(after(qk_gain, packed), to_next)
-    gain_far = go(after(qk_gain, packed), opposite_x)
     got = lax.all_to_all(packed, ("y", "core"), split_axis=0, concat_axis=0, tiled=True)
     placed = vmem_call(
         place_body, jax.ShapeDtypeStruct((tok, width + LANES), BF16), 3
@@ -239,16 +251,13 @@
         image_ids.reshape(tok, 1),
         ln_gain[None, :],
     )
-    placed = after(placed, near_qk, gain_next, gain_far)
+    placed = after(placed, near_qk)
     gathered = lax.all_gather(placed, ("core", "z"), axis=0, tiled=True)
     half = width // 2
     near_v = go(v_weight, to_next)
     far = [go(after(near_qk[0], placed), on_by_side), go(after(near_qk[1], placed), on_by_mirror)]
     far.append(go(near_v[:half], on_by_side))
     far.append(go(near_v[half:], on_by_mirror))
-    gain = jnp.concatenate(
-        [jnp.where(first_core, qk_gain, gain_next), jnp.where(first_core, gain_next, gain_far)], axis=0
-    )
     place = jnp.stack([c, lax.axis_index(("half", "side"))])
 
     rows = gathered.shape[0]
@@ -272,11 +281,13 @@
             pl.BlockSpec((step, HD), lambda k: (jnp.minimum(k, steps // 2 - 1), 0)),
             pl.BlockSpec((step, HD), lambda k: (jnp.maximum(k - steps // 2, 0), 0)),
             pl.BlockSpec(memory_space=VMEM),
+            pl.BlockSpec((16, HD), lambda k: (width // 16, 0)),
+            pl.BlockSpec((16, HD), lambda k: (half // 16, 0)),
         ],
         out_specs=(pl.BlockSpec(memory_space=VMEM),) * 5,
         scratch_shapes=[VMEM((rows, 6 * HD), F32)],
         compiler_params=pltpu.CompilerParams(vmem_limit_bytes=48 << 20),
-    )(place, gathered, gathered, qkv_weight, near_qk, near_v, *far, gain)
+    )(place, gathered, gathered, qkv_weight, near_qk, near_v, *far, qk_gain, near_v, far[3])
     swapped = [go(array, move) for array, move in zip(sent, EXCHANGE)]
     result = vmem_call(
         attend_body,

time: 166 us -> 167 us (level)
  starting transfers between devices: 41 us -> 36.4 us
  blocking collectives: 13.2 us -> 17 us
  waiting for transfers between devices: 67.7 us -> 69.9 us
    all_to_all x1, waiting for transfers between devices: 15.7 us -> 22.9 us  [local(): lax.all_to_all(packed, ('y', 'core'), split_axis=0, concat_axis=0, tiled=...]
    ppermute x12 -> x10, waiting for transfers between devices: 51.9 us -> 45.4 us  [send(): return lax.ppermute(array, AXES, pairs(n_dp, move))]
    ppermute x12 -> x10, starting transfers between devices: 33.7 us -> 29.1 us  [send(): return lax.ppermute(array, AXES, pairs(n_dp, move))]
    all_to_all x1, blocking collectives: 13.2 us -> 17 us  [local(): lax.all_to_all(result, ('half', 'side', 'z'), split_axis=0, concat_axis=0...]
    all_gather x1, waiting for transfers between devices: 0.01 us -> 1.7 us  [local(): gathered = lax.all_gather(placed, ('core', 'z'), axis=0, tiled=True)]
    unnamed x10 -> x14, local copies, waits for them, and re-layouts: 3.35 us -> 4.03 us
  transfers between devices with their start and end apart: 14 -> 12, of which waited for: 6 -> 8; matrix products, arithmetic and copies ran while one was open for 3% -> 4% of each run, Pallas kernels for 1% -> 1%
where the time goes in v6:
time: 167 us
  waiting for transfers between devices  69.9 us (42%)
  starting transfers between devices  36.4 us (22%)
  Pallas kernels  18.2 us (11%)
  blocking collectives  17 us (10%)
  between operations  13.6 us (8%)
  local copies, waits for them, and re-layouts  10.7 us (6%)
    ppermute x10, waiting for transfers between devices, send(): return lax.ppermute(array, AXES, pairs(n_dp, move))  45.4 us
    ppermute x10, starting transfers between devices, send(): return lax.ppermute(array, AXES, pairs(n_dp, move))  29.1 us
    all_to_all x1, waiting for transfers between devices, local(): lax.all_to_all(packed, ('y', 'core'), split_axis=0, concat_axis=0, tiled=...  22.9 us
    all_to_all x1, blocking collectives, local(): lax.all_to_all(result, ('half', 'side', 'z'), split_axis=0, concat_axis=0...  17 us
    pallas_call x1, Pallas kernels, local(): pl.pallas_call(project_body, grid=(steps,), out_shape=(qkv,) * 5, in_spec...  10.4 us
    all_to_all x1, starting transfers between devices, local(): lax.all_to_all(packed, ('y', 'core'), split_axis=0, concat_axis=0, tiled=...  7.24 us
    unnamed x14, local copies, waits for them, and re-layouts  4.03 us
    squeeze x1, local copies, waits for them, and re-layouts, local(): near_qk[1]  3.72 us
  transfers between devices with their start and end apart: 12, of which 8 were waited for; matrix products, arithmetic and copies ran while one was open for 4% of the time, Pallas kernels for 1%

profile of v6, /device:TPU:1, one launch (start us, length us, event | category | flops | bytes accessed | tf_op | source)
XLA Modules:
  0.0 166.6 jit_solution(15764105651462282427)
XLA Ops:
  6.5 0.7 pad_add_fusion.plan
  7.2 2.3 %copy-done = bf16[3,6144,128]{2,1,0:T(8,128)(2,1)S(1)} copy-done((bf16[3,6144,128]{2,1,0:T(8,128)(2,1)S(1)}, bf16[3,6144,128]{2,1,0:T(8,128)(2,1)}, u32[]{:S(2)}) %copy-start) | copy-done | bytes 4718616
  9.6 1.0 copy-done.1
  10.6 0.7 copy-done.3
  11.2 3.1 %shard_map.73 = (bf16[16,4,6272]{2,1,0:T(4,128)(2,1)}, bf16[2,6144,128]{2,1,0:T(8,128)(2,1)}, bf16[6160,128]{1,0:T(8,128)(2,1)}) custom-call(bf16[32,6144]{1,0:T(8,128)(2,1)S(1)} %copy-done.1, s32[2,32]{1,0:T(2,128)S(1)} %pad_add_fusion.plan, f32[2,128]{1,0:T(2,128)S(1)} %copy-done.3, bf16[3,6144,128]{2,1,0:T(8,128)(2,1)S(1)} %copy-done), custom_call_target="tpu_custom_call" | custom-call | tf_op jit(solution)/shard_map/pallas_call | solution.py:224
  14.3 0.0 copy-start.6
  14.3 5.2 %collective-permute-start = (bf16[2,6144,128]{2,1,0:T(8,128)(2,1)}, bf16[2,6144,128]{2,1,0:T(8,128)(2,1)}, u32[]{:S(2)}, u32[]{:S(2)}) collective-permute-start(bf16[2,6144,128]{2,1,0:T(8,128)(2,1)} %get-tuple-element.17), channel_id=1, source_target_pairs={{0,8},{1,9},{2,10},{3,11},{4,12},{5,13},{6,14},{7,15},{8,0},{9,1},... | collective-permute-start | bytes 9437192 | tf_op jit(solution)/shard_map/ppermute | solution.py:47
  19.5 0.0 copy-start.2
  19.6 7.2 %all-to-all-start = ((bf16[16,4,6272]{2,1,0:T(4,128)(2,1)}), bf16[16,4,6272]{2,1,0:T(4,128)(2,1)S(1)}, u32[]{:S(2)}, u32[]{:S(2)}) async-start(bf16[16,4,6272]{2,1,0:T(4,128)(2,1)} %get-tuple-element.16), calls=%async_computation | async-start | bytes 1605632 | tf_op jit(solution)/shard_map/all_to_all | solution.py:246
  26.8 0.0 all-gather.2.cloned.1.call-start
  26.8 0.0 copy-done.6
  26.8 0.1 copy.9.ids_col
  26.9 22.9 %all-to-all-done = bf16[16,4,6272]{2,1,0:T(4,128)(2,1)S(1)} async-done(((bf16[16,4,6272]{2,1,0:T(4,128)(2,1)}), bf16[16,4,6272]{2,1,0:T(4,128)(2,1)S(1)}, u32[]{:S(2)}, u32[]{:S(2)}) %all-to-all-start) | async-done | bytes 802848 | tf_op jit(solution)/shard_map/all_to_all | solution.py:246
  49.8 0.2 reshape.9.got
  50.0 0.0 copy-done.2
  50.0 1.4 shard_map.74
  51.4 3.1 %collective-permute-done.nqk = bf16[2,6144,128]{2,1,0:T(8,128)(2,1)} collective-permute-done((bf16[2,6144,128]{2,1,0:T(8,128)(2,1)}, bf16[2,6144,128]{2,1,0:T(8,128)(2,1)}, u32[]{:S(2)}, u32[]{:S(2)}) %collective-permute-start) | collective-permute-done | bytes 3145760 | tf_op jit(solution)/shard_map/ppermute | solution.py:47
  54.5 0.0 all-gather.2.cloned.1.call-update
  54.5 4.6 %collective-permute-start.1 = (bf16[6160,128]{1,0:T(8,128)(2,1)}, bf16[6160,128]{1,0:T(8,128)(2,1)S(1)}, u32[]{:S(2)}, u32[]{:S(2)}) collective-permute-start(bf16[6160,128]{1,0:T(8,128)(2,1)} %get-tuple-element.19), channel_id=1, source_target_pairs={{0,8},{1,9},{2,10},{3,11},{4,12},{5,13},{6,14},{7,15},{8,0},{9,1},... | collective-permute-start | bytes 4730888 | tf_op jit(solution)/shard_map/ppermute | solution.py:47
  59.1 3.7 %slice_bitcast_fusion = (bf16[6144,128]{1,0:T(8,128)(2,1)}, bf16[6144,128]{1,0:T(8,128)(2,1)}) fusion(bf16[2,6144,128]{2,1,0:T(8,128)(2,1)} %collective-permute-done.nqk), kind=kLoop, calls=%fused_computation | loop fusion | bytes 6291456 | tf_op jit(solution)/shard_map/squeeze | solution.py:258
  62.8 1.3 collective-permute-start.3
  64.1 0.0 copy-start.4
  64.1 1.9 %collective-permute-start.2 = (bf16[6144,128]{1,0:T(8,128)(2,1)}, bf16[6144,128]{1,0:T(8,128)(2,1)}, u32[]{:S(2)}, u32[]{:S(2)}) collective-permute-start(bf16[6144,128]{1,0:T(8,128)(2,1)} %get-tuple-element.20), channel_id=1, source_target_pairs={{32,40},{33,41},{34,42},{35,43},{36,44},{37,45},{38,46},{39,47},{4... | collective-permute-start | bytes 4718600 | tf_op jit(solution)/shard_map/ppermute | solution.py:47
  66.1 19.5 %collective-permute-done.1.nv.refs_0_ = bf16[6160,128]{1,0:T(8,128)(2,1)S(1)} collective-permute-done((bf16[6160,128]{1,0:T(8,128)(2,1)}, bf16[6160,128]{1,0:T(8,128)(2,1)S(1)}, u32[]{:S(2)}, u32[]{:S(2)}) %collective-permute-start.1) | collective-permute-done | bytes 1576992 | tf_op jit(solution)/shard_map/ppermute | solution.py:47
  85.5 1.0 slice.19
  86.5 1.3 collective-permute-start.5
  87.8 0.9 slice.18
  88.8 0.0 copy-done.5
  88.8 2.4 %collective-permute-start.4 = (bf16[3072,128]{1,0:T(8,128)(2,1)}, bf16[3072,128]{1,0:T(8,128)(2,1)S(1)}, u32[]{:S(2)}, u32[]{:S(2)}) collective-permute-start(bf16[3072,128]{1,0:T(8,128)(2,1)} %slice.18), channel_id=1, source_target_pairs={{32,40},{33,41},{34,42},{35,43},{36,44},{37,45},{38,46},{39,47},{4... | collective-permute-start | bytes 2359304 | tf_op jit(solution)/shard_map/ppermute | solution.py:47
  91.2 0.1 pad_add_fusion.1.place
  91.2 17.0 %collective-permute-done.4.fv0 = bf16[3072,128]{1,0:T(8,128)(2,1)S(1)} collective-permute-done((bf16[3072,128]{1,0:T(8,128)(2,1)}, bf16[3072,128]{1,0:T(8,128)(2,1)S(1)}, u32[]{:S(2)}, u32[]{:S(2)}) %collective-permute-start.4) | collective-permute-done | bytes 786464 | tf_op jit(solution)/shard_map/ppermute | solution.py:47
  108.3 0.0 collective-permute-done.5.fv1.refs_1_
  108.3 0.0 collective-permute-done.3.fk
  108.3 0.0 collective-permute-done.2.fq
  108.3 1.7 %all-gather.2.cloned.1.call-done.tokens.ids = bf16[512,6272]{1,0:T(8,128)(2,1)} async-done(((bf16[32,6272]{1,0:T(8,128)(2,1)}), bf16[512,6272]{1,0:T(8,128)(2,1)}) %all-gather.2.cloned.1.call-update) | async-done | bytes 6422544 | tf_op jit(solution)/shard_map/all_gather | solution.py:255
  110.0 0.0 copy-done.4
  110.0 10.4 %shard_map.75 = (bf16[272,384]{1,0:T(8,128)(2,1)S(1)}, bf16[272,384]{1,0:T(8,128)(2,1)S(1)}, bf16[272,384]{1,0:T(8,128)(2,1)S(1)}, bf16[272,384]{1,0:T(8,128)(2,1)S(1)}, bf16[272,384]{1,0:T(8,128)(2,1)S(1)}) custom-call(s32[2]{0:T(128)S(1)} %pad_add_fusion.1.place, bf16[512,6272]{1,0:T(8,128)(2,1)} %all-gather.2.cloned.1.call-done.tokens.ids, ...), custom_call_target="tpu_custom_call" | custom-call | tf_op jit(solution)/shard_map/pallas_call | solution.py:268
  120.4 4.5 %collective-permute-start.6 = (bf16[272,384]{1,0:T(8,128)(2,1)S(1)}, bf16[272,384]{1,0:T(8,128)(2,1)S(1)}, u32[]{:S(2)}, u32[]{:S(2)}) collective-permute-start(bf16[272,384]{1,0:T(8,128)(2,1)S(1)} %get-tuple-element.23), channel_id=1, source_target_pairs={{0,32},{1,33},{2,34},{3,35},{4,36},{5,37},{6,38},{7,39},{8,40},{9,... | collective-permute-start | bytes 626696 | tf_op jit(solution)/shard_map/ppermute | solution.py:47
  124.9 2.2 %collective-permute-start.7 = (bf16[272,384]{1,0:T(8,128)(2,1)S(1)}, bf16[272,384]{1,0:T(8,128)(2,1)S(1)}, u32[]{:S(2)}, u32[]{:S(2)}) collective-permute-start(bf16[272,384]{1,0:T(8,128)(2,1)S(1)} %get-tuple-element.24), channel_id=1, source_target_pairs={{0,8},{1,9},{2,10},{3,11},{4,12},{5,13},{6,14},{7,15},{8,0},{9,1},... | collective-permute-start | bytes 626696 | tf_op jit(solution)/shard_map/ppermute | solution.py:47
  127.1 3.4 %collective-permute-start.8 = (bf16[272,384]{1,0:T(8,128)(2,1)S(1)}, bf16[272,384]{1,0:T(8,128)(2,1)S(1)}, u32[]{:S(2)}, u32[]{:S(2)}) collective-permute-start(bf16[272,384]{1,0:T(8,128)(2,1)S(1)} %get-tuple-element.25), channel_id=1, source_target_pairs={{0,40},{1,41},{2,42},{3,43},{4,44},{5,45},{6,46},{7,47},{8,32},{9,... | collective-permute-start | bytes 626696 | tf_op jit(solution)/shard_map/ppermute | solution.py:47
  130.4 2.5 %collective-permute-start.9 = (bf16[272,384]{1,0:T(8,128)(2,1)S(1)}, bf16[272,384]{1,0:T(8,128)(2,1)S(1)}, u32[]{:S(2)}, u32[]{:S(2)}) collective-permute-start(bf16[272,384]{1,0:T(8,128)(2,1)S(1)} %get-tuple-element.26), channel_id=1, source_target_pairs={{32,48},{33,49},{34,50},{35,51},{36,52},{37,53},{38,54},{39,55},{4... | collective-permute-start | bytes 626696 | tf_op jit(solution)/shard_map/ppermute | solution.py:47
  132.9 0.0 collective-permute-done.6.got0
  132.9 2.0 %collective-permute-done.7.got1 = bf16[272,384]{1,0:T(8,128)(2,1)S(1)} collective-permute-done((bf16[272,384]{1,0:T(8,128)(2,1)S(1)}, bf16[272,384]{1,0:T(8,128)(2,1)S(1)}, u32[]{:S(2)}, u32[]{:S(2)}) %collective-permute-start.7) | collective-permute-done | bytes 208928 | tf_op jit(solution)/shard_map/ppermute | solution.py:47
  134.9 1.5 collective-permute-done.8.got2
  136.4 2.4 %collective-permute-done.9.got3 = bf16[272,384]{1,0:T(8,128)(2,1)S(1)} collective-permute-done((bf16[272,384]{1,0:T(8,128)(2,1)S(1)}, bf16[272,384]{1,0:T(8,128)(2,1)S(1)}, u32[]{:S(2)}, u32[]{:S(2)}) %collective-permute-start.9) | collective-permute-done | bytes 208928 | tf_op jit(solution)/shard_map/ppermute | solution.py:47
  138.7 3.3 %shard_map.76 = bf16[32,32,128]{2,1,0:T(8,128)(2,1)S(1)} custom-call(s32[2]{0:T(128)S(1)} %pad_add_fusion.1.place, bf16[272,384]{1,0:T(8,128)(2,1)S(1)} %get-tuple-element.22.kept, bf16[272,384]{1,0:T(8,128)(2,1)S(1)} %collective-permute-done.6.got0, bf16[272,384]{1,0:T(8,128)(2,1)S(1)} %collective-permute-done.7.got1, ...), custom_call_target="tpu_custom_call" | custom-call | tf_op jit(solution)/shard_map/pallas_call | solution.py:292
  142.0 17.0 %all_to_all.10 = bf16[32,32,128]{2,1,0:T(8,128)(2,1)S(1)} all-to-all(bf16[32,32,128]{2,1,0:T(8,128)(2,1)S(1)} %shard_map.76), channel_id=1, replica_groups=mesh['y'=8,'core'=2,'half'=2,'side'=2,'z'=8] {'half','side','z'}, dimensions={0} | all-to-all | bytes 524288 | tf_op jit(solution)/shard_map/all_to_all | solution.py:301
  159.0 0.7 copy_bitcast_fusion
  (4 shorter events, 0.0 us)
Async XLA Ops:
  7.2 2.3 %copy-start = (bf16[3,6144,128]{2,1,0:T(8,128)(2,1)S(1)}, bf16[3,6144,128]{2,1,0:T(8,128)(2,1)}, u32[]{:S(2)}) copy-start(bf16[3,6144,128]{2,1,0:T(8,128)(2,1)} %own.1) | copy-start | bytes 14155780
  9.6 1.0 copy-start.1
  10.5 0.7 copy-start.3
  14.3 12.5 %copy-start.6 = (s32[1,32]{1,0:T(1,128)S(1)}, s32[1,32]{1,0:T(1,128)}, u32[]{:S(2)}) copy-start(s32[1,32]{1,0:T(1,128)} %param.10) | copy-start | bytes 388
  14.3 40.2 %collective-permute-start = (bf16[2,6144,128]{2,1,0:T(8,128)(2,1)}, bf16[2,6144,128]{2,1,0:T(8,128)(2,1)}, u32[]{:S(2)}, u32[]{:S(2)}) collective-permute-start(bf16[2,6144,128]{2,1,0:T(8,128)(2,1)} %get-tuple-element.17), channel_id=1, source_target_pairs={{0,8},{1,9},{2,10},{3,11},{4,12},{5,13},{6,14},{7,15},{8,0},{9,1},... | collective-permute-start | bytes 9437192 | tf_op jit(solution)/shard_map/ppermute | solution.py:47
  19.5 30.4 %copy-start.2 = (f32[6144]{0:T(1024)S(1)}, f32[6144]{0:T(1024)}, u32[]{:S(2)}) copy-start(f32[6144]{0:T(1024)} %param.11) | copy-start | bytes 73732
  19.6 30.2 %all-to-all-start = ((bf16[16,4,6272]{2,1,0:T(4,128)(2,1)}), bf16[16,4,6272]{2,1,0:T(4,128)(2,1)S(1)}, u32[]{:S(2)}, u32[]{:S(2)}) async-start(bf16[16,4,6272]{2,1,0:T(4,128)(2,1)} %get-tuple-element.16), calls=%async_computation | async-start | bytes 1605632 | tf_op jit(solution)/shard_map/all_to_all | solution.py:246
  26.8 83.2 %all-gather.2.cloned.1.call-start = ((), (), s32[]{:S(2)}) async-start(), calls=%async_computation.2 | async-start | bytes 6823936 | tf_op jit(solution)/shard_map/all_gather | solution.py:255
  54.5 31.0 %collective-permute-start.1 = (bf16[6160,128]{1,0:T(8,128)(2,1)}, bf16[6160,128]{1,0:T(8,128)(2,1)S(1)}, u32[]{:S(2)}, u32[]{:S(2)}) collective-permute-start(bf16[6160,128]{1,0:T(8,128)(2,1)} %get-tuple-element.19), channel_id=1, source_target_pairs={{0,8},{1,9},{2,10},{3,11},{4,12},{5,13},{6,14},{7,15},{8,0},{9,1},... | collective-permute-start | bytes 4730888 | tf_op jit(solution)/shard_map/ppermute | solution.py:47
  62.8 45.4 %collective-permute-start.3 = (bf16[6144,128]{1,0:T(8,128)(2,1)}, bf16[6144,128]{1,0:T(8,128)(2,1)S(1)}, u32[]{:S(2)}, u32[]{:S(2)}) collective-permute-start(bf16[6144,128]{1,0:T(8,128)(2,1)} %get-tuple-element.21), channel_id=1, source_target_pairs={{0,56},{1,57},{2,58},{3,59},{4,60},{5,61},{6,62},{7,63},{8,48},{9,... | collective-permute-start | bytes 4718600 | tf_op jit(solution)/shard_map/ppermute | solution.py:47
  64.1 45.9 %copy-start.4 = (f32[2,128]{1,0:T(2,128)S(1)}, f32[2,128]{1,0:T(2,128)}, u32[]{:S(2)}) copy-start(f32[2,128]{1,0:T(2,128)} %own_gain.1) | copy-start | bytes 3076
  64.1 44.1 %collective-permute-start.2 = (bf16[6144,128]{1,0:T(8,128)(2,1)}, bf16[6144,128]{1,0:T(8,128)(2,1)}, u32[]{:S(2)}, u32[]{:S(2)}) collective-permute-start(bf16[6144,128]{1,0:T(8,128)(2,1)} %get-tuple-element.20), channel_id=1, source_target_pairs={{32,40},{33,41},{34,42},{35,43},{36,44},{37,45},{38,46},{39,47},{4... | collective-permute-start | bytes 4718600 | tf_op jit(solution)/shard_map/ppermute | solution.py:47
  85.5 3.3 %copy-start.5 = (bf16[6160,128]{1,0:T(8,128)(2,1)}, bf16[6160,128]{1,0:T(8,128)(2,1)S(1)}, u32[]{:S(2)}) copy-start(bf16[6160,128]{1,0:T(8,128)(2,1)S(1)} %collective-permute-done.1.nv.refs_0_) | copy-start | bytes 4730884
  86.5 21.7 %collective-permute-start.5 = (bf16[3088,128]{1,0:T(8,128)(2,1)}, bf16[3088,128]{1,0:T(8,128)(2,1)S(1)}, u32[]{:S(2)}, u32[]{:S(2)}) collective-permute-start(bf16[3088,128]{1,0:T(8,128)(2,1)} %slice.19), channel_id=1, source_target_pairs={{0,56},{1,57},{2,58},{3,59},{4,60},{5,61},{6,62},{7,63},{8,48},{9,... | collective-permute-start | bytes 2371592 | tf_op jit(solution)/shard_map/ppermute | solution.py:47
  88.8 19.5 %collective-permute-start.4 = (bf16[3072,128]{1,0:T(8,128)(2,1)}, bf16[3072,128]{1,0:T(8,128)(2,1)S(1)}, u32[]{:S(2)}, u32[]{:S(2)}) collective-permute-start(bf16[3072,128]{1,0:T(8,128)(2,1)} %slice.18), channel_id=1, source_target_pairs={{32,40},{33,41},{34,42},{35,43},{36,44},{37,45},{38,46},{39,47},{4... | collective-permute-start | bytes 2359304 | tf_op jit(solution)/shard_map/ppermute | solution.py:47
  120.4 12.5 %collective-permute-start.6 = (bf16[272,384]{1,0:T(8,128)(2,1)S(1)}, bf16[272,384]{1,0:T(8,128)(2,1)S(1)}, u32[]{:S(2)}, u32[]{:S(2)}) collective-permute-start(bf16[272,384]{1,0:T(8,128)(2,1)S(1)} %get-tuple-element.23), channel_id=1, source_target_pairs={{0,32},{1,33},{2,34},{3,35},{4,36},{5,37},{6,38},{7,39},{8,40},{9,... | collective-permute-start | bytes 626696 | tf_op jit(solution)/shard_map/ppermute | solution.py:47
  124.9 10.0 %collective-permute-start.7 = (bf16[272,384]{1,0:T(8,128)(2,1)S(1)}, bf16[272,384]{1,0:T(8,128)(2,1)S(1)}, u32[]{:S(2)}, u32[]{:S(2)}) collective-permute-start(bf16[272,384]{1,0:T(8,128)(2,1)S(1)} %get-tuple-element.24), channel_id=1, source_target_pairs={{0,8},{1,9},{2,10},{3,11},{4,12},{5,13},{6,14},{7,15},{8,0},{9,1},... | collective-permute-start | bytes 626696 | tf_op jit(solution)/shard_map/ppermute | solution.py:47
  127.1 9.3 %collective-permute-start.8 = (bf16[272,384]{1,0:T(8,128)(2,1)S(1)}, bf16[272,384]{1,0:T(8,128)(2,1)S(1)}, u32[]{:S(2)}, u32[]{:S(2)}) collective-permute-start(bf16[272,384]{1,0:T(8,128)(2,1)S(1)} %get-tuple-element.25), channel_id=1, source_target_pairs={{0,40},{1,41},{2,42},{3,43},{4,44},{5,45},{6,46},{7,47},{8,32},{9,... | collective-permute-start | bytes 626696 | tf_op jit(solution)/shard_map/ppermute | solution.py:47
  130.4 8.3 %collective-permute-start.9 = (bf16[272,384]{1,0:T(8,128)(2,1)S(1)}, bf16[272,384]{1,0:T(8,128)(2,1)S(1)}, u32[]{:S(2)}, u32[]{:S(2)}) collective-permute-start(bf16[272,384]{1,0:T(8,128)(2,1)S(1)} %get-tuple-element.26), channel_id=1, source_target_pairs={{32,48},{33,49},{34,50},{35,51},{36,52},{37,53},{38,54},{39,55},{4... | collective-permute-start | bytes 626696 | tf_op jit(solution)/shard_map/ppermute | solution.py:47
Sparse Core Ops, SparseCore 0:
  54.6 55.2 all-gather.1
